TPU v7x, 512 devices: a whole 4x4x16 slice. The times are simulated.
512 devices in a mesh: step: 64 (over x, z), tp: 8 (over y, core).
Axes of the slice: x: 4, y: 4, z: 16, core: 2. Of those that a mesh axis runs over, the one named last changes fastest.
Arguments:
- trajectory: float32 [64, 128, 5120], P('step', None, 'tp'), may hold values from -3 to 3
- timesteps: int32 [64], replicated, may hold values from 1 to 999, as said below
- context_keys: bfloat16 [512, 3072], P(None, 'tp'), may hold values from -200 to 200
- context_values: bfloat16 [512, 3072], P(None, 'tp'), may hold values from -6 to 6
- ln_gain: float32 [5120], P('tp'), may hold values from 0.1 to 1.9
- q_gain: float32 [3072], P('tp'), may hold values from 0.1 to 1.9
- w_query: bfloat16 [5120, 3072], P('step', 'tp'), may hold values from -0.078125 to 0.078125
- w_out: bfloat16 [3072, 5120], P('step', 'tp'), may hold values from -0.625 to 0.625
Outputs:
- new_trajectory: float32 [64, 128, 5120], P('step', None, 'tp')
- errors: float32 [64], P('step')
Inputs may be any that keep to these rules, and one draw needn't show every extreme that they name: `timesteps`: strictly decreasing over the steps; the first is 999.
All inputs are finite; a program needn't handle non-finite values.
Results may differ from a plain program's by a relative error of at most 0.002.
The roundings to bfloat16 on the way count: a program that leaves them out, or rounds other values in their place, can miss the bound.
Values may be sent and summed in bfloat16 or wider, within the bound.
No kernel may reach another device: no remote copies, remote signals or barrier semaphores. Data moves between devices by JAX's collectives and lax.ppermute only.
A program may use at most 64 MiB of HBM per device.

v0:
```python
import math

import jax
import jax.numpy as jnp
from jax import lax
from jax.sharding import PartitionSpec as P

HD = 128


epsilon = 1e-06


def entering(value, axis, join, neutral):
    count, mine = (lax.axis_size(axis), lax.axis_index(axis))
    pieces = lax.all_gather(value, axis)
    total = jnp.full_like(value, 0) + jnp.asarray(neutral, value.dtype)

    def lap(position, total):
        longer = join(total, pieces[position])
        return jnp.where(position < mine, longer, total)

    return lax.fori_loop(0, count - 1, lap, total)


def spread(block, axis, source):
    block = jnp.where(lax.axis_index(axis) == source, block, jnp.zeros_like(block))
    return lax.psum(block, axis)


def sigma_of(levels):
    scaled = levels.astype(jnp.float32) / 1000.0
    return 5.0 * scaled / (1.0 + 4.0 * scaled)


def add_terms(earlier_sum, later_sum):
    return earlier_sum + later_sum


def on_device(trajectory, timesteps, context_keys, context_values, ln_gain, q_gain, w_query, w_out):
    latent = trajectory[0]
    token_count = latent.shape[0]
    full_width = latent.shape[1] * lax.axis_size("tp")
    whole_rows, whole_gain = (
        lax.all_gather(latent, "tp", axis=1, tiled=True),
        lax.all_gather(ln_gain, "tp", axis=0, tiled=True),
    )
    row_mean = jnp.mean(whole_rows, axis=-1, keepdims=True)
    row_square = jnp.mean(whole_rows * whole_rows, axis=-1, keepdims=True)
    row_var = row_square - row_mean * row_mean
    normed = ((whole_rows - row_mean) * lax.rsqrt(row_var + epsilon) * whole_gain).astype(
        jnp.bfloat16
    )
    columns = normed
    query = jnp.dot(
        columns,
        lax.all_gather(w_query, "step", axis=0, tiled=True),
        preferred_element_type=jnp.float32,
    )
    query_width = query.shape[1] * lax.axis_size("tp")
    square_sum = lax.psum(jnp.sum(query * query, axis=-1), "tp")
    query_scale = lax.rsqrt(square_sum / query_width + epsilon)[:, None]
    q_normed = (query * query_scale * q_gain).astype(jnp.bfloat16)
    local_heads = query.shape[1] // HD
    q_heads = q_normed.reshape(token_count, local_heads, HD)
    key_heads = context_keys.reshape(context_keys.shape[0], local_heads, HD)
    value_heads = context_values.reshape(context_values.shape[0], local_heads, HD)
    scores = jnp.einsum(
        "thd,khd->htk", q_heads, key_heads, preferred_element_type=jnp.float32
    ) / math.sqrt(HD)
    soft_weights = jax.nn.softmax(scores, axis=-1).astype(jnp.bfloat16)
    attended = jnp.einsum(
        "htk,khd->thd", soft_weights, value_heads, preferred_element_type=jnp.float32
    )
    attended = attended.reshape(token_count, local_heads * HD).astype(jnp.bfloat16)
    attended_all = lax.all_gather(attended, "tp", axis=1, tiled=True)
    columns = attended_all
    velocity = jnp.dot(
        columns,
        lax.all_gather(w_out, "step", axis=0, tiled=True),
        preferred_element_type=jnp.float32,
    )
    position = lax.axis_index("step")
    step_total = timesteps.shape[0]
    level_now = timesteps[position]
    level_next = jnp.where(
        position + 1 < step_total, timesteps[jnp.minimum(position + 1, step_total - 1)], 0
    )
    step_size = sigma_of(level_next) - sigma_of(level_now)
    drift = step_size * velocity
    prior_sum = entering(drift, "step", add_terms, jnp.zeros_like(drift))
    before = spread(latent, "step", 0) + prior_sum
    new_rows = before + drift
    change = before - latent
    change_sum = lax.psum(jnp.sum(change * change), "tp")
    error_value = change_sum / (token_count * full_width)
    return (new_rows[None], error_value.reshape(1))


def solution(mesh):
    placed = (
        P("step", None, "tp"),
        P(),
        P(None, "tp"),
        P(None, "tp"),
        P("tp"),
        P("tp"),
        P("step", "tp"),
        P("step", "tp"),
    )
    return jax.shard_map(
        on_device,
        mesh=mesh,
        in_specs=placed,
        out_specs=(P("step", None, "tp"), P("step")),
        check_vma=False,
    )
```

profile of v0, /device:TPU:1, one launch (start us, length us, event | category | flops | bytes accessed | tf_op | source)
XLA Modules:
  0.0 846.4 jit_solution(17794152583572053559)
XLA Ops:
  9.4 1.4 fusion.16
  12.8 1.2 copy.19
  14.0 1.9 copy.22
  16.1 19.3 %all-gather.2 = f32[8,1,640]{2,1,0:T(1,128)S(1)} all-gather(f32[1,1,640]{2,1,0:T(1,128)S(1)} %reshape.55), channel_id=1, replica_groups=mesh['step'=64,'tp'=8] {'tp'}, dimensions={0}, use_global_device_ids=true | all-gather | bytes 23040 | tf_op jit(solution)/shard_map/all_gather | solution.py:46
  35.4 14.3 %all-gather.12.cloned.1.call-done = f32[1,128,5120]{2,1,0:T(8,128)} async-done(((f32[1,128,640]{2,1,0:T(8,128)}), f32[1,128,5120]{2,1,0:T(8,128)}) %all-gather.12.cloned.1.call-update) | async-done | bytes 2621456 | tf_op jit(solution)/shard_map/all_gather | solution.py:45
  49.7 2.1 reduce_sum.45
  52.5 137.7 %all-gather.8.cloned.1.call-done = bf16[5120,384]{1,0:T(8,128)(2,1)} async-done(((bf16[80,384]{1,0:T(8,128)(2,1)}), bf16[5120,384]{1,0:T(8,128)(2,1)}) %all-gather.8.cloned.1.call-update) | async-done | bytes 3932176 | tf_op jit(solution)/shard_map/all_gather | solution.py:57
  190.2 3.1 multiply_reduce_fusion
  193.3 21.5 %psum.22 = f32[128]{0:T(128)S(1)} all-reduce(f32[128]{0:T(128)S(1)} %get-tuple-element.111), channel_id=1, replica_groups=mesh['step'=64,'tp'=8] {'tp'}, use_global_device_ids=true, to_apply=%region_4.0 | all-reduce | flops 128 | bytes 1024 | tf_op jit(solution)/shard_map/psum | solution.py:61
  216.8 14.0 %all_gather.24 = bf16[128,3072]{0,1:T(8,128)(2,1)S(1)} all-gather(bf16[128,384]{0,1:T(8,128)(2,1)S(1)} %bitcast.53), channel_id=1, replica_groups=mesh['step'=64,'tp'=8] {'tp'}, dimensions={1}, use_global_device_ids=true | all-gather | bytes 884736 | tf_op jit(solution)/shard_map/all_gather | solution.py:76
  230.7 102.8 %all-gather.10.cloned.1.call-done = bf16[3072,640]{1,0:T(8,128)(2,1)} async-done(((bf16[48,640]{1,0:T(8,128)(2,1)}), bf16[3072,640]{1,0:T(8,128)(2,1)}) %all-gather.10.cloned.1.call-update) | async-done | bytes 3932176 | tf_op jit(solution)/shard_map/all_gather | solution.py:80
  333.5 3.7 convolution_multiply_fusion.1
  338.1 221.3 %all-gather.14.cloned.1.call-done = f32[8192,640]{1,0:T(8,128)} async-done(((f32[128,640]{1,0:T(8,128)}), f32[8192,640]{1,0:T(8,128)}) %all-gather.14.cloned.1.call-update) | async-done | bytes 20971536 | tf_op jit(solution)/shard_map/all_gather | solution.py:16
  559.4 68.4 %while.14 = (s32[]{:T(128)}, f32[128,640]{1,0:T(8,128)S(1)}, s32[]{:T(128)}, f32[64,128,640]{2,1,0:T(8,128)}, s32[]{:T(128)}, /*index=5*/s32[]{:T(128)}) while((s32[]{:T(128)}, f32[128,640]{1,0:T(8,128)S(1)}, s32[]{:T(128)}, f32[64,128,640]{2,1,0:T(8,128)}, s32[]{:T(128)}, /*index=5*/s32[]{:T(128)}) %tuple.53), condition=%wide.region_8.9_spmd.clone, body=%wide.region_7.8_spmd.clone.sunk | while | flops 245764 | bytes 983133 | solution.py:23
  560.5 1.1 add_select_fusion.2
  561.6 1.1 add_select_fusion.2
  562.7 1.1 add_select_fusion.2
  575.7 1.1 add_select_fusion.2
  581.1 1.1 add_select_fusion.2
  582.2 1.1 add_select_fusion.2
  584.4 1.1 add_select_fusion.2
  585.5 1.1 add_select_fusion.2
  587.7 1.1 add_select_fusion.2
  589.8 1.1 add_select_fusion.2
  592.0 1.1 add_select_fusion.2
  593.1 1.1 add_select_fusion.2
  595.3 1.1 add_select_fusion.2
  596.3 1.1 add_select_fusion.2
  597.4 1.1 add_select_fusion.2
  598.5 1.1 add_select_fusion.2
  599.6 1.1 add_select_fusion.2
  600.7 1.1 add_select_fusion.2
  602.9 1.1 add_select_fusion.2
  604.0 1.1 add_select_fusion.2
  605.0 1.1 add_select_fusion.2
  606.1 1.1 add_select_fusion.2
  607.2 1.1 add_select_fusion.2
  608.3 1.1 add_select_fusion.2
  610.5 1.1 add_select_fusion.2
  611.6 1.1 add_select_fusion.2
  612.7 1.1 add_select_fusion.2
  613.7 1.1 add_select_fusion.2
  615.9 1.1 add_select_fusion.2
  618.1 1.1 add_select_fusion.2
  619.2 1.1 add_select_fusion.2
  627.9 185.0 %all-reduce.2.cloned.1.call-done = f32[128,640]{1,0:T(8,128)} async-done(((f32[128,640]{1,0:T(8,128)}), f32[128,640]{1,0:T(8,128)}) %all-reduce.2.cloned.1.call-update) | async-done | bytes 327696 | tf_op jit(solution)/shard_map/psum | solution.py:28
  812.9 2.3 fusion.13
  815.2 22.9 %psum.23 = f32[]{:T(128)} all-reduce(f32[]{:T(128)} %get-tuple-element.105), channel_id=1, replica_groups=mesh['step'=64,'tp'=8] {'tp'}, use_global_device_ids=true, to_apply=%region_10.11 | all-reduce | flops 1 | bytes 8 | tf_op jit(solution)/shard_map/psum | solution.py:95
  (63 shorter events, 40.4 us)
Async XLA Ops:
  7.2 42.5 %all-gather.12.cloned.1.call-start = ((), (), s32[]{:S(2)}) async-start(), calls=%async_computation.3 | async-start | bytes 2949120 | tf_op jit(solution)/shard_map/all_gather | solution.py:45
  7.9 182.3 %all-gather.8.cloned.1.call-start = ((), (), s32[]{:S(2)}) async-start(), calls=%async_computation.1 | async-start | bytes 3993600 | tf_op jit(solution)/shard_map/all_gather | solution.py:57
  8.6 324.9 %all-gather.10.cloned.1.call-start = ((), (), s32[]{:S(2)}) async-start(), calls=%async_computation.2 | async-start | bytes 3993600 | tf_op jit(solution)/shard_map/all_gather | solution.py:80
  9.4 550.0 %all-gather.14.cloned.1.call-start = ((), (), s32[]{:S(2)}) async-start(), calls=%async_computation.4 | async-start | bytes 21299200 | tf_op jit(solution)/shard_map/all_gather | solution.py:16
  49.7 2.5 copy-start
  190.2 24.6 %copy-start.4 = (f32[384]{0:T(512)S(1)}, f32[384]{0:T(512)}, u32[]{:S(2)}) copy-start(f32[384]{0:T(512)} %param.15) | copy-start | bytes 4612
  193.3 22.6 %copy-start.3 = (bf16[512,384]{0,1:T(8,128)(2,1)S(1)}, bf16[512,384]{0,1:T(8,128)(2,1)}, u32[]{:S(2)}) copy-start(bf16[512,384]{0,1:T(8,128)(2,1)} %copy.22) | copy-start | bytes 1179652
  230.7 106.6 %copy-start.1 = (f32[1,128,640]{2,1,0:T(8,128)S(1)}, f32[1,128,640]{2,1,0:T(8,128)}, u32[]{:S(2)}) copy-start(f32[1,128,640]{2,1,0:T(8,128)} %param.10) | copy-start | bytes 983044
  337.2 475.6 %all-reduce.2.cloned.1.call-start = ((), (), s32[]{:S(2)}) async-start(), calls=%async_computation | async-start | bytes 655360 | tf_op jit(solution)/shard_map/psum | solution.py:28
  338.0 474.8 %copy-start.2 = (f32[128,640]{1,0:T(8,128)S(1)}, f32[128,640]{1,0:T(8,128)}, u32[]{:S(2)}) copy-start(f32[128,640]{1,0:T(8,128)} %convolution_multiply_fusion.1) | copy-start | bytes 983044
Sparse Core Ops, SparseCore 0:
  10.1 39.5 all-gather.11
  52.7 137.4 all-gather.7
  193.2 140.3 all-gather.9
  337.3 222.0 all-gather.13
  563.2 249.5 all-reduce.1
where the time goes:
time: 849 us; the launch traced here: 846 us
  waiting for transfers between devices  663 us (78%)
  blocking collectives  77.7 us (9%)
  other arithmetic  72.6 us (9%)
  between operations  17.1 us (2%)
    all_gather x1, waiting for transfers between devices, entering(): pieces = lax.all_gather(value, axis)  221 us
    psum x1, waiting for transfers between devices, spread(): return lax.psum(block, axis)  185 us
    all_gather x1, waiting for transfers between devices, on_device(): lax.all_gather(w_query, 'step', axis=0, tiled=True)  138 us
    all_gather x1, waiting for transfers between devices, on_device(): lax.all_gather(w_out, 'step', axis=0, tiled=True)  103 us
    select_n x63, other arithmetic, lap(): return jnp.where(position < mine, longer, total)  67 us
    psum x1, blocking collectives, on_device(): change_sum = lax.psum(jnp.sum(change * change), 'tp')  22.9 us
    psum x1, blocking collectives, on_device(): square_sum = lax.psum(jnp.sum(query * query, axis=-1), 'tp')  21.5 us
    all_gather x1, blocking collectives, on_device(): lax.all_gather(ln_gain, 'tp', axis=0, tiled=True)  19.3 us
  transfers between devices with their start and end apart: 5, of which 5 were waited for; matrix products, arithmetic and copies ran while one was open for 9% of the time, Pallas kernels for 0%

commit v1 on v0

v1 whole, which is shorter than its diff:
```python
import math

import jax
import jax.numpy as jnp
from jax import lax
from jax.sharding import Mesh
from jax.sharding import PartitionSpec as P

HD = 128
STEP = ("x", "z")
TP = ("y", "core")

epsilon = 1e-06


def sigma_of(levels):
    scaled = levels.astype(jnp.float32) / 1000.0
    return 5.0 * scaled / (1.0 + 4.0 * scaled)


def transpose_plane(value):
    side = lax.axis_size("x")
    pairs = [(a * side + b, b * side + a) for a in range(side) for b in range(side)]
    return lax.ppermute(value, ("x", "y"), pairs)


def prefix_over_steps(term):
    z_size, x_size = lax.axis_size("z"), lax.axis_size("x")
    rows, width = term.shape
    slices = lax.all_to_all(term.reshape(z_size, rows // z_size, width), "z", 0, 0)
    running = [slices[0]]
    for at in range(1, z_size):
        running.append(running[-1] + slices[at])
    totals = lax.all_gather(running[-1], "x")
    mine = lax.axis_index("x")
    earlier = jnp.zeros_like(running[0])
    for at in range(x_size - 1):
        earlier = earlier + jnp.where(at < mine, totals[at], 0.0)
    summed = jnp.stack(running) + earlier[None]
    return lax.all_to_all(summed, "z", 0, 0).reshape(rows, width)


def on_device(trajectory, timesteps, context_keys, context_values, ln_gain, q_gain, w_query, w_out):
    latent = trajectory[0]
    token_count, block = latent.shape
    full_width = block * lax.axis_size(TP)
    x_size = lax.axis_size("x")

    query_rows = lax.all_gather(w_query, "z", axis=0, tiled=True)
    out_rows = lax.all_gather(w_out, "x")
    out_rows = lax.all_gather(out_rows, "z", axis=1)
    out_rows = out_rows.reshape(-1, w_out.shape[1])

    sums = jnp.stack([jnp.sum(latent, axis=-1), jnp.sum(latent * latent, axis=-1)])
    sums = lax.psum(sums, TP) / full_width
    row_mean, row_square = sums[0][:, None], sums[1][:, None]
    row_var = row_square - row_mean * row_mean
    normed = ((latent - row_mean) * lax.rsqrt(row_var + epsilon) * ln_gain).astype(jnp.bfloat16)

    flipped = transpose_plane(normed)
    half = token_count // 2
    parts = [lax.all_gather(flipped[at * half : (at + 1) * half], TP) for at in range(2)]
    query_weights = query_rows.reshape(2, block, -1)
    partial = []
    for part in parts:
        part = part.reshape(x_size, 2, half, block)
        partial.append(
            jnp.einsum("xctk,ckn->xtn", part, query_weights, preferred_element_type=jnp.float32)
        )
    partial = jnp.concatenate(partial, axis=1)
    query = jnp.sum(lax.all_to_all(partial, "x", 0, 0), axis=0)

    query_width = query.shape[1] * lax.axis_size(TP)
    square_sum = lax.psum(jnp.sum(query * query, axis=-1), TP)
    query_scale = lax.rsqrt(square_sum / query_width + epsilon)[:, None]
    q_normed = (query * query_scale * q_gain).astype(jnp.bfloat16)
    local_heads = query.shape[1] // HD
    q_heads = q_normed.reshape(token_count, local_heads, HD)
    key_heads = context_keys.reshape(context_keys.shape[0], local_heads, HD)
    value_heads = context_values.reshape(context_values.shape[0], local_heads, HD)
    scores = jnp.einsum(
        "thd,khd->htk", q_heads, key_heads, preferred_element_type=jnp.float32
    ) / math.sqrt(HD)
    soft_weights = jax.nn.softmax(scores, axis=-1).astype(jnp.bfloat16)
    attended = jnp.einsum(
        "htk,khd->thd", soft_weights, value_heads, preferred_element_type=jnp.float32
    )
    attended = attended.reshape(token_count, local_heads * HD).astype(jnp.bfloat16)
    attended_all = lax.all_gather(attended, TP, axis=1, tiled=True)
    velocity = jnp.dot(attended_all, out_rows, preferred_element_type=jnp.float32)

    position = lax.axis_index(STEP)
    step_total = timesteps.shape[0]
    level_now = timesteps[position]
    level_next = jnp.where(
        position + 1 < step_total, timesteps[jnp.minimum(position + 1, step_total - 1)], 0
    )
    step_size = sigma_of(level_next) - sigma_of(level_now)
    drift = step_size * velocity
    first = position == 0
    new_rows = prefix_over_steps(drift + jnp.where(first, latent, 0.0))
    before = jnp.where(first, latent, new_rows - drift)
    change = before - latent
    change_sum = lax.psum(jnp.sum(change * change), TP)
    error_value = change_sum / (token_count * full_width)
    return (new_rows[None], error_value.reshape(1))


def solution(mesh):
    fine = Mesh(mesh.devices.reshape(4, 16, 4, 2), ("x", "z", "y", "core"))
    placed = (
        P(STEP, None, TP),
        P(),
        P(None, TP),
        P(None, TP),
        P(TP),
        P(TP),
        P(STEP, TP),
        P(STEP, TP),
    )
    return jax.shard_map(
        on_device,
        mesh=fine,
        in_specs=placed,
        out_specs=(P(STEP, None, TP), P(STEP)),
        check_vma=False,
    )
```

time: 849 us -> 260 us (0.31)
  waiting for transfers between devices: 663 us -> 25.4 us
  blocking collectives: 77.7 us -> 191 us
  other arithmetic: 72.6 us -> 6 us
  starting transfers between devices: 0.19 us -> 11.7 us
    all_gather x4 -> x1, waiting for transfers between devices: 476 us -> 0.01 us  [on_device(): out_rows = lax.all_gather(out_rows, 'z', axis=1)]
    psum x1 -> x0, waiting for transfers between devices: 185 us -> none  [spread(): return lax.psum(block, axis)]
    all_gather x2 -> x6, blocking collectives: 33.3 us -> 114 us  [the longest x1 41.8 us: on_device(): query_rows = lax.all_gather(w_query, 'z', axis=0, tiled=True)]
    select_n x64 -> x0, other arithmetic: 67.8 us -> none  [the longest x63 67 us: lap(): return jnp.where(position < mine, longer, total)]
    all_to_all x0 -> x2, waiting for transfers between devices: none -> 25.4 us  [the longest x1 15.5 us: prefix_over_steps(): lax.all_to_all(term.reshape(z_size, rows // z_size, width), 'z', 0, 0)]
    all_to_all x0 -> x1, blocking collectives: none -> 24.6 us  [prefix_over_steps(): return lax.all_to_all(summed, 'z', 0, 0).reshape(rows, width)]
    all_to_all x0 -> x2, starting transfers between devices: none -> 11 us  [the longest x1 7.46 us: prefix_over_steps(): lax.all_to_all(term.reshape(z_size, rows // z_size, width), 'z', 0, 0)]
    psum x2 -> x3, blocking collectives: 44.4 us -> 52.6 us  [the longest x1 20.6 us: on_device(): change_sum = lax.psum(jnp.sum(change * change), TP)]
  transfers between devices with their start and end apart: 5 -> 4, of which waited for: 5 -> 2; matrix products, arithmetic and copies ran while one was open for 9% -> 3% of each run, Pallas kernels for 0% -> 0%
where the time goes in v1:
time: 260 us; the launch traced here: 259 us
  blocking collectives  191 us (73%)
  waiting for transfers between devices  25.4 us (10%)
  between operations  17.5 us (7%)
  starting transfers between devices  11.7 us (4%)
  other arithmetic  6 us (2%)
  matrix products  5.75 us (2%)
    all_gather x1, blocking collectives, on_device(): query_rows = lax.all_gather(w_query, 'z', axis=0, tiled=True)  41.8 us
    all_gather x2, blocking collectives, on_device(): lax.all_gather(flipped[at * half:(at + 1) * half], TP)  34.9 us
    all_to_all x1, blocking collectives, prefix_over_steps(): return lax.all_to_all(summed, 'z', 0, 0).reshape(rows, width)  24.6 us
    psum x1, blocking collectives, on_device(): change_sum = lax.psum(jnp.sum(change * change), TP)  20.6 us
    psum x1, blocking collectives, on_device(): sums = lax.psum(sums, TP) / full_width  19.3 us
    all_to_all x1, waiting for transfers between devices, prefix_over_steps(): lax.all_to_all(term.reshape(z_size, rows // z_size, width), 'z', 0, 0)  15.5 us
    all_gather x1, blocking collectives, on_device(): attended_all = lax.all_gather(attended, TP, axis=1, tiled=True)  15 us
    all_gather x1, blocking collectives, on_device(): out_rows = lax.all_gather(w_out, 'x')  12.8 us
  transfers between devices with their start and end apart: 4, of which 2 were waited for; matrix products, arithmetic and copies ran while one was open for 3% of the time, Pallas kernels for 0%

profile of v1, /device:TPU:1, one launch (start us, length us, event | category | flops | bytes accessed | tf_op | source)
XLA Modules:
  0.0 259.2 jit_solution(1968374863456793788)
XLA Ops:
  7.2 0.0 all-gather.6.cloned.1.call-start
  7.2 12.8 %all-gather.2 = bf16[192,640]{1,0:T(8,128)(2,1)} all-gather(bf16[48,640]{1,0:T(8,128)(2,1)} %param.15), channel_id=4, replica_groups=mesh['x'=4,'z'=16,'y'=4,'core'=2] {'x'}, dimensions={0}, use_global_device_ids=true | all-gather | bytes 307200 | tf_op jit(solution)/shard_map/all_gather | solution.py:50
  20.0 0.0 all-gather.6.cloned.1.call-update
  20.0 1.1 reduce_sum.56
  21.1 1.1 fusion.5
  22.2 19.3 %psum.21 = f32[2,128]{1,0:T(2,128)S(1)} all-reduce(f32[2,128]{1,0:T(2,128)S(1)} %pad_maximum_fusion.1), channel_id=1, replica_groups=mesh['x'=4,'z'=16,'y'=4,'core'=2] {'y','core'}, use_global_device_ids=true, to_apply=%region_2.0 | all-reduce | flops 256 | bytes 2048 | tf_op jit(solution)/shard_map/psum | solution.py:55
  41.5 1.1 fusion.8
  42.6 0.7 collective-permute-start
  43.3 41.8 %all_gather.36 = bf16[1280,384]{1,0:T(8,128)(2,1)S(1)} all-gather(bf16[80,384]{1,0:T(8,128)(2,1)} %param.14), channel_id=1, replica_groups=mesh['x'=4,'z'=16,'y'=4,'core'=2] {'z'}, dimensions={0}, use_global_device_ids=true | all-gather | bytes 1044480 | tf_op jit(solution)/shard_map/all_gather | solution.py:49
  85.1 0.0 collective-permute-done
  85.1 21.7 %all-gather.1 = bf16[512,640]{1,0:T(8,128)(2,1)S(1)} all-gather(bf16[64,640]{1,0:T(8,128)(2,1)S(1)} %get-tuple-element.17), channel_id=3, replica_groups=mesh['x'=4,'z'=16,'y'=4,'core'=2] {'y','core'}, dimensions={0}, use_global_device_ids=true | all-gather | bytes 737280 | tf_op jit(solution)/shard_map/all_gather | solution.py:62
  106.8 0.0 copy-start.4
  106.8 0.0 copy-start.1
  106.8 0.0 copy-start.2
  106.8 0.5 convolution_bitcast_fusion
  107.3 13.3 %all-gather = bf16[512,640]{1,0:T(8,128)(2,1)S(1)} all-gather(bf16[64,640]{1,0:T(8,128)(2,1)S(1)} %get-tuple-element.16), channel_id=2, replica_groups=mesh['x'=4,'z'=16,'y'=4,'core'=2] {'y','core'}, dimensions={0}, use_global_device_ids=true | all-gather | bytes 737280 | tf_op jit(solution)/shard_map/all_gather | solution.py:62
  120.6 0.0 copy-start.3
  120.6 0.5 convolution_bitcast_fusion.1
  121.1 0.9 pad_maximum_fusion
  122.0 3.5 %all-to-all-start = ((f32[4,128,384]{2,1,0:T(8,128)}), f32[4,128,384]{2,1,0:T(8,128)S(1)}, u32[]{:S(2)}, u32[]{:S(2)}) async-start(f32[4,128,384]{2,1,0:T(8,128)} %pad_maximum_fusion), calls=%async_computation | async-start | bytes 1572864 | tf_op jit(solution)/shard_map/all_to_all | solution.py:71
  125.5 0.0 copy-done.4
  125.5 0.6 fusion.21
  127.4 0.0 copy-done.1
  127.4 0.2 copy.17
  127.6 0.0 copy-done.2
  127.6 0.2 copy.20
  127.9 9.8 %all-to-all-done = f32[4,128,384]{2,1,0:T(8,128)S(1)} async-done(((f32[4,128,384]{2,1,0:T(8,128)}), f32[4,128,384]{2,1,0:T(8,128)S(1)}, u32[]{:S(2)}, u32[]{:S(2)}) %all-to-all-start) | async-done | bytes 786464 | tf_op jit(solution)/shard_map/all_to_all | solution.py:71
  137.8 0.1 copy.16
  137.9 0.1 multiply_reduce_fusion
  138.0 12.7 %psum.22 = f32[128]{0:T(128)S(1)} all-reduce(f32[128]{0:T(128)S(1)} %multiply_reduce_fusion), channel_id=1, replica_groups=mesh['x'=4,'z'=16,'y'=4,'core'=2] {'y','core'}, use_global_device_ids=true, to_apply=%region_5.0 | all-reduce | flops 128 | bytes 1024 | tf_op jit(solution)/shard_map/psum | solution.py:74
  150.8 0.0 copy-done.3
  150.8 0.6 fusion.22
  151.4 0.4 convolution_multiply_fusion
  151.8 0.0 copy-start
  151.8 0.9 convolution_convert_fusion
  152.6 15.0 %all_gather.39 = bf16[128,3072]{0,1:T(8,128)(2,1)S(1)} all-gather(bf16[128,384]{0,1:T(8,128)(2,1)S(1)} %bitcast.83), channel_id=1, replica_groups=mesh['x'=4,'z'=16,'y'=4,'core'=2] {'y','core'}, dimensions={1}, use_global_device_ids=true | all-gather | bytes 884736 | tf_op jit(solution)/shard_map/all_gather | solution.py:89
  167.6 0.0 all-gather.6.cloned.1.call-done
  167.6 2.9 %convolution_multiply_fusion.1 = f32[128,640]{1,0:T(8,128)S(1)} fusion(bf16[128,3072]{0,1:T(8,128)(2,1)S(1)} %all_gather.39, bf16[3072,640]{1,0:T(8,128)(2,1)} %bitcast.73, f32[]{:T(128)S(6)} %sub.35), kind=kOutput, calls=%fused_computation.6 | convolution fusion | flops 503398400 | bytes 5046276 | tf_op jit(solution)/shard_map/dot_general | solution.py:90
  170.5 0.0 copy-done
  170.6 0.8 fusion.10
  171.3 7.5 %all-to-all-start.1 = ((f32[16,8,640]{2,1,0:T(8,128)}), f32[16,8,640]{2,1,0:T(8,128)S(1)}, u32[]{:S(2)}, u32[]{:S(2)}) async-start(f32[16,8,640]{2,1,0:T(8,128)} %fusion.10), calls=%async_computation.1 | async-start | bytes 655360 | tf_op jit(solution)/shard_map/all_to_all | solution.py:30
  178.8 15.5 %all-to-all-done.1 = f32[16,8,640]{2,1,0:T(8,128)S(1)} async-done(((f32[16,8,640]{2,1,0:T(8,128)}), f32[16,8,640]{2,1,0:T(8,128)S(1)}, u32[]{:S(2)}, u32[]{:S(2)}) %all-to-all-start.1) | async-done | bytes 327712 | tf_op jit(solution)/shard_map/all_to_all | solution.py:30
  194.6 9.3 %all_gather.44 = f32[4,8,640]{2,1,0:T(8,128)S(1)} all-gather(f32[1,8,640]{2,1,0:T(8,128)S(1)} %get-tuple-element.3), channel_id=1, replica_groups=mesh['x'=4,'z'=16,'y'=4,'core'=2] {'x'}, dimensions={0}, use_global_device_ids=true | all-gather | bytes 102400 | tf_op jit(solution)/shard_map/all_gather | solution.py:34
  203.9 24.6 %all_to_all.15 = f32[16,8,640]{2,1,0:T(8,128)S(1)} all-to-all(f32[16,8,640]{2,1,0:T(8,128)S(1)} %broadcast_add_fusion), channel_id=1, replica_groups=mesh['x'=4,'z'=16,'y'=4,'core'=2] {'z'}, dimensions={0} | all-to-all | bytes 655360 | tf_op jit(solution)/shard_map/all_to_all | solution.py:40
  228.5 0.7 fusion.4
  229.2 20.6 %psum.23 = f32[]{:T(128)} all-reduce(f32[]{:T(128)} %fusion.4), channel_id=1, replica_groups=mesh['x'=4,'z'=16,'y'=4,'core'=2] {'y','core'}, use_global_device_ids=true, to_apply=%region_9.10 | all-reduce | flops 1 | bytes 8 | tf_op jit(solution)/shard_map/psum | solution.py:104
  250.5 0.7 copy.41
  (25 shorter events, 0.2 us)
Async XLA Ops:
  7.2 160.4 %all-gather.6.cloned.1.call-start = ((), (), s32[]{:S(2)}) async-start(), calls=%async_computation.3 | async-start | bytes 4177920 | tf_op jit(solution)/shard_map/all_gather | solution.py:51
  42.6 42.5 %collective-permute-start = (bf16[128,640]{1,0:T(8,128)(2,1)S(1)}, bf16[128,640]{1,0:T(8,128)(2,1)S(1)}, u32[]{:S(2)}, u32[]{:S(2)}) collective-permute-start(bf16[128,640]{1,0:T(8,128)(2,1)S(1)} %fusion.8), channel_id=1, source_target_pairs={{0,0},{2,128},{4,256},{6,384},{128,2},{130,130},{132,258},{134,386... | collective-permute-start | bytes 491528 | tf_op jit(solution)/shard_map/ppermute | solution.py:24
  106.8 18.7 %copy-start.4 = (s32[64]{0:T(128)S(1)}, s32[64]{0:T(128)}, u32[]{:S(2)}) copy-start(s32[64]{0:T(128)} %param.9) | copy-start | bytes 772
  106.8 20.6 %copy-start.1 = (bf16[512,384]{1,0:T(8,128)(2,1)S(1)}, bf16[512,384]{1,0:T(8,128)(2,1)}, u32[]{:S(2)}) copy-start(bf16[512,384]{1,0:T(8,128)(2,1)} %param.10) | copy-start | bytes 1179652
  106.8 20.8 %copy-start.2 = (bf16[512,384]{1,0:T(8,128)(2,1)S(1)}, bf16[512,384]{1,0:T(8,128)(2,1)}, u32[]{:S(2)}) copy-start(bf16[512,384]{1,0:T(8,128)(2,1)} %param.11) | copy-start | bytes 1179652
  120.6 30.2 %copy-start.3 = (f32[384]{0:T(512)S(1)}, f32[384]{0:T(512)}, u32[]{:S(2)}) copy-start(f32[384]{0:T(512)} %param.13) | copy-start | bytes 4612
  122.0 15.7 %all-to-all-start = ((f32[4,128,384]{2,1,0:T(8,128)}), f32[4,128,384]{2,1,0:T(8,128)S(1)}, u32[]{:S(2)}, u32[]{:S(2)}) async-start(f32[4,128,384]{2,1,0:T(8,128)} %pad_maximum_fusion), calls=%async_computation | async-start | bytes 1572864 | tf_op jit(solution)/shard_map/all_to_all | solution.py:71
  151.8 18.8 %copy-start = (f32[1,128,640]{2,1,0:T(8,128)S(1)}, f32[1,128,640]{2,1,0:T(8,128)}, u32[]{:S(2)}) copy-start(f32[1,128,640]{2,1,0:T(8,128)} %param.8) | copy-start | bytes 983044
  171.3 23.0 %all-to-all-start.1 = ((f32[16,8,640]{2,1,0:T(8,128)}), f32[16,8,640]{2,1,0:T(8,128)S(1)}, u32[]{:S(2)}, u32[]{:S(2)}) async-start(f32[16,8,640]{2,1,0:T(8,128)} %fusion.10), calls=%async_computation.1 | async-start | bytes 655360 | tf_op jit(solution)/shard_map/all_to_all | solution.py:30
Sparse Core Ops, SparseCore 0:
  20.1 82.5 all-gather.5

commit v2 on v1

--- a/solution.py
+++ b/solution.py
@@ -16,6 +16,10 @@
 def sigma_of(levels):
     scaled = levels.astype(jnp.float32) / 1000.0
     return 5.0 * scaled / (1.0 + 4.0 * scaled)
+
+
+def tp_sum(value):
+    return lax.psum(lax.psum(value, "core"), "y")
 
 
 def transpose_plane(value):
@@ -46,32 +50,34 @@
     full_width = block * lax.axis_size(TP)
     x_size = lax.axis_size("x")
 
-    query_rows = lax.all_gather(w_query, "z", axis=0, tiled=True)
-    out_rows = lax.all_gather(w_out, "x")
-    out_rows = lax.all_gather(out_rows, "z", axis=1)
-    out_rows = out_rows.reshape(-1, w_out.shape[1])
+    query_depth, query_cols = w_query.shape
+    both = jnp.concatenate([jnp.pad(w_query, ((0, 0), (0, block - query_cols))), w_out])
+    both = lax.all_gather(both, "z")
+    query_rows = both[:, :query_depth, :query_cols].reshape(-1, query_cols)
+    out_rows = both[:, query_depth:].reshape(-1, block)
+    out_rows = lax.all_gather(out_rows, "x", axis=0, tiled=True)
 
     sums = jnp.stack([jnp.sum(latent, axis=-1), jnp.sum(latent * latent, axis=-1)])
-    sums = lax.psum(sums, TP) / full_width
+    sums = tp_sum(sums) / full_width
     row_mean, row_square = sums[0][:, None], sums[1][:, None]
     row_var = row_square - row_mean * row_mean
     normed = ((latent - row_mean) * lax.rsqrt(row_var + epsilon) * ln_gain).astype(jnp.bfloat16)
 
     flipped = transpose_plane(normed)
-    half = token_count // 2
-    parts = [lax.all_gather(flipped[at * half : (at + 1) * half], TP) for at in range(2)]
-    query_weights = query_rows.reshape(2, block, -1)
+    gathered = lax.all_gather(flipped, "y")
+    half = x_size // 2
+    query_weights = query_rows.reshape(2, block, query_cols)
     partial = []
-    for part in parts:
-        part = part.reshape(x_size, 2, half, block)
+    for at in range(2):
+        part = lax.all_gather(gathered[at * half : (at + 1) * half], "core")
         partial.append(
-            jnp.einsum("xctk,ckn->xtn", part, query_weights, preferred_element_type=jnp.float32)
+            jnp.einsum("cxtk,ckn->xtn", part, query_weights, preferred_element_type=jnp.float32)
         )
-    partial = jnp.concatenate(partial, axis=1)
+    partial = jnp.concatenate(partial)
     query = jnp.sum(lax.all_to_all(partial, "x", 0, 0), axis=0)
 
     query_width = query.shape[1] * lax.axis_size(TP)
-    square_sum = lax.psum(jnp.sum(query * query, axis=-1), TP)
+    square_sum = tp_sum(jnp.sum(query * query, axis=-1))
     query_scale = lax.rsqrt(square_sum / query_width + epsilon)[:, None]
     q_normed = (query * query_scale * q_gain).astype(jnp.bfloat16)
     local_heads = query.shape[1] // HD
@@ -101,7 +107,7 @@
     new_rows = prefix_over_steps(drift + jnp.where(first, latent, 0.0))
     before = jnp.where(first, latent, new_rows - drift)
     change = before - latent
-    change_sum = lax.psum(jnp.sum(change * change), TP)
+    change_sum = tp_sum(jnp.sum(change * change))
     error_value = change_sum / (token_count * full_width)
     return (new_rows[None], error_value.reshape(1))
 

time: 260 us -> 279 us (1.073)
  waiting for transfers between devices: 25.4 us -> 98.1 us
  blocking collectives: 191 us -> 132 us
  local copies, waits for them, and re-layouts: 1.86 us -> 5.5 us
    all_gather x1 -> x2, waiting for transfers between devices: 0.01 us -> 73.2 us  [the longest x1 73.2 us: on_device(): both = lax.all_gather(both, 'z')]
    all_gather x4 -> x3, blocking collectives: 89.5 us -> 34.3 us  [the longest x1 24.3 us: on_device(): gathered = lax.all_gather(flipped, 'y')]
    psum x3 -> x6, blocking collectives: 52.6 us -> 48.3 us  [tp_sum(): return lax.psum(lax.psum(value, 'core'), 'y')]
    slice x1 -> x3, local copies, waits for them, and re-layouts: 0.01 us -> 3.65 us  [the longest x1 2.25 us: on_device(): out_rows = both[:, query_depth:].reshape(-1, block)]
  transfers between devices with their start and end apart: 4 -> 5, of which waited for: 2 -> 3; matrix products, arithmetic and copies ran while one was open for 3% -> 3% of each run, Pallas kernels for 0% -> 0%
where the time goes in v2:
time: 279 us; the launch traced here: 277 us
  blocking collectives  132 us (47%)
  waiting for transfers between devices  98.1 us (35%)
  between operations  17.5 us (6%)
  starting transfers between devices  12.4 us (4%)
  matrix products  5.76 us (2%)
  other arithmetic  5.59 us (2%)
  local copies, waits for them, and re-layouts  5.5 us (2%)
    all_gather x1, waiting for transfers between devices, on_device(): both = lax.all_gather(both, 'z')  73.2 us
    psum x6, blocking collectives, tp_sum(): return lax.psum(lax.psum(value, 'core'), 'y')  48.3 us
    all_to_all x1, blocking collectives, prefix_over_steps(): return lax.all_to_all(summed, 'z', 0, 0).reshape(rows, width)  24.6 us
    all_gather x1, blocking collectives, on_device(): gathered = lax.all_gather(flipped, 'y')  24.3 us
    all_gather x1, blocking collectives, on_device(): attended_all = lax.all_gather(attended, TP, axis=1, tiled=True)  15.7 us
    all_to_all x1, waiting for transfers between devices, prefix_over_steps(): lax.all_to_all(term.reshape(z_size, rows // z_size, width), 'z', 0, 0)  15.5 us
    all_gather x2, blocking collectives, on_device(): part = lax.all_gather(gathered[at * half:(at + 1) * half], 'core')  9.98 us
    all_to_all x1, waiting for transfers between devices, on_device(): query = jnp.sum(lax.all_to_all(partial, 'x', 0, 0), axis=0)  9.32 us
  transfers between devices with their start and end apart: 5, of which 3 were waited for; matrix products, arithmetic and copies ran while one was open for 3% of the time, Pallas kernels for 0%

profile of v2, /device:TPU:1, one launch (start us, length us, event | category | flops | bytes accessed | tf_op | source)
XLA Modules:
  0.0 277.1 jit_solution(7671201417849676276)
XLA Ops:
  7.2 0.0 copy-start
  7.2 0.0 all-gather.9.cloned.1.call-start
  7.2 1.6 fusion.12
  8.8 0.0 all-gather.9.cloned.1.call-update
  8.8 0.0 all-gather.7.cloned.1.call-start
  8.9 73.2 %all-gather.9.cloned.1.call-done = bf16[2048,640]{1,0:T(8,128)(2,1)} async-done(((bf16[128,640]{1,0:T(8,128)(2,1)}), bf16[2048,640]{1,0:T(8,128)(2,1)}) %all-gather.9.cloned.1.call-update) | async-done | bytes 2621456 | tf_op jit(solution)/shard_map/all_gather | solution.py:55
  82.0 2.3 slice.105
  84.3 0.0 all-gather.7.cloned.1.call-update
  84.3 1.1 reduce_sum.56
  85.4 0.1 fusion.5
  85.5 11.7 %psum.42 = f32[2,128]{1,0:T(2,128)S(1)} all-reduce(f32[2,128]{1,0:T(2,128)S(1)} %pad_maximum_fusion.1), channel_id=1, replica_groups=mesh['x'=4,'z'=16,'y'=4,'core'=2] {'core'}, use_global_device_ids=true, to_apply=%region_2.3 | all-reduce | flops 256 | bytes 2048 | tf_op jit(solution)/shard_map/psum | solution.py:22
  97.3 8.4 %psum.43 = f32[2,128]{1,0:T(2,128)S(1)} all-reduce(f32[2,128]{1,0:T(2,128)S(1)} %psum.42), channel_id=1, replica_groups=mesh['x'=4,'z'=16,'y'=4,'core'=2] {'y'}, use_global_device_ids=true, to_apply=%region_3.4 | all-reduce | flops 256 | bytes 2048 | tf_op jit(solution)/shard_map/psum | solution.py:22
  105.7 0.1 fusion.8
  105.9 0.7 collective-permute-start
  106.5 24.3 %all-gather = bf16[512,640]{1,0:T(8,128)(2,1)S(1)} all-gather(bf16[128,640]{1,0:T(8,128)(2,1)S(1)} %collective-permute-done), channel_id=2, replica_groups=mesh['x'=4,'z'=16,'y'=4,'core'=2] {'y'}, dimensions={0}, use_global_device_ids=true | all-gather | bytes 819200 | tf_op jit(solution)/shard_map/all_gather | solution.py:67
  130.9 0.1 fusion.22
  130.9 7.7 %all-gather.3 = bf16[4,128,640]{2,1,0:T(8,128)(2,1)S(1)} all-gather(bf16[2,128,640]{2,1,0:T(8,128)(2,1)S(1)} %bitcast.84), channel_id=5, replica_groups=mesh['x'=4,'z'=16,'y'=4,'core'=2] {'core'}, dimensions={0}, use_global_device_ids=true | all-gather | bytes 983040 | tf_op jit(solution)/shard_map/all_gather | solution.py:72
  138.6 2.3 all-gather.1
  140.9 1.3 slice.103
  142.2 0.0 copy-start.5
  142.2 0.0 copy-start.1
  142.3 0.0 copy-start.2
  142.3 0.5 convolution_bitcast_fusion
  142.8 0.5 convolution_bitcast_fusion.1
  143.3 0.9 pad_maximum_fusion
  144.2 5.4 %all-to-all-start = ((f32[4,128,384]{2,1,0:T(8,128)}), f32[4,128,384]{2,1,0:T(8,128)S(1)}, u32[]{:S(2)}, u32[]{:S(2)}) async-start(f32[4,128,384]{2,1,0:T(8,128)} %pad_maximum_fusion), calls=%async_computation | async-start | bytes 1572864 | tf_op jit(solution)/shard_map/all_to_all | solution.py:77
  149.6 0.6 fusion.23
  151.5 0.2 copy.19
  151.7 0.2 copy.22
  152.0 9.3 %all-to-all-done = f32[4,128,384]{2,1,0:T(8,128)S(1)} async-done(((f32[4,128,384]{2,1,0:T(8,128)}), f32[4,128,384]{2,1,0:T(8,128)S(1)}, u32[]{:S(2)}, u32[]{:S(2)}) %all-to-all-start) | async-done | bytes 786464 | tf_op jit(solution)/shard_map/all_to_all | solution.py:77
  161.4 0.1 copy.18
  161.5 0.1 multiply_reduce_fusion
  161.6 3.6 %psum.44 = f32[128]{0:T(128)S(1)} all-reduce(f32[128]{0:T(128)S(1)} %multiply_reduce_fusion), channel_id=1, replica_groups=mesh['x'=4,'z'=16,'y'=4,'core'=2] {'core'}, use_global_device_ids=true, to_apply=%region_6.7 | all-reduce | flops 128 | bytes 1024 | tf_op jit(solution)/shard_map/psum | solution.py:22
  165.3 6.1 %psum.45 = f32[128]{0:T(128)S(1)} all-reduce(f32[128]{0:T(128)S(1)} %psum.44), channel_id=1, replica_groups=mesh['x'=4,'z'=16,'y'=4,'core'=2] {'y'}, use_global_device_ids=true, to_apply=%region_7.8 | all-reduce | flops 128 | bytes 1024 | tf_op jit(solution)/shard_map/psum | solution.py:22
  171.4 0.6 fusion.24
  172.0 0.4 convolution_multiply_fusion
  172.3 0.9 convolution_convert_fusion
  173.2 15.7 %all_gather.42 = bf16[128,3072]{0,1:T(8,128)(2,1)S(1)} all-gather(bf16[128,384]{0,1:T(8,128)(2,1)S(1)} %bitcast.88), channel_id=1, replica_groups=mesh['x'=4,'z'=16,'y'=4,'core'=2] {'y','core'}, dimensions={1}, use_global_device_ids=true | all-gather | bytes 884736 | tf_op jit(solution)/shard_map/all_gather | solution.py:95
  188.9 2.9 %convolution_multiply_fusion.1 = f32[128,640]{1,0:T(8,128)S(1)} fusion(bf16[128,3072]{0,1:T(8,128)(2,1)S(1)} %all_gather.42, bf16[3072,640]{1,0:T(8,128)(2,1)} %all-gather.7.cloned.1.call-done, f32[]{:T(128)S(6)} %sub.35), kind=kOutput, calls=%fused_computation.6 | convolution fusion | flops 503398400 | bytes 5046276 | tf_op jit(solution)/shard_map/dot_general | solution.py:96
  191.8 0.8 fusion.10
  192.6 6.3 %all-to-all-start.1 = ((f32[16,8,640]{2,1,0:T(8,128)}), f32[16,8,640]{2,1,0:T(8,128)S(1)}, u32[]{:S(2)}, u32[]{:S(2)}) async-start(f32[16,8,640]{2,1,0:T(8,128)} %fusion.10), calls=%async_computation.1 | async-start | bytes 655360 | tf_op jit(solution)/shard_map/all_to_all | solution.py:34
  198.9 15.5 %all-to-all-done.1 = f32[16,8,640]{2,1,0:T(8,128)S(1)} async-done(((f32[16,8,640]{2,1,0:T(8,128)}), f32[16,8,640]{2,1,0:T(8,128)S(1)}, u32[]{:S(2)}, u32[]{:S(2)}) %all-to-all-start.1) | async-done | bytes 327712 | tf_op jit(solution)/shard_map/all_to_all | solution.py:34
  214.7 9.3 %all_gather.44 = f32[4,8,640]{2,1,0:T(8,128)S(1)} all-gather(f32[1,8,640]{2,1,0:T(8,128)S(1)} %get-tuple-element.3), channel_id=1, replica_groups=mesh['x'=4,'z'=16,'y'=4,'core'=2] {'x'}, dimensions={0}, use_global_device_ids=true | all-gather | bytes 102400 | tf_op jit(solution)/shard_map/all_gather | solution.py:38
  224.0 24.6 %all_to_all.15 = f32[16,8,640]{2,1,0:T(8,128)S(1)} all-to-all(f32[16,8,640]{2,1,0:T(8,128)S(1)} %broadcast_add_fusion), channel_id=1, replica_groups=mesh['x'=4,'z'=16,'y'=4,'core'=2] {'z'}, dimensions={0} | all-to-all | bytes 655360 | tf_op jit(solution)/shard_map/all_to_all | solution.py:44
  248.6 0.7 fusion.4
  249.3 11.0 %psum.46 = f32[]{:T(128)} all-reduce(f32[]{:T(128)} %fusion.4), channel_id=1, replica_groups=mesh['x'=4,'z'=16,'y'=4,'core'=2] {'core'}, use_global_device_ids=true, to_apply=%region_11.12 | all-reduce | flops 1 | bytes 8 | tf_op jit(solution)/shard_map/psum | solution.py:22
  260.3 7.4 %psum.47 = f32[]{:T(128)} all-reduce(f32[]{:T(128)} %psum.46), channel_id=1, replica_groups=mesh['x'=4,'z'=16,'y'=4,'core'=2] {'y'}, use_global_device_ids=true, to_apply=%region_12.13 | all-reduce | flops 1 | bytes 8 | tf_op jit(solution)/shard_map/psum | solution.py:22
  268.4 0.7 copy.42
  (34 shorter events, 0.2 us)
Async XLA Ops:
  7.2 78.2 %copy-start = (f32[1,128,640]{2,1,0:T(8,128)S(1)}, f32[1,128,640]{2,1,0:T(8,128)}, u32[]{:S(2)}) copy-start(f32[1,128,640]{2,1,0:T(8,128)} %param.8) | copy-start | bytes 983044
  7.2 98.5 %copy-start.3 = (f32[640]{0:T(1024)S(1)}, f32[640]{0:T(1024)}, u32[]{:S(2)}) copy-start(f32[640]{0:T(1024)} %param.12) | copy-start | bytes 7684
  7.2 74.9 %all-gather.9.cloned.1.call-start = ((), (), s32[]{:S(2)}) async-start(), calls=%async_computation.4 | async-start | bytes 2785280 | tf_op jit(solution)/shard_map/all_gather | solution.py:55
  8.8 180.0 %all-gather.7.cloned.1.call-start = ((), (), s32[]{:S(2)}) async-start(), calls=%async_computation.3 | async-start | bytes 4915200 | tf_op jit(solution)/shard_map/all_gather | solution.py:58
  105.9 0.7 collective-permute-start
  142.2 7.4 %copy-start.5 = (s32[64]{0:T(128)S(1)}, s32[64]{0:T(128)}, u32[]{:S(2)}) copy-start(s32[64]{0:T(128)} %param.9) | copy-start | bytes 772
  142.2 9.2 %copy-start.1 = (bf16[512,384]{1,0:T(8,128)(2,1)S(1)}, bf16[512,384]{1,0:T(8,128)(2,1)}, u32[]{:S(2)}) copy-start(bf16[512,384]{1,0:T(8,128)(2,1)} %param.10) | copy-start | bytes 1179652
  142.3 9.4 %copy-start.2 = (bf16[512,384]{1,0:T(8,128)(2,1)S(1)}, bf16[512,384]{1,0:T(8,128)(2,1)}, u32[]{:S(2)}) copy-start(bf16[512,384]{1,0:T(8,128)(2,1)} %param.11) | copy-start | bytes 1179652
  142.8 28.6 %copy-start.4 = (f32[384]{0:T(512)S(1)}, f32[384]{0:T(512)}, u32[]{:S(2)}) copy-start(f32[384]{0:T(512)} %param.13) | copy-start | bytes 4612
  144.2 17.1 %all-to-all-start = ((f32[4,128,384]{2,1,0:T(8,128)}), f32[4,128,384]{2,1,0:T(8,128)S(1)}, u32[]{:S(2)}, u32[]{:S(2)}) async-start(f32[4,128,384]{2,1,0:T(8,128)} %pad_maximum_fusion), calls=%async_computation | async-start | bytes 1572864 | tf_op jit(solution)/shard_map/all_to_all | solution.py:77
  192.6 21.9 %all-to-all-start.1 = ((f32[16,8,640]{2,1,0:T(8,128)}), f32[16,8,640]{2,1,0:T(8,128)S(1)}, u32[]{:S(2)}, u32[]{:S(2)}) async-start(f32[16,8,640]{2,1,0:T(8,128)} %fusion.10), calls=%async_computation.1 | async-start | bytes 655360 | tf_op jit(solution)/shard_map/all_to_all | solution.py:34
Sparse Core Ops, SparseCore 0:
  10.7 71.3 all-gather.8
  84.4 65.8 all-gather.6

commit v3 on v2

--- a/solution.py
+++ b/solution.py
@@ -53,9 +53,6 @@
     query_depth, query_cols = w_query.shape
     both = jnp.concatenate([jnp.pad(w_query, ((0, 0), (0, block - query_cols))), w_out])
     both = lax.all_gather(both, "z")
-    query_rows = both[:, :query_depth, :query_cols].reshape(-1, query_cols)
-    out_rows = both[:, query_depth:].reshape(-1, block)
-    out_rows = lax.all_gather(out_rows, "x", axis=0, tiled=True)
 
     sums = jnp.stack([jnp.sum(latent, axis=-1), jnp.sum(latent * latent, axis=-1)])
     sums = tp_sum(sums) / full_width
@@ -66,13 +63,15 @@
     flipped = transpose_plane(normed)
     gathered = lax.all_gather(flipped, "y")
     half = x_size // 2
-    query_weights = query_rows.reshape(2, block, query_cols)
-    partial = []
-    for at in range(2):
-        part = lax.all_gather(gathered[at * half : (at + 1) * half], "core")
-        partial.append(
-            jnp.einsum("cxtk,ckn->xtn", part, query_weights, preferred_element_type=jnp.float32)
-        )
+    parts = [lax.all_gather(gathered[at * half : (at + 1) * half], "core") for at in range(2)]
+    both, parts = lax.optimization_barrier((both, parts))
+    query_weights = both[:, :query_depth, :query_cols].reshape(2, block, query_cols)
+    out_rows = both[:, query_depth:].reshape(-1, block)
+    out_rows = lax.all_gather(out_rows, "x", axis=0, tiled=True)
+    partial = [
+        jnp.einsum("cxtk,ckn->xtn", part, query_weights, preferred_element_type=jnp.float32)
+        for part in parts
+    ]
     partial = jnp.concatenate(partial)
     query = jnp.sum(lax.all_to_all(partial, "x", 0, 0), axis=0)
 

time: 279 us -> 241 us (0.86)
  waiting for transfers between devices: 98.1 us -> 49.4 us
  starting transfers between devices: 12.4 us -> 16.8 us
  blocking collectives: 132 us -> 136 us
    all_gather x1, waiting for transfers between devices: 73.2 us -> 23.8 us  [on_device(): both = lax.all_gather(both, 'z')]
    psum x6, blocking collectives: 48.3 us -> 57 us  [tp_sum(): return lax.psum(lax.psum(value, 'core'), 'y')]
    all_to_all x1, starting transfers between devices: 6.31 us -> 12 us  [prefix_over_steps(): lax.all_to_all(term.reshape(z_size, rows // z_size, width), 'z', 0, 0)]
    all_gather x1, waiting for transfers between devices: 0.01 us -> 4.41 us  [on_device(): out_rows = lax.all_gather(out_rows, 'x', axis=0, tiled=True)]
    all_to_all x1, waiting for transfers between devices: 9.32 us -> 5.94 us  [on_device(): query = jnp.sum(lax.all_to_all(partial, 'x', 0, 0), axis=0)]
    all_gather x2, blocking collectives: 9.98 us -> 6.69 us  [on_device(): lax.all_gather(gathered[at * half:(at + 1) * half], 'core')]
  transfers between devices with their start and end apart: 5 -> 5, of which waited for: 3 -> 4; matrix products, arithmetic and copies ran while one was open for 3% -> 4% of each run, Pallas kernels for 0% -> 0%
where the time goes in v3:
time: 241 us; the launch traced here: 239 us
  blocking collectives  136 us (56%)
  waiting for transfers between devices  49.4 us (20%)
  between operations  17.5 us (7%)
  starting transfers between devices  16.8 us (7%)
  other arithmetic  7.51 us (3%)
  matrix products  5.76 us (2%)
  local copies, waits for them, and re-layouts  5.49 us (2%)
    psum x6, blocking collectives, tp_sum(): return lax.psum(lax.psum(value, 'core'), 'y')  57 us
    all_to_all x1, blocking collectives, prefix_over_steps(): return lax.all_to_all(summed, 'z', 0, 0).reshape(rows, width)  24.6 us
    all_gather x1, blocking collectives, on_device(): gathered = lax.all_gather(flipped, 'y')  23.8 us
    all_gather x1, waiting for transfers between devices, on_device(): both = lax.all_gather(both, 'z')  23.8 us
    all_to_all x1, waiting for transfers between devices, prefix_over_steps(): lax.all_to_all(term.reshape(z_size, rows // z_size, width), 'z', 0, 0)  15.2 us
    all_gather x1, blocking collectives, on_device(): attended_all = lax.all_gather(attended, TP, axis=1, tiled=True)  14.8 us
    all_to_all x1, starting transfers between devices, prefix_over_steps(): lax.all_to_all(term.reshape(z_size, rows // z_size, width), 'z', 0, 0)  12 us
    all_gather x1, blocking collectives, prefix_over_steps(): totals = lax.all_gather(running[-1], 'x')  9.3 us
  transfers between devices with their start and end apart: 5, of which 4 were waited for; matrix products, arithmetic and copies ran while one was open for 4% of the time, Pallas kernels for 0%

profile of v3, /device:TPU:1, one launch (start us, length us, event | category | flops | bytes accessed | tf_op | source)
XLA Modules:
  0.0 238.7 jit_solution(9869963438056065941)
XLA Ops:
  7.2 0.0 all-gather.9.cloned.1.call-start
  7.2 1.5 fusion.12
  8.7 0.0 all-gather.9.cloned.1.call-update
  8.8 0.0 all-gather.7.cloned.1.call-start
  8.8 1.1 reduce_sum.56
  9.9 1.1 fusion.5
  11.0 9.0 %psum.42 = f32[2,128]{1,0:T(2,128)S(1)} all-reduce(f32[2,128]{1,0:T(2,128)S(1)} %pad_maximum_fusion.1), channel_id=1, replica_groups=mesh['x'=4,'z'=16,'y'=4,'core'=2] {'core'}, use_global_device_ids=true, to_apply=%region_2.3 | all-reduce | flops 256 | bytes 2048 | tf_op jit(solution)/shard_map/psum | solution.py:22
  20.0 6.1 %psum.43 = f32[2,128]{1,0:T(2,128)S(1)} all-reduce(f32[2,128]{1,0:T(2,128)S(1)} %psum.42), channel_id=1, replica_groups=mesh['x'=4,'z'=16,'y'=4,'core'=2] {'y'}, use_global_device_ids=true, to_apply=%region_3.4 | all-reduce | flops 256 | bytes 2048 | tf_op jit(solution)/shard_map/psum | solution.py:22
  26.1 1.1 fusion.8
  27.2 0.7 collective-permute-start
  27.9 23.8 %all-gather.1 = bf16[512,640]{1,0:T(8,128)(2,1)S(1)} all-gather(bf16[128,640]{1,0:T(8,128)(2,1)S(1)} %collective-permute-done), channel_id=3, replica_groups=mesh['x'=4,'z'=16,'y'=4,'core'=2] {'y'}, dimensions={0}, use_global_device_ids=true | all-gather | bytes 819200 | tf_op jit(solution)/shard_map/all_gather | solution.py:64
  51.7 0.1 fusion.22
  51.8 4.4 %all-gather.3 = bf16[4,128,640]{2,1,0:T(8,128)(2,1)S(1)} all-gather(bf16[2,128,640]{2,1,0:T(8,128)(2,1)S(1)} %bitcast.84), channel_id=5, replica_groups=mesh['x'=4,'z'=16,'y'=4,'core'=2] {'core'}, dimensions={0}, use_global_device_ids=true | all-gather | bytes 983040 | tf_op jit(solution)/shard_map/all_gather | solution.py:66
  56.2 2.3 all-gather.2
  58.5 23.8 %all-gather.9.cloned.1.call-done = bf16[2048,640]{1,0:T(8,128)(2,1)} async-done(((bf16[128,640]{1,0:T(8,128)(2,1)}), bf16[2048,640]{1,0:T(8,128)(2,1)}) %all-gather.9.cloned.1.call-update) | async-done | bytes 2621456 | tf_op jit(solution)/shard_map/all_gather | solution.py:55
  82.3 2.3 slice.80
  84.5 0.0 all-gather.7.cloned.1.call-update
  84.5 1.3 slice.79
  85.9 0.0 copy-start.4
  85.9 0.0 copy-start.2
  85.9 0.5 convolution_bitcast_fusion.1
  86.4 0.0 copy-start.3
  86.4 0.5 convolution_bitcast_fusion
  86.9 0.9 pad_maximum_fusion
  87.9 4.0 %all-to-all-start = ((f32[4,128,384]{2,1,0:T(8,128)}), f32[4,128,384]{2,1,0:T(8,128)S(1)}, u32[]{:S(2)}, u32[]{:S(2)}) async-start(f32[4,128,384]{2,1,0:T(8,128)} %pad_maximum_fusion), calls=%async_computation | async-start | bytes 1572864 | tf_op jit(solution)/shard_map/all_to_all | solution.py:76
  91.9 0.6 fusion.23
  93.8 0.2 copy.19
  94.0 0.2 copy.22
  94.3 5.9 %all-to-all-done = f32[4,128,384]{2,1,0:T(8,128)S(1)} async-done(((f32[4,128,384]{2,1,0:T(8,128)}), f32[4,128,384]{2,1,0:T(8,128)S(1)}, u32[]{:S(2)}, u32[]{:S(2)}) %all-to-all-start) | async-done | bytes 786464 | tf_op jit(solution)/shard_map/all_to_all | solution.py:76
  100.3 0.1 copy.18
  100.4 0.1 multiply_reduce_fusion
  100.5 13.0 %psum.44 = f32[128]{0:T(128)S(1)} all-reduce(f32[128]{0:T(128)S(1)} %multiply_reduce_fusion), channel_id=1, replica_groups=mesh['x'=4,'z'=16,'y'=4,'core'=2] {'core'}, use_global_device_ids=true, to_apply=%region_6.7 | all-reduce | flops 128 | bytes 1024 | tf_op jit(solution)/shard_map/psum | solution.py:22
  113.5 9.1 %psum.45 = f32[128]{0:T(128)S(1)} all-reduce(f32[128]{0:T(128)S(1)} %psum.44), channel_id=1, replica_groups=mesh['x'=4,'z'=16,'y'=4,'core'=2] {'y'}, use_global_device_ids=true, to_apply=%region_7.8 | all-reduce | flops 128 | bytes 1024 | tf_op jit(solution)/shard_map/psum | solution.py:22
  122.6 0.6 fusion.24
  123.1 0.4 convolution_multiply_fusion
  123.5 0.9 convolution_convert_fusion
  124.4 14.8 %all_gather.42 = bf16[128,3072]{0,1:T(8,128)(2,1)S(1)} all-gather(bf16[128,384]{0,1:T(8,128)(2,1)S(1)} %bitcast.88), channel_id=1, replica_groups=mesh['x'=4,'z'=16,'y'=4,'core'=2] {'y','core'}, dimensions={1}, use_global_device_ids=true | all-gather | bytes 884736 | tf_op jit(solution)/shard_map/all_gather | solution.py:94
  139.2 4.4 %all-gather.7.cloned.1.call-done = bf16[3072,640]{1,0:T(8,128)(2,1)} async-done(((bf16[768,640]{1,0:T(8,128)(2,1)}), bf16[3072,640]{1,0:T(8,128)(2,1)}) %all-gather.7.cloned.1.call-update) | async-done | bytes 3932176 | tf_op jit(solution)/shard_map/all_gather | solution.py:70
  143.6 2.9 %convolution_multiply_fusion.1 = f32[128,640]{1,0:T(8,128)S(1)} fusion(bf16[128,3072]{0,1:T(8,128)(2,1)S(1)} %all_gather.42, bf16[3072,640]{1,0:T(8,128)(2,1)} %all-gather.7.cloned.1.call-done, f32[]{:T(128)S(6)} %sub.35), kind=kOutput, calls=%fused_computation.6 | convolution fusion | flops 503398400 | bytes 5046276 | tf_op jit(solution)/shard_map/dot_general | solution.py:95
  146.6 0.8 fusion.10
  147.3 12.0 %all-to-all-start.1 = ((f32[16,8,640]{2,1,0:T(8,128)}), f32[16,8,640]{2,1,0:T(8,128)S(1)}, u32[]{:S(2)}, u32[]{:S(2)}) async-start(f32[16,8,640]{2,1,0:T(8,128)} %fusion.10), calls=%async_computation.1 | async-start | bytes 655360 | tf_op jit(solution)/shard_map/all_to_all | solution.py:34
  159.3 15.2 %all-to-all-done.1 = f32[16,8,640]{2,1,0:T(8,128)S(1)} async-done(((f32[16,8,640]{2,1,0:T(8,128)}), f32[16,8,640]{2,1,0:T(8,128)S(1)}, u32[]{:S(2)}, u32[]{:S(2)}) %all-to-all-start.1) | async-done | bytes 327712 | tf_op jit(solution)/shard_map/all_to_all | solution.py:34
  174.8 9.3 %all_gather.44 = f32[4,8,640]{2,1,0:T(8,128)S(1)} all-gather(f32[1,8,640]{2,1,0:T(8,128)S(1)} %get-tuple-element.9), channel_id=1, replica_groups=mesh['x'=4,'z'=16,'y'=4,'core'=2] {'x'}, dimensions={0}, use_global_device_ids=true | all-gather | bytes 102400 | tf_op jit(solution)/shard_map/all_gather | solution.py:38
  184.1 24.6 %all_to_all.15 = f32[16,8,640]{2,1,0:T(8,128)S(1)} all-to-all(f32[16,8,640]{2,1,0:T(8,128)S(1)} %broadcast_add_fusion), channel_id=1, replica_groups=mesh['x'=4,'z'=16,'y'=4,'core'=2] {'z'}, dimensions={0} | all-to-all | bytes 655360 | tf_op jit(solution)/shard_map/all_to_all | solution.py:44
  208.7 0.7 fusion.4
  209.4 10.9 %psum.46 = f32[]{:T(128)} all-reduce(f32[]{:T(128)} %fusion.4), channel_id=1, replica_groups=mesh['x'=4,'z'=16,'y'=4,'core'=2] {'core'}, use_global_device_ids=true, to_apply=%region_11.12 | all-reduce | flops 1 | bytes 8 | tf_op jit(solution)/shard_map/psum | solution.py:22
  220.3 9.1 %psum.47 = f32[]{:T(128)} all-reduce(f32[]{:T(128)} %psum.46), channel_id=1, replica_groups=mesh['x'=4,'z'=16,'y'=4,'core'=2] {'y'}, use_global_device_ids=true, to_apply=%region_12.13 | all-reduce | flops 1 | bytes 8 | tf_op jit(solution)/shard_map/psum | solution.py:22
  230.0 0.7 copy.42
  (32 shorter events, 0.2 us)
Async XLA Ops:
  7.2 75.1 %all-gather.9.cloned.1.call-start = ((), (), s32[]{:S(2)}) async-start(), calls=%async_computation.4 | async-start | bytes 2785280 | tf_op jit(solution)/shard_map/all_gather | solution.py:55
  8.8 134.8 %all-gather.7.cloned.1.call-start = ((), (), s32[]{:S(2)}) async-start(), calls=%async_computation.3 | async-start | bytes 4915200 | tf_op jit(solution)/shard_map/all_gather | solution.py:70
  27.2 0.7 collective-permute-start
  85.9 6.0 %copy-start.4 = (s32[64]{0:T(128)S(1)}, s32[64]{0:T(128)}, u32[]{:S(2)}) copy-start(s32[64]{0:T(128)} %param.9) | copy-start | bytes 772
  85.9 7.9 %copy-start.1 = (bf16[512,384]{1,0:T(8,128)(2,1)S(1)}, bf16[512,384]{1,0:T(8,128)(2,1)}, u32[]{:S(2)}) copy-start(bf16[512,384]{1,0:T(8,128)(2,1)} %param.10) | copy-start | bytes 1179652
  85.9 8.1 %copy-start.2 = (bf16[512,384]{1,0:T(8,128)(2,1)S(1)}, bf16[512,384]{1,0:T(8,128)(2,1)}, u32[]{:S(2)}) copy-start(bf16[512,384]{1,0:T(8,128)(2,1)} %param.11) | copy-start | bytes 1179652
  86.4 36.1 %copy-start.3 = (f32[384]{0:T(512)S(1)}, f32[384]{0:T(512)}, u32[]{:S(2)}) copy-start(f32[384]{0:T(512)} %param.13) | copy-start | bytes 4612
  87.9 12.4 %all-to-all-start = ((f32[4,128,384]{2,1,0:T(8,128)}), f32[4,128,384]{2,1,0:T(8,128)S(1)}, u32[]{:S(2)}, u32[]{:S(2)}) async-start(f32[4,128,384]{2,1,0:T(8,128)} %pad_maximum_fusion), calls=%async_computation | async-start | bytes 1572864 | tf_op jit(solution)/shard_map/all_to_all | solution.py:76
  123.5 23.0 %copy-start = (f32[1,128,640]{2,1,0:T(8,128)S(1)}, f32[1,128,640]{2,1,0:T(8,128)}, u32[]{:S(2)}) copy-start(f32[1,128,640]{2,1,0:T(8,128)} %param.8) | copy-start | bytes 983044
  147.3 27.2 %all-to-all-start.1 = ((f32[16,8,640]{2,1,0:T(8,128)}), f32[16,8,640]{2,1,0:T(8,128)S(1)}, u32[]{:S(2)}, u32[]{:S(2)}) async-start(f32[16,8,640]{2,1,0:T(8,128)} %fusion.10), calls=%async_computation.1 | async-start | bytes 655360 | tf_op jit(solution)/shard_map/all_to_all | solution.py:34
Sparse Core Ops, SparseCore 0:
  10.7 71.5 all-gather.8
  84.7 58.8 all-gather.6

commit v4 on v3

v4 whole, which is shorter than its diff:
```python
import math

import jax
import jax.numpy as jnp
from jax import lax
from jax.sharding import Mesh
from jax.sharding import PartitionSpec as P

HD = 128
STEP = ("x", "z")
TP = ("y", "core")

epsilon = 1e-06


def sigma_of(levels):
    scaled = levels.astype(jnp.float32) / 1000.0
    return 5.0 * scaled / (1.0 + 4.0 * scaled)


def tp_sum(value):
    return lax.psum(lax.psum(value, "core"), "y")


def transpose_plane(value):
    side = lax.axis_size("x")
    pairs = [(a * side + b, b * side + a) for a in range(side) for b in range(side)]
    return lax.ppermute(value, ("x", "y"), pairs)


def on_device(trajectory, timesteps, context_keys, context_values, ln_gain, q_gain, w_query, w_out):
    latent = trajectory[0]
    token_count, block = latent.shape
    full_width = block * lax.axis_size(TP)
    x_size = lax.axis_size("x")

    z_size = lax.axis_size("z")
    x_here = lax.axis_index("x")
    slice_tokens = token_count // z_size

    rows_here = lax.all_to_all(latent.reshape(z_size, slice_tokens, block), "z", 0, 0)

    out_depth = w_out.shape[0]
    out_rows = lax.all_gather(jnp.pad(w_out, ((0, 16), (0, 0))), "z")

    sums = jnp.stack([jnp.sum(latent, axis=-1), jnp.sum(latent * latent, axis=-1)])
    sums = tp_sum(sums) / full_width
    row_mean, row_square = sums[0][:, None], sums[1][:, None]
    row_var = row_square - row_mean * row_mean
    normed = ((latent - row_mean) * lax.rsqrt(row_var + epsilon) * ln_gain).astype(jnp.bfloat16)

    w_query, normed = lax.optimization_barrier((w_query, normed))
    query_rows = lax.all_gather(w_query, "z")
    flipped = transpose_plane(normed)
    gathered = lax.all_gather(flipped, "y")
    half = x_size // 2
    parts = [lax.all_gather(gathered[at * half : (at + 1) * half], "core") for at in range(2)]
    query_weights = query_rows.reshape(2, block, w_query.shape[1])
    partial = [
        jnp.einsum("cxtk,ckn->xtn", part, query_weights, preferred_element_type=jnp.float32)
        for part in parts
    ]
    partial = jnp.concatenate(partial)
    out_rows, partial = lax.optimization_barrier((out_rows, partial))
    out_rows = out_rows[:, :out_depth].reshape(-1, block)
    out_rows = lax.all_gather(out_rows, "x", axis=0, tiled=True)
    query = jnp.sum(lax.all_to_all(partial, "x", 0, 0), axis=0)

    query_width = query.shape[1] * lax.axis_size(TP)
    square_sum = tp_sum(jnp.sum(query * query, axis=-1))
    query_scale = lax.rsqrt(square_sum / query_width + epsilon)[:, None]
    q_normed = (query * query_scale * q_gain).astype(jnp.bfloat16)
    local_heads = query.shape[1] // HD
    q_heads = q_normed.reshape(token_count, local_heads, HD)
    key_heads = context_keys.reshape(context_keys.shape[0], local_heads, HD)
    value_heads = context_values.reshape(context_values.shape[0], local_heads, HD)
    scores = jnp.einsum(
        "thd,khd->htk", q_heads, key_heads, preferred_element_type=jnp.float32
    ) / math.sqrt(HD)
    soft_weights = jax.nn.softmax(scores, axis=-1).astype(jnp.bfloat16)
    attended = jnp.einsum(
        "htk,khd->thd", soft_weights, value_heads, preferred_element_type=jnp.float32
    )
    attended = attended.reshape(token_count, local_heads * HD).astype(jnp.bfloat16)
    attended = attended.reshape(z_size, slice_tokens, -1)
    attended = lax.all_to_all(attended, "z", 0, 0).reshape(token_count, -1)
    attended_all = lax.all_gather(attended, TP, axis=1, tiled=True)
    velocity = jnp.dot(attended_all, out_rows, preferred_element_type=jnp.float32)
    velocity = velocity.reshape(z_size, slice_tokens, block)

    later = jnp.concatenate([timesteps[1:], jnp.zeros((1,), timesteps.dtype)])
    step_sizes = sigma_of(later) - sigma_of(timesteps)
    step_sizes = lax.dynamic_slice_in_dim(step_sizes, x_here * z_size, z_size)
    drift = step_sizes[:, None, None] * velocity

    running = [drift[0]]
    for at in range(1, z_size):
        running.append(running[-1] + drift[at])
    start = jnp.where(x_here == 0, rows_here[0], 0.0)
    totals = lax.all_gather(running[-1] + start, "x")
    for at in range(x_size - 1):
        start = start + jnp.where(at < x_here, totals[at], 0.0)
    ends = jnp.stack([start] + [start + one for one in running])
    new_rows = lax.all_to_all(ends[1:], "z", 0, 0).reshape(token_count, block)

    change = ends[:-1] - rows_here
    change_sum = jnp.sum(change * change, axis=(1, 2))
    change_sum = tp_sum(jnp.broadcast_to(change_sum[:, None, None], (z_size, 1, 128)))
    change_sum = jnp.sum(lax.all_to_all(change_sum, "z", 0, 0)[:, 0, 0])
    error_value = change_sum / (token_count * full_width)
    return (new_rows[None], error_value.reshape(1))


def solution(mesh):
    fine = Mesh(mesh.devices.reshape(4, 16, 4, 2), ("x", "z", "y", "core"))
    placed = (
        P(STEP, None, TP),
        P(),
        P(None, TP),
        P(None, TP),
        P(TP),
        P(TP),
        P(STEP, TP),
        P(STEP, TP),
    )
    return jax.shard_map(
        on_device,
        mesh=fine,
        in_specs=placed,
        out_specs=(P(STEP, None, TP), P(STEP)),
        check_vma=False,
    )
```

time: 241 us -> 262 us (1.087)
  the two profiles are of different devices: /device:TPU:1 before, /device:TPU:32 now
where the time goes in v4:
time: 262 us; the launch traced here: 261 us
  blocking collectives  169 us (65%)
  waiting for transfers between devices  31.1 us (12%)
  other arithmetic  20.2 us (8%)
  between operations  16 us (6%)
  starting transfers between devices  13.7 us (5%)
  matrix products  5.71 us (2%)
  local copies, waits for them, and re-layouts  5.44 us (2%)
    all_gather x1, blocking collectives, on_device(): query_rows = lax.all_gather(w_query, 'z')  42.3 us
    psum x6, blocking collectives, tp_sum(): return lax.psum(lax.psum(value, 'core'), 'y')  37.8 us
    all_to_all x1, blocking collectives, on_device(): change_sum = jnp.sum(lax.all_to_all(change_sum, 'z', 0, 0)[:, 0, 0])  21.8 us
    all_to_all x1, blocking collectives, on_device(): attended = lax.all_to_all(attended, 'z', 0, 0).reshape(token_count, -1)  19.8 us
    all_to_all x1, waiting for transfers between devices, on_device(): new_rows = lax.all_to_all(ends[1:], 'z', 0, 0).reshape(token_count, block)  17.4 us
    all_gather x1, blocking collectives, on_device(): gathered = lax.all_gather(flipped, 'y')  17.1 us
    all_gather x1, blocking collectives, on_device(): attended_all = lax.all_gather(attended, TP, axis=1, tiled=True)  13.8 us
    unnamed x16, other arithmetic  13.5 us
  transfers between devices with their start and end apart: 6, of which 3 were waited for; matrix products, arithmetic and copies ran while one was open for 4% of the time, Pallas kernels for 0%

profile of v4, /device:TPU:32, one launch (start us, length us, event | category | flops | bytes accessed | tf_op | source)
XLA Modules:
  0.0 261.1 jit_solution(9280203437601210579)
XLA Ops:
  7.2 1.5 pad.4
  8.8 1.1 fusion.5
  9.8 1.1 reduce_sum.65
  10.9 2.5 psum.42
  13.4 10.7 %psum.43 = f32[2,128]{1,0:T(2,128)S(1)} all-reduce(f32[2,128]{1,0:T(2,128)S(1)} %psum.42), channel_id=1, replica_groups=mesh['x'=4,'z'=16,'y'=4,'core'=2] {'y'}, use_global_device_ids=true, to_apply=%region_3.4 | all-reduce | flops 256 | bytes 2048 | tf_op jit(solution)/shard_map/psum | solution.py:22
  24.2 1.1 fusion.8
  25.3 0.7 collective-permute-start
  25.9 42.3 %all-gather.3 = bf16[1280,384]{1,0:T(8,128)(2,1)S(1)} all-gather(bf16[80,384]{1,0:T(8,128)(2,1)} %param.14), channel_id=5, replica_groups=mesh['x'=4,'z'=16,'y'=4,'core'=2] {'z'}, dimensions={0}, use_global_device_ids=true | all-gather | bytes 1044480 | tf_op jit(solution)/shard_map/all_gather | solution.py:53
  68.2 17.1 %all-gather.1 = bf16[512,640]{1,0:T(8,128)(2,1)S(1)} all-gather(bf16[128,640]{1,0:T(8,128)(2,1)S(1)} %collective-permute-done), channel_id=3, replica_groups=mesh['x'=4,'z'=16,'y'=4,'core'=2] {'y'}, dimensions={0}, use_global_device_ids=true | all-gather | bytes 819200 | tf_op jit(solution)/shard_map/all_gather | solution.py:55
  85.4 2.3 all-gather.4
  87.7 2.3 all-gather.2
  91.0 1.0 pad_maximum_fusion
  91.9 2.3 slice.89
  94.2 3.5 %all-to-all-start.1 = ((f32[4,128,384]{2,1,0:T(8,128)}), f32[4,128,384]{2,1,0:T(8,128)S(1)}, u32[]{:S(2)}, u32[]{:S(2)}) async-start(f32[4,128,384]{2,1,0:T(8,128)} %pad_maximum_fusion), calls=%async_computation.1 | async-start | bytes 1572864 | tf_op jit(solution)/shard_map/all_to_all | solution.py:67
  98.1 12.4 %all-to-all-done.1 = f32[4,128,384]{2,1,0:T(8,128)S(1)} async-done(((f32[4,128,384]{2,1,0:T(8,128)}), f32[4,128,384]{2,1,0:T(8,128)S(1)}, u32[]{:S(2)}, u32[]{:S(2)}) %all-to-all-start.1) | async-done | bytes 786464 | tf_op jit(solution)/shard_map/all_to_all | solution.py:67
  110.9 2.5 psum.44
  113.3 10.1 %psum.45 = f32[128]{0:T(128)S(1)} all-reduce(f32[128]{0:T(128)S(1)} %psum.44), channel_id=1, replica_groups=mesh['x'=4,'z'=16,'y'=4,'core'=2] {'y'}, use_global_device_ids=true, to_apply=%region_7.8 | all-reduce | flops 128 | bytes 1024 | tf_op jit(solution)/shard_map/psum | solution.py:22
  123.4 0.6 fusion.21
  124.4 0.8 fusion.4
  125.4 19.8 %all_to_all.25 = bf16[16,8,384]{2,1,0:T(8,128)(2,1)S(1)} all-to-all(bf16[16,8,384]{2,1,0:T(8,128)(2,1)S(1)} %convert_element_type.35), channel_id=1, replica_groups=mesh['x'=4,'z'=16,'y'=4,'core'=2] {'z'}, dimensions={0} | all-to-all | bytes 196608 | tf_op jit(solution)/shard_map/all_to_all | solution.py:86
  145.2 4.6 %all-to-all-start = ((f32[16,8,640]{2,1,0:T(8,128)}), f32[16,8,640]{2,1,0:T(8,128)S(1)}, u32[]{:S(2)}, u32[]{:S(2)}) async-start(f32[16,8,640]{2,1,0:T(8,128)} %bitcast), calls=%async_computation | async-start | bytes 655360 | tf_op jit(solution)/shard_map/all_to_all | solution.py:41
  150.1 13.8 %all_gather.50 = bf16[128,3072]{1,0:T(8,128)(2,1)S(1)} all-gather(bf16[128,384]{1,0:T(8,128)(2,1)S(1)} %bitcast.76), channel_id=1, replica_groups=mesh['x'=4,'z'=16,'y'=4,'core'=2] {'y','core'}, dimensions={1}, use_global_device_ids=true | all-gather | bytes 884736 | tf_op jit(solution)/shard_map/all_gather | solution.py:87
  163.9 2.9 %fusion.3 = f32[16,8,640]{2,1,0:T(8,128)S(1)} fusion(bf16[128,3072]{1,0:T(8,128)(2,1)S(1)} %all_gather.50, bf16[3072,640]{1,0:T(8,128)(2,1)} %all-gather.8.cloned.1.call-done, f32[16]{0:T(128)S(1)} %dynamic_slice.3), kind=kOutput, calls=%fused_computation.7 | convolution fusion | flops 503398400 | bytes 5046336 | tf_op jit(solution)/shard_map/dot_general | solution.py:88
  166.8 1.3 all-to-all-done
  168.1 11.9 %all_gather.52 = f32[4,8,640]{2,1,0:T(8,128)S(1)} all-gather(f32[1,8,640]{2,1,0:T(8,128)S(1)} %get-tuple-element.12), channel_id=1, replica_groups=mesh['x'=4,'z'=16,'y'=4,'core'=2] {'x'}, dimensions={0}, use_global_device_ids=true | all-gather | bytes 102400 | tf_op jit(solution)/shard_map/all_gather | solution.py:100
  180.0 0.6 constant_dynamic-update-slice_fusion.30
  180.6 0.6 constant_dynamic-update-slice_fusion.29
  181.3 1.3 constant_dynamic-update-slice_fusion.28
  182.6 0.6 constant_dynamic-update-slice_fusion.27
  183.2 1.3 constant_dynamic-update-slice_fusion.26
  184.5 0.6 constant_dynamic-update-slice_fusion.25
  185.2 1.3 constant_dynamic-update-slice_fusion.24
  186.5 0.6 constant_dynamic-update-slice_fusion.23
  187.1 1.3 constant_dynamic-update-slice_fusion.22
  188.4 0.6 constant_dynamic-update-slice_fusion.21
  189.1 1.3 constant_dynamic-update-slice_fusion.20
  190.4 0.6 constant_dynamic-update-slice_fusion.19
  191.0 1.3 constant_dynamic-update-slice_fusion.18
  192.3 0.6 constant_dynamic-update-slice_fusion.17
  193.0 0.6 constant_dynamic-update-slice_fusion.1
  193.6 1.3 constant_dynamic-update-slice_fusion.16
  195.2 2.5 psum.46
  197.7 9.5 %psum.47 = f32[16,1,128]{2,1,0:T(1,128)S(1)} all-reduce(f32[16,1,128]{2,1,0:T(1,128)S(1)} %psum.46), channel_id=1, replica_groups=mesh['x'=4,'z'=16,'y'=4,'core'=2] {'y'}, use_global_device_ids=true, to_apply=%region_12.13 | all-reduce | flops 2048 | bytes 16384 | tf_op jit(solution)/shard_map/psum | solution.py:22
  207.2 21.8 %all_to_all.26 = f32[16,1,128]{2,1,0:T(1,128)S(1)} all-to-all(f32[16,1,128]{2,1,0:T(1,128)S(1)} %psum.47), channel_id=1, replica_groups=mesh['x'=4,'z'=16,'y'=4,'core'=2] {'z'}, dimensions={0} | all-to-all | bytes 16384 | tf_op jit(solution)/shard_map/all_to_all | solution.py:109
  229.0 4.8 %all-to-all-start.3 = ((f32[16,8,640]{2,1,0:T(8,128)}), f32[16,8,640]{2,1,0:T(8,128)S(1)}, u32[]{:S(2)}, u32[]{:S(2)}) async-start(f32[16,8,640]{2,1,0:T(8,128)} %get-tuple-element.38), calls=%async_computation.3 | async-start | bytes 655360 | tf_op jit(solution)/shard_map/all_to_all | solution.py:104
  233.7 0.6 slice_reduce_fusion
  235.0 17.4 %all-to-all-done.3 = f32[16,8,640]{2,1,0:T(8,128)S(1)} async-done(((f32[16,8,640]{2,1,0:T(8,128)}), f32[16,8,640]{2,1,0:T(8,128)S(1)}, u32[]{:S(2)}, u32[]{:S(2)}) %all-to-all-start.3) | async-done | bytes 327712 | tf_op jit(solution)/shard_map/all_to_all | solution.py:104
  252.4 0.7 copy.78
  (40 shorter events, 3.0 us)
Async XLA Ops:
  7.2 84.8 %all-gather.10.cloned.1.call-start = ((), (), s32[]{:S(2)}) async-start(), calls=%async_computation.6 | async-start | bytes 1392640 | tf_op jit(solution)/shard_map/all_gather | solution.py:44
  8.7 155.2 %all-gather.8.cloned.1.call-start = ((), (), s32[]{:S(2)}) async-start(), calls=%async_computation.5 | async-start | bytes 4915200 | tf_op jit(solution)/shard_map/all_gather | solution.py:66
  25.3 43.0 %collective-permute-start = (bf16[128,640]{1,0:T(8,128)(2,1)S(1)}, bf16[128,640]{1,0:T(8,128)(2,1)S(1)}, u32[]{:S(2)}, u32[]{:S(2)}) collective-permute-start(bf16[128,640]{1,0:T(8,128)(2,1)S(1)} %fusion.8), channel_id=1, source_target_pairs={{0,0},{2,128},{4,256},{6,384},{128,2},{130,130},{132,258},{134,386... | collective-permute-start | bytes 491528 | tf_op jit(solution)/shard_map/ppermute | solution.py:28
  90.4 7.3 %copy-start.1 = (bf16[512,384]{1,0:T(8,128)(2,1)S(1)}, bf16[512,384]{1,0:T(8,128)(2,1)}, u32[]{:S(2)}) copy-start(bf16[512,384]{1,0:T(8,128)(2,1)} %param.10) | copy-start | bytes 1179652
  91.0 7.0 %copy-start.2 = (bf16[512,384]{1,0:T(8,128)(2,1)S(1)}, bf16[512,384]{1,0:T(8,128)(2,1)}, u32[]{:S(2)}) copy-start(bf16[512,384]{1,0:T(8,128)(2,1)} %param.11) | copy-start | bytes 1179652
  91.9 31.5 %copy-start.3 = (f32[384]{0:T(512)S(1)}, f32[384]{0:T(512)}, u32[]{:S(2)}) copy-start(f32[384]{0:T(512)} %param.13) | copy-start | bytes 4612
  94.2 16.3 %all-to-all-start.1 = ((f32[4,128,384]{2,1,0:T(8,128)}), f32[4,128,384]{2,1,0:T(8,128)S(1)}, u32[]{:S(2)}, u32[]{:S(2)}) async-start(f32[4,128,384]{2,1,0:T(8,128)} %pad_maximum_fusion), calls=%async_computation.1 | async-start | bytes 1572864 | tf_op jit(solution)/shard_map/all_to_all | solution.py:67
  110.7 39.1 %copy-start.4 = (s32[64]{0:T(128)S(1)}, s32[64]{0:T(128)}, u32[]{:S(2)}) copy-start(s32[64]{0:T(128)} %param.9) | copy-start | bytes 772
  145.2 22.9 %all-to-all-start = ((f32[16,8,640]{2,1,0:T(8,128)}), f32[16,8,640]{2,1,0:T(8,128)S(1)}, u32[]{:S(2)}, u32[]{:S(2)}) async-start(f32[16,8,640]{2,1,0:T(8,128)} %bitcast), calls=%async_computation | async-start | bytes 655360 | tf_op jit(solution)/shard_map/all_to_all | solution.py:41
  166.8 14.4 %copy-start = (f32[16,8,640]{2,1,0:T(8,128)}, f32[16,8,640]{2,1,0:T(8,128)S(1)}, u32[]{:S(2)}) copy-start(f32[16,8,640]{2,1,0:T(8,128)S(1)} %fusion.3) | copy-start | bytes 983044
  229.0 23.4 %all-to-all-start.3 = ((f32[16,8,640]{2,1,0:T(8,128)}), f32[16,8,640]{2,1,0:T(8,128)S(1)}, u32[]{:S(2)}, u32[]{:S(2)}) async-start(f32[16,8,640]{2,1,0:T(8,128)} %get-tuple-element.38), calls=%async_computation.3 | async-start | bytes 655360 | tf_op jit(solution)/shard_map/all_to_all | solution.py:104
Sparse Core Ops, SparseCore 0:
  10.7 76.1 all-gather.9
  94.3 49.2 all-gather.7

commit v5 on v4

--- a/solution.py
+++ b/solution.py
@@ -40,6 +40,9 @@
 
     rows_here = lax.all_to_all(latent.reshape(z_size, slice_tokens, block), "z", 0, 0)
 
+    depth, cols = w_query.shape
+    query_rows = lax.all_to_all(jnp.broadcast_to(w_query, (z_size, depth, cols)), "z", 0, 0)
+
     out_depth = w_out.shape[0]
     out_rows = lax.all_gather(jnp.pad(w_out, ((0, 16), (0, 0))), "z")
 
@@ -49,22 +52,20 @@
     row_var = row_square - row_mean * row_mean
     normed = ((latent - row_mean) * lax.rsqrt(row_var + epsilon) * ln_gain).astype(jnp.bfloat16)
 
-    w_query, normed = lax.optimization_barrier((w_query, normed))
-    query_rows = lax.all_gather(w_query, "z")
     flipped = transpose_plane(normed)
     gathered = lax.all_gather(flipped, "y")
     half = x_size // 2
     parts = [lax.all_gather(gathered[at * half : (at + 1) * half], "core") for at in range(2)]
-    query_weights = query_rows.reshape(2, block, w_query.shape[1])
+    query_weights = query_rows.reshape(2, block, cols)
     partial = [
         jnp.einsum("cxtk,ckn->xtn", part, query_weights, preferred_element_type=jnp.float32)
         for part in parts
     ]
     partial = jnp.concatenate(partial)
-    out_rows, partial = lax.optimization_barrier((out_rows, partial))
+    query = jnp.sum(lax.all_to_all(partial, "x", 0, 0), axis=0)
+    out_rows, query = lax.optimization_barrier((out_rows, query))
     out_rows = out_rows[:, :out_depth].reshape(-1, block)
     out_rows = lax.all_gather(out_rows, "x", axis=0, tiled=True)
-    query = jnp.sum(lax.all_to_all(partial, "x", 0, 0), axis=0)
 
     query_width = query.shape[1] * lax.axis_size(TP)
     square_sum = tp_sum(jnp.sum(query * query, axis=-1))
@@ -93,20 +94,22 @@
     step_sizes = lax.dynamic_slice_in_dim(step_sizes, x_here * z_size, z_size)
     drift = step_sizes[:, None, None] * velocity
 
-    running = [drift[0]]
-    for at in range(1, z_size):
-        running.append(running[-1] + drift[at])
+    running = drift
+    reach = 1
+    while reach < z_size:
+        running = running + jnp.pad(running[:-reach], ((reach, 0), (0, 0), (0, 0)))
+        reach *= 2
     start = jnp.where(x_here == 0, rows_here[0], 0.0)
     totals = lax.all_gather(running[-1] + start, "x")
     for at in range(x_size - 1):
         start = start + jnp.where(at < x_here, totals[at], 0.0)
-    ends = jnp.stack([start] + [start + one for one in running])
-    new_rows = lax.all_to_all(ends[1:], "z", 0, 0).reshape(token_count, block)
-
-    change = ends[:-1] - rows_here
-    change_sum = jnp.sum(change * change, axis=(1, 2))
-    change_sum = tp_sum(jnp.broadcast_to(change_sum[:, None, None], (z_size, 1, 128)))
-    change_sum = jnp.sum(lax.all_to_all(change_sum, "z", 0, 0)[:, 0, 0])
+    change = start + jnp.pad(running[:-1], ((1, 0), (0, 0), (0, 0))) - rows_here
+    change_sum = jnp.sum(change * change, axis=(1, 2), keepdims=True)
+    change_sum = jnp.broadcast_to(change_sum, (z_size, slice_tokens, HD))
+    sent = jnp.concatenate([start + running, change_sum], axis=2)
+    got = lax.all_to_all(sent, "z", 0, 0)
+    new_rows = got[:, :, :block].reshape(token_count, block)
+    change_sum = tp_sum(jnp.sum(got[:, 0, block]))
     error_value = change_sum / (token_count * full_width)
     return (new_rows[None], error_value.reshape(1))
 

time: 262 us -> 240 us (0.916)
  the two profiles are of different devices: /device:TPU:32 before, /device:TPU:1 now
where the time goes in v5:
time: 240 us; the launch traced here: 238 us
  blocking collectives  148 us (62%)
  waiting for transfers between devices  29.1 us (12%)
  starting transfers between devices  27 us (11%)
  between operations  16.1 us (7%)
  local copies, waits for them, and re-layouts  8.07 us (3%)
  matrix products  5.57 us (2%)
  other arithmetic  4.71 us (2%)
    psum x6, blocking collectives, tp_sum(): return lax.psum(lax.psum(value, 'core'), 'y')  48.5 us
    all_to_all x1, blocking collectives, on_device(): got = lax.all_to_all(sent, 'z', 0, 0)  26.5 us
    all_gather x1, blocking collectives, on_device(): gathered = lax.all_gather(flipped, 'y')  23 us
    all_gather x1, waiting for transfers between devices, on_device(): out_rows = lax.all_gather(jnp.pad(w_out, ((0, 16), (0, 0))), 'z')  17.3 us
    all_gather x1, blocking collectives, on_device(): attended_all = lax.all_gather(attended, TP, axis=1, tiled=True)  17.3 us
    all_to_all x1, blocking collectives, on_device(): query = jnp.sum(lax.all_to_all(partial, 'x', 0, 0), axis=0)  16.2 us
    all_to_all x1, starting transfers between devices, on_device(): lax.all_to_all(jnp.broadcast_to(w_query, (z_size, depth, cols)), 'z', 0, 0)  15.7 us
    all_to_all x1, waiting for transfers between devices, on_device(): attended = lax.all_to_all(attended, 'z', 0, 0).reshape(token_count, -1)  11.7 us
  transfers between devices with their start and end apart: 6, of which 2 were waited for; matrix products, arithmetic and copies ran while one was open for 5% of the time, Pallas kernels for 0%

profile of v5, /device:TPU:1, one launch (start us, length us, event | category | flops | bytes accessed | tf_op | source)
XLA Modules:
  0.0 238.2 jit_solution(10971722927339098397)
XLA Ops:
  7.2 1.9 broadcast_in_dim.12
  9.1 15.7 %all-to-all-start.1 = ((bf16[16,80,384]{2,1,0:T(8,128)(2,1)}), bf16[16,80,384]{2,1,0:T(8,128)(2,1)S(1)}, u32[]{:S(2)}, u32[]{:S(2)}) async-start(bf16[16,80,384]{2,1,0:T(8,128)(2,1)} %broadcast_in_dim.12), calls=%async_computation.1 | async-start | bytes 1966080 | tf_op jit(solution)/shard_map/all_to_all | solution.py:44
  24.8 0.0 all-gather.9.cloned.1.call-start
  24.9 1.5 pad.23
  26.4 1.1 reduce_sum.63
  27.5 1.1 fusion.5
  28.6 3.1 %psum.42 = f32[2,128]{1,0:T(2,128)S(1)} all-reduce(f32[2,128]{1,0:T(2,128)S(1)} %pad_maximum_fusion.2), channel_id=1, replica_groups=mesh['x'=4,'z'=16,'y'=4,'core'=2] {'core'}, use_global_device_ids=true, to_apply=%region_2.3 | all-reduce | flops 256 | bytes 2048 | tf_op jit(solution)/shard_map/psum | solution.py:22
  31.7 9.3 %psum.43 = f32[2,128]{1,0:T(2,128)S(1)} all-reduce(f32[2,128]{1,0:T(2,128)S(1)} %psum.42), channel_id=1, replica_groups=mesh['x'=4,'z'=16,'y'=4,'core'=2] {'y'}, use_global_device_ids=true, to_apply=%region_3.4 | all-reduce | flops 256 | bytes 2048 | tf_op jit(solution)/shard_map/psum | solution.py:22
  41.0 1.1 fusion.8
  42.1 0.7 collective-permute-start
  42.8 23.0 %all-gather.1 = bf16[512,640]{1,0:T(8,128)(2,1)S(1)} all-gather(bf16[128,640]{1,0:T(8,128)(2,1)S(1)} %collective-permute-done), channel_id=3, replica_groups=mesh['x'=4,'z'=16,'y'=4,'core'=2] {'y'}, dimensions={0}, use_global_device_ids=true | all-gather | bytes 819200 | tf_op jit(solution)/shard_map/all_gather | solution.py:56
  65.8 0.1 fusion.17
  65.8 4.1 %all-gather.3 = bf16[4,128,640]{2,1,0:T(8,128)(2,1)S(1)} all-gather(bf16[2,128,640]{2,1,0:T(8,128)(2,1)S(1)} %bitcast.74), channel_id=5, replica_groups=mesh['x'=4,'z'=16,'y'=4,'core'=2] {'core'}, dimensions={0}, use_global_device_ids=true | all-gather | bytes 983040 | tf_op jit(solution)/shard_map/all_gather | solution.py:58
  70.0 2.3 all-gather.2
  72.2 0.5 convolution_bitcast_fusion
  72.7 0.5 convolution_bitcast_fusion.1
  73.3 0.1 pad_maximum_fusion
  73.3 16.2 %all_to_all.25 = f32[4,128,384]{2,1,0:T(8,128)S(1)} all-to-all(f32[4,128,384]{2,1,0:T(8,128)S(1)} %pad_maximum_fusion), channel_id=1, replica_groups=mesh['x'=4,'z'=16,'y'=4,'core'=2] {'x'}, dimensions={0} | all-to-all | bytes 1572864 | tf_op jit(solution)/shard_map/all_to_all | solution.py:65
  89.5 17.3 %all-gather.9.cloned.1.call-done = bf16[1024,640]{1,0:T(8,128)(2,1)} async-done(((bf16[64,640]{1,0:T(8,128)(2,1)}), bf16[1024,640]{1,0:T(8,128)(2,1)}) %all-gather.9.cloned.1.call-update) | async-done | bytes 1310736 | tf_op jit(solution)/shard_map/all_gather | solution.py:47
  106.9 2.2 slice.60
  109.2 0.2 copy.24
  109.4 0.2 copy.21
  109.6 0.1 multiply_reduce_fusion.1
  109.7 9.6 %psum.44 = f32[128]{0:T(128)S(1)} all-reduce(f32[128]{0:T(128)S(1)} %multiply_reduce_fusion.1), channel_id=1, replica_groups=mesh['x'=4,'z'=16,'y'=4,'core'=2] {'core'}, use_global_device_ids=true, to_apply=%region_6.7 | all-reduce | flops 128 | bytes 1024 | tf_op jit(solution)/shard_map/psum | solution.py:22
  119.3 8.1 %psum.45 = f32[128]{0:T(128)S(1)} all-reduce(f32[128]{0:T(128)S(1)} %psum.44), channel_id=1, replica_groups=mesh['x'=4,'z'=16,'y'=4,'core'=2] {'y'}, use_global_device_ids=true, to_apply=%region_7.8 | all-reduce | flops 128 | bytes 1024 | tf_op jit(solution)/shard_map/psum | solution.py:22
  127.4 0.1 multiply_convert_fusion
  127.5 0.1 copy.20
  127.6 0.5 fusion.18
  128.1 0.3 convolution_multiply_fusion
  128.4 0.8 fusion.4
  129.3 0.1 copy.26
  129.4 0.7 convert_element_type.43
  130.1 6.9 %all-to-all-start.3 = ((bf16[16,8,384]{2,1,0:T(8,128)(2,1)}), bf16[16,8,384]{2,1,0:T(8,128)(2,1)S(1)}, u32[]{:S(2)}, u32[]{:S(2)}) async-start(bf16[16,8,384]{2,1,0:T(8,128)(2,1)} %convert_element_type.43), calls=%async_computation.3 | async-start | bytes 196608 | tf_op jit(solution)/shard_map/all_to_all | solution.py:87
  137.1 0.1 slice.55
  137.1 0.1 divide_subtract_fusion
  137.2 0.1 dynamic_slice.3
  137.3 11.7 %all-to-all-done.3 = bf16[16,8,384]{2,1,0:T(8,128)(2,1)S(1)} async-done(((bf16[16,8,384]{2,1,0:T(8,128)(2,1)}), bf16[16,8,384]{2,1,0:T(8,128)(2,1)S(1)}, u32[]{:S(2)}, u32[]{:S(2)}) %all-to-all-start.3) | async-done | bytes 98336 | tf_op jit(solution)/shard_map/all_to_all | solution.py:87
  149.0 3.5 %all-to-all-start = ((f32[16,8,640]{2,1,0:T(8,128)}), f32[16,8,640]{2,1,0:T(8,128)S(1)}, u32[]{:S(2)}, u32[]{:S(2)}) async-start(f32[16,8,640]{2,1,0:T(8,128)} %bitcast), calls=%async_computation | async-start | bytes 655360 | tf_op jit(solution)/shard_map/all_to_all | solution.py:41
  152.5 17.3 %all_gather.42 = bf16[128,3072]{1,0:T(8,128)(2,1)S(1)} all-gather(bf16[128,384]{1,0:T(8,128)(2,1)S(1)} %bitcast.77), channel_id=1, replica_groups=mesh['x'=4,'z'=16,'y'=4,'core'=2] {'y','core'}, dimensions={1}, use_global_device_ids=true | all-gather | bytes 884736 | tf_op jit(solution)/shard_map/all_gather | solution.py:88
  169.9 2.9 %fusion.3 = f32[16,8,640]{2,1,0:T(8,128)S(1)} fusion(bf16[128,3072]{1,0:T(8,128)(2,1)S(1)} %all_gather.42, bf16[3072,640]{1,0:T(8,128)(2,1)} %all-gather.7.cloned.1.call-done, f32[16]{0:T(128)S(1)} %dynamic_slice.3), kind=kOutput, calls=%fused_computation.7 | convolution fusion | flops 503398400 | bytes 5046336 | tf_op jit(solution)/shard_map/dot_general | solution.py:89
  173.1 9.8 %all_gather.44 = f32[4,8,640]{2,1,0:T(8,128)S(1)} all-gather(f32[1,8,640]{2,1,0:T(8,128)S(1)} %slice_add_fusion), channel_id=1, replica_groups=mesh['x'=4,'z'=16,'y'=4,'core'=2] {'x'}, dimensions={0}, use_global_device_ids=true | all-gather | bytes 102400 | tf_op jit(solution)/shard_map/all_gather | solution.py:103
  182.9 0.2 broadcast_add_fusion
  183.2 0.1 broadcast_in_dim.13
  183.3 26.5 %all_to_all.26 = f32[16,8,768]{2,1,0:T(8,128)S(1)} all-to-all(f32[16,8,768]{2,1,0:T(8,128)S(1)} %pad_maximum_fusion.1), channel_id=1, replica_groups=mesh['x'=4,'z'=16,'y'=4,'core'=2] {'z'}, dimensions={0} | all-to-all | bytes 786432 | tf_op jit(solution)/shard_map/all_to_all | solution.py:110
  209.8 0.6 slice_reduce_fusion
  210.4 11.7 %psum.46 = f32[]{:T(128)} all-reduce(f32[]{:T(128)} %slice_reduce_fusion), channel_id=1, replica_groups=mesh['x'=4,'z'=16,'y'=4,'core'=2] {'core'}, use_global_device_ids=true, to_apply=%region_12.13 | all-reduce | flops 1 | bytes 8 | tf_op jit(solution)/shard_map/psum | solution.py:22
  222.1 6.7 %psum.47 = f32[]{:T(128)} all-reduce(f32[]{:T(128)} %psum.46), channel_id=1, replica_groups=mesh['x'=4,'z'=16,'y'=4,'core'=2] {'y'}, use_global_device_ids=true, to_apply=%region_13.14 | all-reduce | flops 1 | bytes 8 | tf_op jit(solution)/shard_map/psum | solution.py:22
  229.5 0.7 slice_bitcast_fusion
  (33 shorter events, 0.5 us)
Async XLA Ops:
  9.1 63.2 %all-to-all-start.1 = ((bf16[16,80,384]{2,1,0:T(8,128)(2,1)}), bf16[16,80,384]{2,1,0:T(8,128)(2,1)S(1)}, u32[]{:S(2)}, u32[]{:S(2)}) async-start(bf16[16,80,384]{2,1,0:T(8,128)(2,1)} %broadcast_in_dim.12), calls=%async_computation.1 | async-start | bytes 1966080 | tf_op jit(solution)/shard_map/all_to_all | solution.py:44
  24.8 82.1 %all-gather.9.cloned.1.call-start = ((), (), s32[]{:S(2)}) async-start(), calls=%async_computation.6 | async-start | bytes 1392640 | tf_op jit(solution)/shard_map/all_gather | solution.py:47
  26.4 143.5 %all-gather.7.cloned.1.call-start = ((), (), s32[]{:S(2)}) async-start(), calls=%async_computation.5 | async-start | bytes 4915200 | tf_op jit(solution)/shard_map/all_gather | solution.py:68
  42.1 0.7 collective-permute-start
  73.2 35.9 %copy-start = (bf16[512,384]{1,0:T(8,128)(2,1)S(1)}, bf16[512,384]{1,0:T(8,128)(2,1)}, u32[]{:S(2)}) copy-start(bf16[512,384]{1,0:T(8,128)(2,1)} %param.11) | copy-start | bytes 1179652
  73.2 36.1 %copy-start.1 = (bf16[512,384]{1,0:T(8,128)(2,1)S(1)}, bf16[512,384]{1,0:T(8,128)(2,1)}, u32[]{:S(2)}) copy-start(bf16[512,384]{1,0:T(8,128)(2,1)} %param.10) | copy-start | bytes 1179652
  73.3 54.1 %copy-start.2 = (f32[384]{0:T(512)S(1)}, f32[384]{0:T(512)}, u32[]{:S(2)}) copy-start(f32[384]{0:T(512)} %param.13) | copy-start | bytes 4612
  109.6 27.5 %copy-start.3 = (s32[64]{0:T(128)S(1)}, s32[64]{0:T(128)}, u32[]{:S(2)}) copy-start(s32[64]{0:T(128)} %param.9) | copy-start | bytes 772
  130.1 18.9 %all-to-all-start.3 = ((bf16[16,8,384]{2,1,0:T(8,128)(2,1)}), bf16[16,8,384]{2,1,0:T(8,128)(2,1)S(1)}, u32[]{:S(2)}, u32[]{:S(2)}) async-start(bf16[16,8,384]{2,1,0:T(8,128)(2,1)} %convert_element_type.43), calls=%async_computation.3 | async-start | bytes 196608 | tf_op jit(solution)/shard_map/all_to_all | solution.py:87
  149.0 24.1 %all-to-all-start = ((f32[16,8,640]{2,1,0:T(8,128)}), f32[16,8,640]{2,1,0:T(8,128)S(1)}, u32[]{:S(2)}, u32[]{:S(2)}) async-start(f32[16,8,640]{2,1,0:T(8,128)} %bitcast), calls=%async_computation | async-start | bytes 655360 | tf_op jit(solution)/shard_map/all_to_all | solution.py:41
Sparse Core Ops, SparseCore 0:
  28.3 78.5 all-gather.8
  109.3 56.7 all-gather.6

commit v6 on v5

--- a/solution.py
+++ b/solution.py
@@ -28,6 +28,16 @@
     return lax.ppermute(value, ("x", "y"), pairs)
 
 
+def gather_by_permutes(value, axis):
+    size, mine = lax.axis_size(axis), lax.axis_index(axis)
+    whole = jnp.broadcast_to(value, (size, *value.shape))
+    for shift in range(1, size):
+        pairs = [(at, (at + shift) % size) for at in range(size)]
+        got = lax.ppermute(value, axis, pairs)
+        whole = lax.dynamic_update_index_in_dim(whole, got, (mine - shift) % size, 0)
+    return whole
+
+
 def on_device(trajectory, timesteps, context_keys, context_values, ln_gain, q_gain, w_query, w_out):
     latent = trajectory[0]
     token_count, block = latent.shape
@@ -40,22 +50,24 @@
 
     rows_here = lax.all_to_all(latent.reshape(z_size, slice_tokens, block), "z", 0, 0)
 
+    moved, moved_gain = transpose_plane(latent), transpose_plane(ln_gain)
+
+    out_rows = gather_by_permutes(w_out, "x")
+
     depth, cols = w_query.shape
     query_rows = lax.all_to_all(jnp.broadcast_to(w_query, (z_size, depth, cols)), "z", 0, 0)
 
-    out_depth = w_out.shape[0]
-    out_rows = lax.all_gather(jnp.pad(w_out, ((0, 16), (0, 0))), "z")
-
-    sums = jnp.stack([jnp.sum(latent, axis=-1), jnp.sum(latent * latent, axis=-1)])
-    sums = tp_sum(sums) / full_width
+    sums = jnp.stack([jnp.sum(moved, axis=-1), jnp.sum(moved * moved, axis=-1)])
+    sums = lax.psum(lax.psum(sums, "core"), "x") / full_width
     row_mean, row_square = sums[0][:, None], sums[1][:, None]
     row_var = row_square - row_mean * row_mean
-    normed = ((latent - row_mean) * lax.rsqrt(row_var + epsilon) * ln_gain).astype(jnp.bfloat16)
+    normed = ((moved - row_mean) * lax.rsqrt(row_var + epsilon) * moved_gain).astype(jnp.bfloat16)
 
-    flipped = transpose_plane(normed)
-    gathered = lax.all_gather(flipped, "y")
+    gathered = lax.all_gather(normed, "y")
     half = x_size // 2
     parts = [lax.all_gather(gathered[at * half : (at + 1) * half], "core") for at in range(2)]
+    out_rows, query_rows, parts = lax.optimization_barrier((out_rows, query_rows, parts))
+    out_rows = lax.all_gather(out_rows, "z", axis=1).reshape(-1, block)
     query_weights = query_rows.reshape(2, block, cols)
     partial = [
         jnp.einsum("cxtk,ckn->xtn", part, query_weights, preferred_element_type=jnp.float32)
@@ -63,10 +75,6 @@
     ]
     partial = jnp.concatenate(partial)
     query = jnp.sum(lax.all_to_all(partial, "x", 0, 0), axis=0)
-    out_rows, query = lax.optimization_barrier((out_rows, query))
-    out_rows = out_rows[:, :out_depth].reshape(-1, block)
-    out_rows = lax.all_gather(out_rows, "x", axis=0, tiled=True)
-
     query_width = query.shape[1] * lax.axis_size(TP)
     square_sum = tp_sum(jnp.sum(query * query, axis=-1))
     query_scale = lax.rsqrt(square_sum / query_width + epsilon)[:, None]
@@ -104,12 +112,9 @@
     for at in range(x_size - 1):
         start = start + jnp.where(at < x_here, totals[at], 0.0)
     change = start + jnp.pad(running[:-1], ((1, 0), (0, 0), (0, 0))) - rows_here
-    change_sum = jnp.sum(change * change, axis=(1, 2), keepdims=True)
-    change_sum = jnp.broadcast_to(change_sum, (z_size, slice_tokens, HD))
-    sent = jnp.concatenate([start + running, change_sum], axis=2)
-    got = lax.all_to_all(sent, "z", 0, 0)
-    new_rows = got[:, :, :block].reshape(token_count, block)
-    change_sum = tp_sum(jnp.sum(got[:, 0, block]))
+    change_sum = tp_sum(lax.psum(jnp.sum(change * change, axis=(1, 2)), "z"))
+    change_sum = change_sum[lax.axis_index("z")]
+    new_rows = lax.all_to_all(start + running, "z", 0, 0).reshape(token_count, block)
     error_value = change_sum / (token_count * full_width)
     return (new_rows[None], error_value.reshape(1))
 

time: 240 us -> 260 us (1.083)
  starting transfers between devices: 27 us -> 56.8 us
  blocking collectives: 148 us -> 141 us
    psum x0 -> x3, blocking collectives: none -> 58.7 us  [the longest x1 30.2 us: on_device(): change_sum = tp_sum(lax.psum(jnp.sum(change * change, axis=(1, 2)), 'z'))]
    all_to_all x2 -> x0, blocking collectives: 42.7 us -> none  [the longest x1 26.5 us: on_device(): got = lax.all_to_all(sent, 'z', 0, 0)]
    all_to_all x0 -> x2, waiting for transfers between devices: none -> 11.6 us  [the longest x1 11.6 us: on_device(): query = jnp.sum(lax.all_to_all(partial, 'x', 0, 0), axis=0)]
    all_to_all x0 -> x2, starting transfers between devices: none -> 11.4 us  [the longest x1 7.92 us: on_device(): lax.all_to_all(start + running, 'z', 0, 0).reshape(token_count, block)]
    psum x6 -> x4, blocking collectives: 48.5 us -> 37.4 us  [tp_sum(): return lax.psum(lax.psum(value, 'core'), 'y')]
    all_gather x1, blocking collectives: 23 us -> 11.9 us  [on_device(): gathered = lax.all_gather(normed, 'y')]
    ppermute x0 -> x3, starting transfers between devices: none -> 10.5 us  [gather_by_permutes(): got = lax.ppermute(value, axis, pairs)]
    all_gather x2 -> x1, waiting for transfers between devices: 17.3 us -> 6.86 us  [on_device(): out_rows = lax.all_gather(out_rows, 'z', axis=1).reshape(-1, block)]
  transfers between devices with their start and end apart: 6 -> 11, of which waited for: 2 -> 3; matrix products, arithmetic and copies ran while one was open for 5% -> 4% of each run, Pallas kernels for 0% -> 0%
where the time goes in v6:
time: 260 us; the launch traced here: 259 us
  blocking collectives  141 us (54%)
  starting transfers between devices  56.8 us (22%)
  waiting for transfers between devices  30.5 us (12%)
  between operations  16.2 us (6%)
  local copies, waits for them, and re-layouts  5.72 us (2%)
  matrix products  5.7 us (2%)
    psum x4, blocking collectives, tp_sum(): return lax.psum(lax.psum(value, 'core'), 'y')  37.4 us
    psum x1, blocking collectives, on_device(): change_sum = tp_sum(lax.psum(jnp.sum(change * change, axis=(1, 2)), 'z'))  30.2 us
    psum x2, blocking collectives, on_device(): sums = lax.psum(lax.psum(sums, 'core'), 'x') / full_width  28.5 us
    all_gather x1, blocking collectives, on_device(): attended_all = lax.all_gather(attended, TP, axis=1, tiled=True)  16.3 us
    all_to_all x1, starting transfers between devices, on_device(): lax.all_to_all(jnp.broadcast_to(w_query, (z_size, depth, cols)), 'z', 0, 0)  15.7 us
    all_to_all x1, waiting for transfers between devices, on_device(): attended = lax.all_to_all(attended, 'z', 0, 0).reshape(token_count, -1)  12 us
    all_gather x1, blocking collectives, on_device(): gathered = lax.all_gather(normed, 'y')  11.9 us
    all_to_all x1, waiting for transfers between devices, on_device(): query = jnp.sum(lax.all_to_all(partial, 'x', 0, 0), axis=0)  11.6 us
  transfers between devices with their start and end apart: 11, of which 3 were waited for; matrix products, arithmetic and copies ran while one was open for 4% of the time, Pallas kernels for 0%

profile of v6, /device:TPU:1, one launch (start us, length us, event | category | flops | bytes accessed | tf_op | source)
XLA Modules:
  0.0 258.5 jit_solution(7894434997664177252)
XLA Ops:
  7.2 1.9 broadcast_in_dim.36
  9.0 15.7 %all-to-all-start.1 = ((bf16[16,80,384]{2,1,0:T(8,128)(2,1)}), bf16[16,80,384]{2,1,0:T(8,128)(2,1)S(1)}, u32[]{:S(2)}, u32[]{:S(2)}) async-start(bf16[16,80,384]{2,1,0:T(8,128)(2,1)} %broadcast_in_dim.36), calls=%async_computation.1 | async-start | bytes 1966080 | tf_op jit(solution)/shard_map/all_to_all | solution.py:58
  24.8 3.1 %collective-permute-start = (bf16[48,640]{1,0:T(8,128)(2,1)}, bf16[48,640]{1,0:T(8,128)(2,1)S(1)}, u32[]{:S(2)}, u32[]{:S(2)}) collective-permute-start(bf16[48,640]{1,0:T(8,128)(2,1)} %param.15), channel_id=1, source_target_pairs={{0,128},{128,256},{256,384},{384,0},{1,129},{129,257},{257,385},{3... | collective-permute-start | bytes 184328 | tf_op jit(solution)/shard_map/ppermute | solution.py:36
  28.0 4.4 %collective-permute-start.1 = (bf16[48,640]{1,0:T(8,128)(2,1)}, bf16[48,640]{1,0:T(8,128)(2,1)S(1)}, u32[]{:S(2)}, u32[]{:S(2)}) collective-permute-start(bf16[48,640]{1,0:T(8,128)(2,1)} %param.15), channel_id=1, source_target_pairs={{0,256},{128,384},{256,0},{384,128},{1,257},{129,385},{257,1},{385... | collective-permute-start | bytes 184328 | tf_op jit(solution)/shard_map/ppermute | solution.py:36
  32.3 3.1 %collective-permute-start.2 = (bf16[48,640]{1,0:T(8,128)(2,1)}, bf16[48,640]{1,0:T(8,128)(2,1)S(1)}, u32[]{:S(2)}, u32[]{:S(2)}) collective-permute-start(bf16[48,640]{1,0:T(8,128)(2,1)} %param.15), channel_id=1, source_target_pairs={{0,384},{128,0},{256,128},{384,256},{1,385},{129,1},{257,129},{385... | collective-permute-start | bytes 184328 | tf_op jit(solution)/shard_map/ppermute | solution.py:36
  35.4 1.6 collective-permute-start.3
  37.0 1.3 collective-permute-start.4
  38.4 0.8 broadcast_in_dim.32
  39.3 0.1 fusion.15
  39.5 3.9 %psum.49 = f32[2,128]{1,0:T(2,128)S(1)} all-reduce(f32[2,128]{1,0:T(2,128)S(1)} %pad_maximum_fusion.1), channel_id=1, replica_groups=mesh['x'=4,'z'=16,'y'=4,'core'=2] {'core'}, use_global_device_ids=true, to_apply=%region_2.3 | all-reduce | flops 256 | bytes 2048 | tf_op jit(solution)/shard_map/psum | solution.py:61
  43.4 24.5 %psum.50 = f32[2,128]{1,0:T(2,128)S(1)} all-reduce(f32[2,128]{1,0:T(2,128)S(1)} %psum.49), channel_id=1, replica_groups=mesh['x'=4,'z'=16,'y'=4,'core'=2] {'x'}, use_global_device_ids=true, to_apply=%region_3.4 | all-reduce | flops 256 | bytes 2048 | tf_op jit(solution)/shard_map/psum | solution.py:61
  68.0 0.1 multiply_convert_fusion
  68.1 11.9 %all-gather = bf16[512,640]{1,0:T(8,128)(2,1)S(1)} all-gather(bf16[128,640]{1,0:T(8,128)(2,1)S(1)} %multiply_convert_fusion), channel_id=2, replica_groups=mesh['x'=4,'z'=16,'y'=4,'core'=2] {'y'}, dimensions={0}, use_global_device_ids=true | all-gather | bytes 819200 | tf_op jit(solution)/shard_map/all_gather | solution.py:66
  80.1 5.6 %all-gather.1 = bf16[4,128,640]{2,1,0:T(8,128)(2,1)S(1)} all-gather(bf16[2,128,640]{2,1,0:T(8,128)(2,1)S(1)} %bitcast.67), channel_id=3, replica_groups=mesh['x'=4,'z'=16,'y'=4,'core'=2] {'core'}, dimensions={0}, use_global_device_ids=true | all-gather | bytes 983040 | tf_op jit(solution)/shard_map/all_gather | solution.py:68
  85.7 2.3 all-gather.2
  88.0 0.5 convolution_bitcast_fusion.1
  88.5 0.5 convolution_bitcast_fusion
  89.0 0.9 pad_maximum_fusion
  89.9 3.5 %all-to-all-start.2 = ((f32[4,128,384]{2,1,0:T(8,128)}), f32[4,128,384]{2,1,0:T(8,128)S(1)}, u32[]{:S(2)}, u32[]{:S(2)}) async-start(f32[4,128,384]{2,1,0:T(8,128)} %pad_maximum_fusion), calls=%async_computation.2 | async-start | bytes 1572864 | tf_op jit(solution)/shard_map/all_to_all | solution.py:77
  93.4 0.2 copy.21
  93.6 0.2 copy.24
  93.8 11.6 %all-to-all-done.2 = f32[4,128,384]{2,1,0:T(8,128)S(1)} async-done(((f32[4,128,384]{2,1,0:T(8,128)}), f32[4,128,384]{2,1,0:T(8,128)S(1)}, u32[]{:S(2)}, u32[]{:S(2)}) %all-to-all-start.2) | async-done | bytes 786464 | tf_op jit(solution)/shard_map/all_to_all | solution.py:77
  105.5 0.1 copy.20
  105.6 0.1 multiply_reduce_fusion.2
  105.7 3.3 %psum.51 = f32[128]{0:T(128)S(1)} all-reduce(f32[128]{0:T(128)S(1)} %multiply_reduce_fusion.2), channel_id=1, replica_groups=mesh['x'=4,'z'=16,'y'=4,'core'=2] {'core'}, use_global_device_ids=true, to_apply=%region_6.7 | all-reduce | flops 128 | bytes 1024 | tf_op jit(solution)/shard_map/psum | solution.py:22
  109.1 8.0 %psum.52 = f32[128]{0:T(128)S(1)} all-reduce(f32[128]{0:T(128)S(1)} %psum.51), channel_id=1, replica_groups=mesh['x'=4,'z'=16,'y'=4,'core'=2] {'y'}, use_global_device_ids=true, to_apply=%region_7.8 | all-reduce | flops 128 | bytes 1024 | tf_op jit(solution)/shard_map/psum | solution.py:22
  117.1 0.6 fusion.17
  117.7 0.4 convolution_multiply_fusion
  118.1 0.8 fusion.3
  118.9 0.1 copy.26
  119.0 0.7 convert_element_type.42
  119.7 11.2 %all-to-all-start.3 = ((bf16[16,8,384]{2,1,0:T(8,128)(2,1)}), bf16[16,8,384]{2,1,0:T(8,128)(2,1)S(1)}, u32[]{:S(2)}, u32[]{:S(2)}) async-start(bf16[16,8,384]{2,1,0:T(8,128)(2,1)} %convert_element_type.42), calls=%async_computation.3 | async-start | bytes 196608 | tf_op jit(solution)/shard_map/all_to_all | solution.py:95
  130.9 0.1 slice.46
  131.0 0.1 divide_subtract_fusion
  131.1 0.1 dynamic_slice.6
  131.2 12.0 %all-to-all-done.3 = bf16[16,8,384]{2,1,0:T(8,128)(2,1)S(1)} async-done(((bf16[16,8,384]{2,1,0:T(8,128)(2,1)}), bf16[16,8,384]{2,1,0:T(8,128)(2,1)S(1)}, u32[]{:S(2)}, u32[]{:S(2)}) %all-to-all-start.3) | async-done | bytes 98336 | tf_op jit(solution)/shard_map/all_to_all | solution.py:95
  143.2 4.9 %all-to-all-start = ((f32[16,8,640]{2,1,0:T(8,128)}), f32[16,8,640]{2,1,0:T(8,128)S(1)}, u32[]{:S(2)}, u32[]{:S(2)}) async-start(f32[16,8,640]{2,1,0:T(8,128)} %bitcast), calls=%async_computation | async-start | bytes 655360 | tf_op jit(solution)/shard_map/all_to_all | solution.py:51
  148.1 16.3 %all_gather.37 = bf16[128,3072]{1,0:T(8,128)(2,1)S(1)} all-gather(bf16[128,384]{1,0:T(8,128)(2,1)S(1)} %bitcast.71), channel_id=1, replica_groups=mesh['x'=4,'z'=16,'y'=4,'core'=2] {'y','core'}, dimensions={1}, use_global_device_ids=true | all-gather | bytes 884736 | tf_op jit(solution)/shard_map/all_gather | solution.py:96
  164.4 6.9 %all-gather.6.cloned.1.call-done = bf16[4,768,640]{2,1,0:T(8,128)(2,1)} async-done(((bf16[4,48,640]{2,1,0:T(8,128)(2,1)}), bf16[4,768,640]{2,1,0:T(8,128)(2,1)}) %all-gather.6.cloned.1.call-update) | async-done | bytes 3932176 | tf_op jit(solution)/shard_map/all_gather | solution.py:70
  171.2 2.9 %convolution_multiply_fusion.1 = f32[16,8,640]{2,1,0:T(8,128)S(1)} fusion(bf16[3072,640,1]{1,0,2:T(8,128)(2,1)} %bitcast.60, bf16[128,3072]{1,0:T(8,128)(2,1)S(1)} %all_gather.37, f32[16]{0:T(128)S(1)} %dynamic_slice.6), kind=kOutput, calls=%fused_computation.6 | convolution fusion | flops 503398400 | bytes 5046336 | tf_op jit(solution)/shard_map/dot_general | solution.py:97
  174.5 9.1 %all_gather.40 = f32[4,8,640]{2,1,0:T(8,128)S(1)} all-gather(f32[1,8,640]{2,1,0:T(8,128)S(1)} %slice_add_fusion), channel_id=1, replica_groups=mesh['x'=4,'z'=16,'y'=4,'core'=2] {'x'}, dimensions={0}, use_global_device_ids=true | all-gather | bytes 102400 | tf_op jit(solution)/shard_map/all_gather | solution.py:111
  183.6 0.9 multiply_reduce_fusion
  184.4 7.9 %all-to-all-start.4 = ((f32[16,8,640]{2,1,0:T(8,128)}), f32[16,8,640]{2,1,0:T(8,128)S(1)}, u32[]{:S(2)}, u32[]{:S(2)}) async-start(f32[16,8,640]{2,1,0:T(8,128)} %get-tuple-element.15), calls=%async_computation.4 | async-start | bytes 655360 | tf_op jit(solution)/shard_map/all_to_all | solution.py:117
  192.3 30.2 %psum.53 = f32[16]{0:T(128)S(1)} all-reduce(f32[16]{0:T(128)S(1)} %get-tuple-element.14), channel_id=1, replica_groups=mesh['x'=4,'z'=16,'y'=4,'core'=2] {'z'}, use_global_device_ids=true, to_apply=%region_11.12 | all-reduce | flops 16 | bytes 128 | tf_op jit(solution)/shard_map/psum | solution.py:115
  222.6 18.0 %psum.54 = f32[16]{0:T(128)S(1)} all-reduce(f32[16]{0:T(128)S(1)} %psum.53), channel_id=1, replica_groups=mesh['x'=4,'z'=16,'y'=4,'core'=2] {'core'}, use_global_device_ids=true, to_apply=%region_12.13 | all-reduce | flops 16 | bytes 128 | tf_op jit(solution)/shard_map/psum | solution.py:22
  240.5 8.1 %psum.55 = f32[16]{0:T(128)S(1)} all-reduce(f32[16]{0:T(128)S(1)} %psum.54), channel_id=1, replica_groups=mesh['x'=4,'z'=16,'y'=4,'core'=2] {'y'}, use_global_device_ids=true, to_apply=%region_13.14 | all-reduce | flops 16 | bytes 128 | tf_op jit(solution)/shard_map/psum | solution.py:22
  248.6 0.6 dynamic_slice.7
  249.8 0.7 copy.35
  (41 shorter events, 0.6 us)
Async XLA Ops:
  9.0 78.9 %all-to-all-start.1 = ((bf16[16,80,384]{2,1,0:T(8,128)(2,1)}), bf16[16,80,384]{2,1,0:T(8,128)(2,1)S(1)}, u32[]{:S(2)}, u32[]{:S(2)}) async-start(bf16[16,80,384]{2,1,0:T(8,128)(2,1)} %broadcast_in_dim.36), calls=%async_computation.1 | async-start | bytes 1966080 | tf_op jit(solution)/shard_map/all_to_all | solution.py:58
  24.8 146.5 %all-gather.6.cloned.1.call-start = ((), (), s32[]{:S(2)}) async-start(), calls=%async_computation.5 | async-start | bytes 4177920 | tf_op jit(solution)/shard_map/all_gather | solution.py:70
  24.8 13.5 %collective-permute-start = (bf16[48,640]{1,0:T(8,128)(2,1)}, bf16[48,640]{1,0:T(8,128)(2,1)S(1)}, u32[]{:S(2)}, u32[]{:S(2)}) collective-permute-start(bf16[48,640]{1,0:T(8,128)(2,1)} %param.15), channel_id=1, source_target_pairs={{0,128},{128,256},{256,384},{384,0},{1,129},{129,257},{257,385},{3... | collective-permute-start | bytes 184328 | tf_op jit(solution)/shard_map/ppermute | solution.py:36
  28.0 11.3 %collective-permute-start.1 = (bf16[48,640]{1,0:T(8,128)(2,1)}, bf16[48,640]{1,0:T(8,128)(2,1)S(1)}, u32[]{:S(2)}, u32[]{:S(2)}) collective-permute-start(bf16[48,640]{1,0:T(8,128)(2,1)} %param.15), channel_id=1, source_target_pairs={{0,256},{128,384},{256,0},{384,128},{1,257},{129,385},{257,1},{385... | collective-permute-start | bytes 184328 | tf_op jit(solution)/shard_map/ppermute | solution.py:36
  32.3 7.0 %collective-permute-start.2 = (bf16[48,640]{1,0:T(8,128)(2,1)}, bf16[48,640]{1,0:T(8,128)(2,1)S(1)}, u32[]{:S(2)}, u32[]{:S(2)}) collective-permute-start(bf16[48,640]{1,0:T(8,128)(2,1)} %param.15), channel_id=1, source_target_pairs={{0,384},{128,0},{256,128},{384,256},{1,385},{129,1},{257,129},{385... | collective-permute-start | bytes 184328 | tf_op jit(solution)/shard_map/ppermute | solution.py:36
  35.4 3.9 %collective-permute-start.3 = (f32[128,640]{1,0:T(8,128)}, f32[128,640]{1,0:T(8,128)S(1)}, u32[]{:S(2)}, u32[]{:S(2)}) collective-permute-start(f32[128,640]{1,0:T(8,128)} %bitcast.4), channel_id=1, source_target_pairs={{0,0},{2,128},{4,256},{6,384},{128,2},{130,130},{132,258},{134,386... | collective-permute-start | bytes 983048 | tf_op jit(solution)/shard_map/ppermute | solution.py:28
  37.0 30.9 %collective-permute-start.4 = (f32[640]{0:T(1024)}, f32[640]{0:T(1024)S(1)}, u32[]{:S(2)}, u32[]{:S(2)}) collective-permute-start(f32[640]{0:T(1024)} %param.12), channel_id=1, source_target_pairs={{0,0},{2,128},{4,256},{6,384},{128,2},{130,130},{132,258},{134,386... | collective-permute-start | bytes 7688 | tf_op jit(solution)/shard_map/ppermute | solution.py:28
  39.3 48.6 %copy-start = (bf16[4,48,640]{2,1,0:T(8,128)(2,1)}, bf16[4,48,640]{2,1,0:T(8,128)(2,1)S(1)}, u32[]{:S(2)}) copy-start(bf16[4,48,640]{2,1,0:T(8,128)(2,1)S(1)} %bitcast_dynamic-update-slice_fusion) | copy-start | bytes 737284
  87.9 5.5 %copy-start.1 = (bf16[512,384]{1,0:T(8,128)(2,1)S(1)}, bf16[512,384]{1,0:T(8,128)(2,1)}, u32[]{:S(2)}) copy-start(bf16[512,384]{1,0:T(8,128)(2,1)} %param.10) | copy-start | bytes 1179652
  88.0 5.7 %copy-start.2 = (bf16[512,384]{1,0:T(8,128)(2,1)S(1)}, bf16[512,384]{1,0:T(8,128)(2,1)}, u32[]{:S(2)}) copy-start(bf16[512,384]{1,0:T(8,128)(2,1)} %param.11) | copy-start | bytes 1179652
  88.5 28.6 %copy-start.3 = (f32[384]{0:T(512)S(1)}, f32[384]{0:T(512)}, u32[]{:S(2)}) copy-start(f32[384]{0:T(512)} %param.13) | copy-start | bytes 4612
  89.9 15.5 %all-to-all-start.2 = ((f32[4,128,384]{2,1,0:T(8,128)}), f32[4,128,384]{2,1,0:T(8,128)S(1)}, u32[]{:S(2)}, u32[]{:S(2)}) async-start(f32[4,128,384]{2,1,0:T(8,128)} %pad_maximum_fusion), calls=%async_computation.2 | async-start | bytes 1572864 | tf_op jit(solution)/shard_map/all_to_all | solution.py:77
  105.5 25.5 %copy-start.4 = (s32[64]{0:T(128)S(1)}, s32[64]{0:T(128)}, u32[]{:S(2)}) copy-start(s32[64]{0:T(128)} %param.9) | copy-start | bytes 772
  119.7 23.5 %all-to-all-start.3 = ((bf16[16,8,384]{2,1,0:T(8,128)(2,1)}), bf16[16,8,384]{2,1,0:T(8,128)(2,1)S(1)}, u32[]{:S(2)}, u32[]{:S(2)}) async-start(bf16[16,8,384]{2,1,0:T(8,128)(2,1)} %convert_element_type.42), calls=%async_computation.3 | async-start | bytes 196608 | tf_op jit(solution)/shard_map/all_to_all | solution.py:95
  143.2 31.3 %all-to-all-start = ((f32[16,8,640]{2,1,0:T(8,128)}), f32[16,8,640]{2,1,0:T(8,128)S(1)}, u32[]{:S(2)}, u32[]{:S(2)}) async-start(f32[16,8,640]{2,1,0:T(8,128)} %bitcast), calls=%async_computation | async-start | bytes 655360 | tf_op jit(solution)/shard_map/all_to_all | solution.py:51
  184.4 65.4 %all-to-all-start.4 = ((f32[16,8,640]{2,1,0:T(8,128)}), f32[16,8,640]{2,1,0:T(8,128)S(1)}, u32[]{:S(2)}, u32[]{:S(2)}) async-start(f32[16,8,640]{2,1,0:T(8,128)} %get-tuple-element.15), calls=%async_computation.4 | async-start | bytes 655360 | tf_op jit(solution)/shard_map/all_to_all | solution.py:117
Sparse Core Ops, SparseCore 0:
  88.1 83.1 all-gather.5

commit v7 on v5

--- a/solution.py
+++ b/solution.py
@@ -40,11 +40,7 @@
 
     rows_here = lax.all_to_all(latent.reshape(z_size, slice_tokens, block), "z", 0, 0)
 
-    depth, cols = w_query.shape
-    query_rows = lax.all_to_all(jnp.broadcast_to(w_query, (z_size, depth, cols)), "z", 0, 0)
-
-    out_depth = w_out.shape[0]
-    out_rows = lax.all_gather(jnp.pad(w_out, ((0, 16), (0, 0))), "z")
+    out_rows = lax.all_to_all(jnp.broadcast_to(w_out, (x_size, *w_out.shape)), "x", 0, 0)
 
     sums = jnp.stack([jnp.sum(latent, axis=-1), jnp.sum(latent * latent, axis=-1)])
     sums = tp_sum(sums) / full_width
@@ -52,21 +48,21 @@
     row_var = row_square - row_mean * row_mean
     normed = ((latent - row_mean) * lax.rsqrt(row_var + epsilon) * ln_gain).astype(jnp.bfloat16)
 
+    w_query, normed = lax.optimization_barrier((w_query, normed))
+    query_rows = lax.all_gather(w_query, "z")
     flipped = transpose_plane(normed)
+    out_rows, query_rows, flipped = lax.optimization_barrier((out_rows, query_rows, flipped))
+    out_rows = lax.all_gather(out_rows, "z", axis=1).reshape(-1, block)
     gathered = lax.all_gather(flipped, "y")
     half = x_size // 2
     parts = [lax.all_gather(gathered[at * half : (at + 1) * half], "core") for at in range(2)]
-    query_weights = query_rows.reshape(2, block, cols)
+    query_weights = query_rows.reshape(2, block, w_query.shape[1])
     partial = [
         jnp.einsum("cxtk,ckn->xtn", part, query_weights, preferred_element_type=jnp.float32)
         for part in parts
     ]
     partial = jnp.concatenate(partial)
     query = jnp.sum(lax.all_to_all(partial, "x", 0, 0), axis=0)
-    out_rows, query = lax.optimization_barrier((out_rows, query))
-    out_rows = out_rows[:, :out_depth].reshape(-1, block)
-    out_rows = lax.all_gather(out_rows, "x", axis=0, tiled=True)
-
     query_width = query.shape[1] * lax.axis_size(TP)
     square_sum = tp_sum(jnp.sum(query * query, axis=-1))
     query_scale = lax.rsqrt(square_sum / query_width + epsilon)[:, None]
@@ -104,12 +100,11 @@
     for at in range(x_size - 1):
         start = start + jnp.where(at < x_here, totals[at], 0.0)
     change = start + jnp.pad(running[:-1], ((1, 0), (0, 0), (0, 0))) - rows_here
-    change_sum = jnp.sum(change * change, axis=(1, 2), keepdims=True)
-    change_sum = jnp.broadcast_to(change_sum, (z_size, slice_tokens, HD))
-    sent = jnp.concatenate([start + running, change_sum], axis=2)
-    got = lax.all_to_all(sent, "z", 0, 0)
-    new_rows = got[:, :, :block].reshape(token_count, block)
-    change_sum = tp_sum(jnp.sum(got[:, 0, block]))
+    change_sum = tp_sum(jnp.sum(change * change, axis=(1, 2)))
+    new_rows = lax.all_to_all(start + running, "z", 0, 0).reshape(token_count, block)
+    change_sum, new_rows = lax.optimization_barrier((change_sum, new_rows))
+    change_sum = jnp.broadcast_to(change_sum[:, None, None], (z_size, 1, HD))
+    change_sum = jnp.sum(lax.all_to_all(change_sum, "z", 0, 0)[:, 0, 0])
     error_value = change_sum / (token_count * full_width)
     return (new_rows[None], error_value.reshape(1))
 

time: 240 us -> 242 us (level)
  blocking collectives: 148 us -> 124 us
  starting transfers between devices: 27 us -> 47.6 us
  waiting for transfers between devices: 29.1 us -> 35.5 us
  local copies, waits for them, and re-layouts: 8.07 us -> 5.27 us
    all_to_all x2 -> x0, blocking collectives: 42.7 us -> none  [the longest x1 26.5 us: on_device(): got = lax.all_to_all(sent, 'z', 0, 0)]
    all_gather x0 -> x1, blocking collectives: none -> 32.8 us  [on_device(): query_rows = lax.all_gather(w_query, 'z')]
    all_to_all x1 -> x4, waiting for transfers between devices: 0.01 us -> 23.9 us  [the longest x1 11.3 us: on_device(): query = jnp.sum(lax.all_to_all(partial, 'x', 0, 0), axis=0)]
    all_to_all x1 -> x4, starting transfers between devices: 15.7 us -> 34.5 us  [the longest x1 12.3 us: on_device(): change_sum = jnp.sum(lax.all_to_all(change_sum, 'z', 0, 0)[:, 0, 0])]
    all_gather x2 -> x1, waiting for transfers between devices: 17.3 us -> 0.01 us  [on_device(): out_rows = lax.all_gather(out_rows, 'z', axis=1).reshape(-1, block)]
    all_gather x1, blocking collectives: 23 us -> 12.3 us  [on_device(): gathered = lax.all_gather(flipped, 'y')]
    psum x6, blocking collectives: 48.5 us -> 39 us  [tp_sum(): return lax.psum(lax.psum(value, 'core'), 'y')]
    all_gather x2, blocking collectives: 6.4 us -> 15.2 us  [on_device(): lax.all_gather(gathered[at * half:(at + 1) * half], 'core')]
  transfers between devices with their start and end apart: 6 -> 8, of which waited for: 2 -> 4; matrix products, arithmetic and copies ran while one was open for 5% -> 4% of each run, Pallas kernels for 0% -> 0%
where the time goes in v7:
time: 242 us; the launch traced here: 240 us
  blocking collectives  124 us (51%)
  starting transfers between devices  47.6 us (20%)
  waiting for transfers between devices  35.5 us (15%)
  between operations  16.1 us (7%)
  other arithmetic  6.11 us (3%)
  matrix products  5.71 us (2%)
  local copies, waits for them, and re-layouts  5.27 us (2%)
    psum x6, blocking collectives, tp_sum(): return lax.psum(lax.psum(value, 'core'), 'y')  39 us
    all_gather x1, blocking collectives, on_device(): query_rows = lax.all_gather(w_query, 'z')  32.8 us
    all_gather x1, blocking collectives, on_device(): attended_all = lax.all_gather(attended, TP, axis=1, tiled=True)  15.9 us
    all_gather x2, blocking collectives, on_device(): lax.all_gather(gathered[at * half:(at + 1) * half], 'core')  15.2 us
    all_to_all x1, starting transfers between devices, on_device(): change_sum = jnp.sum(lax.all_to_all(change_sum, 'z', 0, 0)[:, 0, 0])  12.3 us
    all_gather x1, blocking collectives, on_device(): gathered = lax.all_gather(flipped, 'y')  12.3 us
    all_to_all x1, waiting for transfers between devices, on_device(): attended = lax.all_to_all(attended, 'z', 0, 0).reshape(token_count, -1)  11.6 us
    all_to_all x1, starting transfers between devices, on_device(): lax.all_to_all(start + running, 'z', 0, 0).reshape(token_count, block)  11.5 us
  transfers between devices with their start and end apart: 8, of which 4 were waited for; matrix products, arithmetic and copies ran while one was open for 4% of the time, Pallas kernels for 0%

profile of v7, /device:TPU:1, one launch (start us, length us, event | category | flops | bytes accessed | tf_op | source)
XLA Modules:
  0.0 240.4 jit_solution(7551870684906679190)
XLA Ops:
  7.2 1.1 fusion.5
  8.2 1.1 reduce_sum.65
  9.4 9.0 %psum.42 = f32[2,128]{1,0:T(2,128)S(1)} all-reduce(f32[2,128]{1,0:T(2,128)S(1)} %pad_maximum_fusion.1), channel_id=1, replica_groups=mesh['x'=4,'z'=16,'y'=4,'core'=2] {'core'}, use_global_device_ids=true, to_apply=%region_2.0 | all-reduce | flops 256 | bytes 2048 | tf_op jit(solution)/shard_map/psum | solution.py:22
  18.4 6.1 %psum.43 = f32[2,128]{1,0:T(2,128)S(1)} all-reduce(f32[2,128]{1,0:T(2,128)S(1)} %psum.42), channel_id=1, replica_groups=mesh['x'=4,'z'=16,'y'=4,'core'=2] {'y'}, use_global_device_ids=true, to_apply=%region_3.0 | all-reduce | flops 256 | bytes 2048 | tf_op jit(solution)/shard_map/psum | solution.py:22
  24.4 1.1 fusion.8
  25.5 0.7 collective-permute-start
  26.2 1.5 broadcast_in_dim.14
  27.8 6.3 %all-to-all-start.1 = ((bf16[4,48,640]{2,1,0:T(8,128)(2,1)}), bf16[4,48,640]{2,1,0:T(8,128)(2,1)S(1)}, u32[]{:S(2)}, u32[]{:S(2)}) async-start(bf16[4,48,640]{2,1,0:T(8,128)(2,1)} %broadcast_in_dim.14), calls=%async_computation.1 | async-start | bytes 491520 | tf_op jit(solution)/shard_map/all_to_all | solution.py:43
  34.0 32.8 %all-gather = bf16[1280,384]{1,0:T(8,128)(2,1)S(1)} all-gather(bf16[80,384]{1,0:T(8,128)(2,1)} %param.14), channel_id=2, replica_groups=mesh['x'=4,'z'=16,'y'=4,'core'=2] {'z'}, dimensions={0}, use_global_device_ids=true | all-gather | bytes 1044480 | tf_op jit(solution)/shard_map/all_gather | solution.py:52
  66.8 0.7 copy-done
  67.5 12.3 %all-gather.1 = bf16[512,640]{1,0:T(8,128)(2,1)S(1)} all-gather(bf16[128,640]{1,0:T(8,128)(2,1)S(1)} %collective-permute-done), channel_id=3, replica_groups=mesh['x'=4,'z'=16,'y'=4,'core'=2] {'y'}, dimensions={0}, use_global_device_ids=true | all-gather | bytes 819200 | tf_op jit(solution)/shard_map/all_gather | solution.py:56
  79.9 12.9 %all-gather.2 = bf16[4,128,640]{2,1,0:T(8,128)(2,1)S(1)} all-gather(bf16[2,128,640]{2,1,0:T(8,128)(2,1)S(1)} %bitcast.74), channel_id=4, replica_groups=mesh['x'=4,'z'=16,'y'=4,'core'=2] {'core'}, dimensions={0}, use_global_device_ids=true | all-gather | bytes 983040 | tf_op jit(solution)/shard_map/all_gather | solution.py:58
  92.7 2.4 all-gather.3
  95.1 0.5 convolution_bitcast_fusion.1
  95.6 0.5 convolution_bitcast_fusion
  96.1 0.9 pad_maximum_fusion
  97.1 4.4 %all-to-all-start.2 = ((f32[4,128,384]{2,1,0:T(8,128)}), f32[4,128,384]{2,1,0:T(8,128)S(1)}, u32[]{:S(2)}, u32[]{:S(2)}) async-start(f32[4,128,384]{2,1,0:T(8,128)} %pad_maximum_fusion), calls=%async_computation.2 | async-start | bytes 1572864 | tf_op jit(solution)/shard_map/all_to_all | solution.py:65
  101.5 0.2 copy.35
  101.7 0.2 copy.38
  101.9 11.3 %all-to-all-done.2 = f32[4,128,384]{2,1,0:T(8,128)S(1)} async-done(((f32[4,128,384]{2,1,0:T(8,128)}), f32[4,128,384]{2,1,0:T(8,128)S(1)}, u32[]{:S(2)}, u32[]{:S(2)}) %all-to-all-start.2) | async-done | bytes 786464 | tf_op jit(solution)/shard_map/all_to_all | solution.py:65
  113.2 0.1 copy.34
  113.4 0.1 multiply_reduce_fusion.1
  113.5 3.7 %psum.44 = f32[128]{0:T(128)S(1)} all-reduce(f32[128]{0:T(128)S(1)} %multiply_reduce_fusion.1), channel_id=1, replica_groups=mesh['x'=4,'z'=16,'y'=4,'core'=2] {'core'}, use_global_device_ids=true, to_apply=%region_6.0 | all-reduce | flops 128 | bytes 1024 | tf_op jit(solution)/shard_map/psum | solution.py:22
  117.1 8.2 %psum.45 = f32[128]{0:T(128)S(1)} all-reduce(f32[128]{0:T(128)S(1)} %psum.44), channel_id=1, replica_groups=mesh['x'=4,'z'=16,'y'=4,'core'=2] {'y'}, use_global_device_ids=true, to_apply=%region_7.0 | all-reduce | flops 128 | bytes 1024 | tf_op jit(solution)/shard_map/psum | solution.py:22
  125.4 0.6 fusion.20
  125.9 0.4 convolution_multiply_fusion
  126.3 0.8 fusion.3
  127.2 0.1 copy.40
  127.3 0.7 convert_element_type.42
  128.0 7.1 %all-to-all-start.3 = ((bf16[16,8,384]{2,1,0:T(8,128)(2,1)}), bf16[16,8,384]{2,1,0:T(8,128)(2,1)S(1)}, u32[]{:S(2)}, u32[]{:S(2)}) async-start(bf16[16,8,384]{2,1,0:T(8,128)(2,1)} %convert_element_type.42), calls=%async_computation.3 | async-start | bytes 196608 | tf_op jit(solution)/shard_map/all_to_all | solution.py:83
  135.1 0.1 slice.49
  135.2 0.1 divide_subtract_fusion
  135.2 0.1 dynamic_slice.3
  135.3 11.6 %all-to-all-done.3 = bf16[16,8,384]{2,1,0:T(8,128)(2,1)S(1)} async-done(((bf16[16,8,384]{2,1,0:T(8,128)(2,1)}), bf16[16,8,384]{2,1,0:T(8,128)(2,1)S(1)}, u32[]{:S(2)}, u32[]{:S(2)}) %all-to-all-start.3) | async-done | bytes 98336 | tf_op jit(solution)/shard_map/all_to_all | solution.py:83
  146.9 5.3 %all-to-all-start = ((f32[16,8,640]{2,1,0:T(8,128)}), f32[16,8,640]{2,1,0:T(8,128)S(1)}, u32[]{:S(2)}, u32[]{:S(2)}) async-start(f32[16,8,640]{2,1,0:T(8,128)} %bitcast), calls=%async_computation | async-start | bytes 655360 | tf_op jit(solution)/shard_map/all_to_all | solution.py:41
  152.2 15.9 %all_gather.45 = bf16[128,3072]{1,0:T(8,128)(2,1)S(1)} all-gather(bf16[128,384]{1,0:T(8,128)(2,1)S(1)} %bitcast.78), channel_id=1, replica_groups=mesh['x'=4,'z'=16,'y'=4,'core'=2] {'y','core'}, dimensions={1}, use_global_device_ids=true | all-gather | bytes 884736 | tf_op jit(solution)/shard_map/all_gather | solution.py:84
  168.1 2.9 %convolution_multiply_fusion.1 = f32[16,8,640]{2,1,0:T(8,128)S(1)} fusion(bf16[3072,640,1]{1,0,2:T(8,128)(2,1)} %bitcast.67, bf16[128,3072]{1,0:T(8,128)(2,1)S(1)} %all_gather.45, f32[16]{0:T(128)S(1)} %dynamic_slice.3), kind=kOutput, calls=%fused_computation.6 | convolution fusion | flops 503398400 | bytes 5046336 | tf_op jit(solution)/shard_map/dot_general | solution.py:85
  171.3 9.0 %all_gather.48 = f32[4,8,640]{2,1,0:T(8,128)S(1)} all-gather(f32[1,8,640]{2,1,0:T(8,128)S(1)} %slice_add_fusion), channel_id=1, replica_groups=mesh['x'=4,'z'=16,'y'=4,'core'=2] {'x'}, dimensions={0}, use_global_device_ids=true | all-gather | bytes 102400 | tf_op jit(solution)/shard_map/all_gather | solution.py:99
  180.3 0.9 broadcast_add_fusion
  181.2 11.5 %all-to-all-start.4 = ((f32[16,8,640]{2,1,0:T(8,128)}), f32[16,8,640]{2,1,0:T(8,128)S(1)}, u32[]{:S(2)}, u32[]{:S(2)}) async-start(f32[16,8,640]{2,1,0:T(8,128)} %get-tuple-element.18), calls=%async_computation.4 | async-start | bytes 655360 | tf_op jit(solution)/shard_map/all_to_all | solution.py:104
  192.8 5.5 %psum.46 = f32[16]{0:T(128)S(1)} all-reduce(f32[16]{0:T(128)S(1)} %get-tuple-element.19), channel_id=1, replica_groups=mesh['x'=4,'z'=16,'y'=4,'core'=2] {'core'}, use_global_device_ids=true, to_apply=%region_11.12 | all-reduce | flops 16 | bytes 128 | tf_op jit(solution)/shard_map/psum | solution.py:22
  198.2 6.6 %psum.47 = f32[16]{0:T(128)S(1)} all-reduce(f32[16]{0:T(128)S(1)} %psum.46), channel_id=1, replica_groups=mesh['x'=4,'z'=16,'y'=4,'core'=2] {'y'}, use_global_device_ids=true, to_apply=%region_12.13 | all-reduce | flops 16 | bytes 128 | tf_op jit(solution)/shard_map/psum | solution.py:22
  204.8 1.4 all-to-all-done.4
  206.2 0.7 broadcast_in_dim.30
  206.9 12.3 %all-to-all-start.5 = ((f32[16,1,128]{2,1,0:T(1,128)}), f32[16,1,128]{2,1,0:T(1,128)S(1)}, u32[]{:S(2)}, u32[]{:S(2)}) async-start(f32[16,1,128]{2,1,0:T(1,128)} %broadcast_in_dim.30), calls=%async_computation.5 | async-start | bytes 16384 | tf_op jit(solution)/shard_map/all_to_all | solution.py:107
  219.3 11.2 %all-to-all-done.5 = f32[16,1,128]{2,1,0:T(1,128)S(1)} async-done(((f32[16,1,128]{2,1,0:T(1,128)}), f32[16,1,128]{2,1,0:T(1,128)S(1)}, u32[]{:S(2)}, u32[]{:S(2)}) %all-to-all-start.5) | async-done | bytes 8224 | tf_op jit(solution)/shard_map/all_to_all | solution.py:107
  230.5 0.6 slice_reduce_fusion
  231.7 0.7 copy.48
  (33 shorter events, 0.5 us)
Async XLA Ops:
  25.5 41.3 %collective-permute-start = (bf16[128,640]{1,0:T(8,128)(2,1)S(1)}, bf16[128,640]{1,0:T(8,128)(2,1)S(1)}, u32[]{:S(2)}, u32[]{:S(2)}) collective-permute-start(bf16[128,640]{1,0:T(8,128)(2,1)S(1)} %fusion.8), channel_id=1, source_target_pairs={{0,0},{2,128},{4,256},{6,384},{128,2},{130,130},{132,258},{134,386... | collective-permute-start | bytes 491528 | tf_op jit(solution)/shard_map/ppermute | solution.py:28
  27.8 39.0 %all-to-all-start.1 = ((bf16[4,48,640]{2,1,0:T(8,128)(2,1)}), bf16[4,48,640]{2,1,0:T(8,128)(2,1)S(1)}, u32[]{:S(2)}, u32[]{:S(2)}) async-start(bf16[4,48,640]{2,1,0:T(8,128)(2,1)} %broadcast_in_dim.14), calls=%async_computation.1 | async-start | bytes 491520 | tf_op jit(solution)/shard_map/all_to_all | solution.py:43
  34.0 134.0 %all-gather.7.cloned.1.call-start = ((), (), s32[]{:S(2)}) async-start(), calls=%async_computation.6 | async-start | bytes 4177920 | tf_op jit(solution)/shard_map/all_gather | solution.py:55
  66.8 0.7 copy-start
  92.7 8.8 %copy-start.1 = (bf16[512,384]{1,0:T(8,128)(2,1)S(1)}, bf16[512,384]{1,0:T(8,128)(2,1)}, u32[]{:S(2)}) copy-start(bf16[512,384]{1,0:T(8,128)(2,1)} %param.10) | copy-start | bytes 1179652
  95.1 6.6 %copy-start.2 = (bf16[512,384]{1,0:T(8,128)(2,1)S(1)}, bf16[512,384]{1,0:T(8,128)(2,1)}, u32[]{:S(2)}) copy-start(bf16[512,384]{1,0:T(8,128)(2,1)} %param.11) | copy-start | bytes 1179652
  95.6 29.7 %copy-start.3 = (f32[384]{0:T(512)S(1)}, f32[384]{0:T(512)}, u32[]{:S(2)}) copy-start(f32[384]{0:T(512)} %param.13) | copy-start | bytes 4612
  97.1 16.1 %all-to-all-start.2 = ((f32[4,128,384]{2,1,0:T(8,128)}), f32[4,128,384]{2,1,0:T(8,128)S(1)}, u32[]{:S(2)}, u32[]{:S(2)}) async-start(f32[4,128,384]{2,1,0:T(8,128)} %pad_maximum_fusion), calls=%async_computation.2 | async-start | bytes 1572864 | tf_op jit(solution)/shard_map/all_to_all | solution.py:65
  113.2 21.9 %copy-start.4 = (s32[64]{0:T(128)S(1)}, s32[64]{0:T(128)}, u32[]{:S(2)}) copy-start(s32[64]{0:T(128)} %param.9) | copy-start | bytes 772
  128.0 18.9 %all-to-all-start.3 = ((bf16[16,8,384]{2,1,0:T(8,128)(2,1)}), bf16[16,8,384]{2,1,0:T(8,128)(2,1)S(1)}, u32[]{:S(2)}, u32[]{:S(2)}) async-start(bf16[16,8,384]{2,1,0:T(8,128)(2,1)} %convert_element_type.42), calls=%async_computation.3 | async-start | bytes 196608 | tf_op jit(solution)/shard_map/all_to_all | solution.py:83
  146.9 24.4 %all-to-all-start = ((f32[16,8,640]{2,1,0:T(8,128)}), f32[16,8,640]{2,1,0:T(8,128)S(1)}, u32[]{:S(2)}, u32[]{:S(2)}) async-start(f32[16,8,640]{2,1,0:T(8,128)} %bitcast), calls=%async_computation | async-start | bytes 655360 | tf_op jit(solution)/shard_map/all_to_all | solution.py:41
  181.2 25.1 %all-to-all-start.4 = ((f32[16,8,640]{2,1,0:T(8,128)}), f32[16,8,640]{2,1,0:T(8,128)S(1)}, u32[]{:S(2)}, u32[]{:S(2)}) async-start(f32[16,8,640]{2,1,0:T(8,128)} %get-tuple-element.18), calls=%async_computation.4 | async-start | bytes 655360 | tf_op jit(solution)/shard_map/all_to_all | solution.py:104
  206.9 23.5 %all-to-all-start.5 = ((f32[16,1,128]{2,1,0:T(1,128)}), f32[16,1,128]{2,1,0:T(1,128)S(1)}, u32[]{:S(2)}, u32[]{:S(2)}) async-start(f32[16,1,128]{2,1,0:T(1,128)} %broadcast_in_dim.30), calls=%async_computation.5 | async-start | bytes 16384 | tf_op jit(solution)/shard_map/all_to_all | solution.py:107
Sparse Core Ops, SparseCore 0:
  67.7 78.9 all-gather.6

commit v8 on v5

--- a/solution.py
+++ b/solution.py
@@ -43,8 +43,7 @@
     depth, cols = w_query.shape
     query_rows = lax.all_to_all(jnp.broadcast_to(w_query, (z_size, depth, cols)), "z", 0, 0)
 
-    out_depth = w_out.shape[0]
-    out_rows = lax.all_gather(jnp.pad(w_out, ((0, 16), (0, 0))), "z")
+    out_rows = lax.all_gather(w_out, STEP, axis=0, tiled=True)
 
     sums = jnp.stack([jnp.sum(latent, axis=-1), jnp.sum(latent * latent, axis=-1)])
     sums = tp_sum(sums) / full_width
@@ -63,10 +62,6 @@
     ]
     partial = jnp.concatenate(partial)
     query = jnp.sum(lax.all_to_all(partial, "x", 0, 0), axis=0)
-    out_rows, query = lax.optimization_barrier((out_rows, query))
-    out_rows = out_rows[:, :out_depth].reshape(-1, block)
-    out_rows = lax.all_gather(out_rows, "x", axis=0, tiled=True)
-
     query_width = query.shape[1] * lax.axis_size(TP)
     square_sum = tp_sum(jnp.sum(query * query, axis=-1))
     query_scale = lax.rsqrt(square_sum / query_width + epsilon)[:, None]
@@ -85,24 +80,32 @@
     attended = attended.reshape(token_count, local_heads * HD).astype(jnp.bfloat16)
     attended = attended.reshape(z_size, slice_tokens, -1)
     attended = lax.all_to_all(attended, "z", 0, 0).reshape(token_count, -1)
-    attended_all = lax.all_gather(attended, TP, axis=1, tiled=True)
-    velocity = jnp.dot(attended_all, out_rows, preferred_element_type=jnp.float32)
-    velocity = velocity.reshape(z_size, slice_tokens, block)
-
     later = jnp.concatenate([timesteps[1:], jnp.zeros((1,), timesteps.dtype)])
     step_sizes = sigma_of(later) - sigma_of(timesteps)
-    step_sizes = lax.dynamic_slice_in_dim(step_sizes, x_here * z_size, z_size)
-    drift = step_sizes[:, None, None] * velocity
+    step_sizes = lax.dynamic_slice_in_dim(step_sizes, x_here * z_size, z_size)[:, None, None]
+
+    weighted = jnp.sum(step_sizes * attended.reshape(z_size, slice_tokens, -1), axis=0)
+    width = weighted.shape[1]
+    sides = lax.all_gather(jnp.concatenate([weighted, rows_here[0]], axis=1), "x")
+    weighted = jnp.zeros_like(weighted)
+    for at in range(x_size - 1):
+        weighted = weighted + jnp.where(at < x_here, sides[at, :, :width], 0.0)
+    high = lax.reduce_precision(weighted, 8, 7)
+    terms = [high.astype(jnp.bfloat16), (weighted - high).astype(jnp.bfloat16)]
+    rows = jnp.concatenate([attended, *terms])
+
+    rows = lax.all_gather(rows, TP, axis=1, tiled=True)
+    product = jnp.dot(rows, out_rows, preferred_element_type=jnp.float32)
+    velocity = product[:token_count].reshape(z_size, slice_tokens, block)
+    terms = product[token_count:].reshape(2, slice_tokens, block)
+    start = sides[0, :, width:] + (terms[0] + terms[1])
+    drift = step_sizes * velocity
 
     running = drift
     reach = 1
     while reach < z_size:
         running = running + jnp.pad(running[:-reach], ((reach, 0), (0, 0), (0, 0)))
         reach *= 2
-    start = jnp.where(x_here == 0, rows_here[0], 0.0)
-    totals = lax.all_gather(running[-1] + start, "x")
-    for at in range(x_size - 1):
-        start = start + jnp.where(at < x_here, totals[at], 0.0)
     change = start + jnp.pad(running[:-1], ((1, 0), (0, 0), (0, 0))) - rows_here
     change_sum = jnp.sum(change * change, axis=(1, 2), keepdims=True)
     change_sum = jnp.broadcast_to(change_sum, (z_size, slice_tokens, HD))

time: 240 us -> 226 us (0.942)
  waiting for transfers between devices: 29.1 us -> 12.9 us
  starting transfers between devices: 27 us -> 42 us
  blocking collectives: 148 us -> 138 us
  local copies, waits for them, and re-layouts: 8.07 us -> 4.34 us
    all_gather x2 -> x1, waiting for transfers between devices: 17.3 us -> 0.01 us  [on_device(): out_rows = lax.all_gather(w_out, STEP, axis=0, tiled=True)]
    all_to_all x1, starting transfers between devices: 3.55 us -> 13.5 us  [on_device(): lax.all_to_all(latent.reshape(z_size, slice_tokens, block), 'z', 0, 0)]
    all_to_all x1, blocking collectives: 26.5 us -> 18 us  [on_device(): got = lax.all_to_all(sent, 'z', 0, 0)]
    all_to_all x1, starting transfers between devices: 6.93 us -> 12 us  [on_device(): attended = lax.all_to_all(attended, 'z', 0, 0).reshape(token_count, -1)]
    psum x6, blocking collectives: 48.5 us -> 44.5 us  [tp_sum(): return lax.psum(lax.psum(value, 'core'), 'y')]
    all_gather x2, blocking collectives: 27.1 us -> 29.6 us  [the longest x1 19.9 us: on_device(): rows = lax.all_gather(rows, TP, axis=1, tiled=True)]
  transfers between devices with their start and end apart: 6 -> 5, of which waited for: 2 -> 1; matrix products, arithmetic and copies ran while one was open for 5% -> 4% of each run, Pallas kernels for 0% -> 0%
where the time goes in v8:
time: 226 us; the launch traced here: 224 us
  blocking collectives  138 us (61%)
  starting transfers between devices  42 us (19%)
  between operations  16.1 us (7%)
  waiting for transfers between devices  12.9 us (6%)
  matrix products  5.77 us (3%)
  other arithmetic  4.87 us (2%)
  local copies, waits for them, and re-layouts  4.34 us (2%)
    psum x6, blocking collectives, tp_sum(): return lax.psum(lax.psum(value, 'core'), 'y')  44.5 us
    all_gather x1, blocking collectives, on_device(): gathered = lax.all_gather(flipped, 'y')  23 us
    all_gather x1, blocking collectives, on_device(): rows = lax.all_gather(rows, TP, axis=1, tiled=True)  19.9 us
    all_to_all x1, blocking collectives, on_device(): got = lax.all_to_all(sent, 'z', 0, 0)  18 us
    all_to_all x1, blocking collectives, on_device(): query = jnp.sum(lax.all_to_all(partial, 'x', 0, 0), axis=0)  16 us
    all_to_all x1, starting transfers between devices, on_device(): lax.all_to_all(jnp.broadcast_to(w_query, (z_size, depth, cols)), 'z', 0, 0)  15.7 us
    all_to_all x1, starting transfers between devices, on_device(): lax.all_to_all(latent.reshape(z_size, slice_tokens, block), 'z', 0, 0)  13.5 us
    all_to_all x1, waiting for transfers between devices, on_device(): attended = lax.all_to_all(attended, 'z', 0, 0).reshape(token_count, -1)  12.2 us
  transfers between devices with their start and end apart: 5, of which 1 were waited for; matrix products, arithmetic and copies ran while one was open for 4% of the time, Pallas kernels for 0%

profile of v8, /device:TPU:1, one launch (start us, length us, event | category | flops | bytes accessed | tf_op | source)
XLA Modules:
  0.0 223.5 jit_solution(1736908350824911033)
XLA Ops:
  7.2 0.0 all-gather.6.cloned.1.call-start
  7.2 0.7 all-gather.6.cloned.1.call-update
  7.9 1.9 broadcast_in_dim.10
  9.8 15.7 %all-to-all-start = ((bf16[16,80,384]{2,1,0:T(8,128)(2,1)}), bf16[16,80,384]{2,1,0:T(8,128)(2,1)S(1)}, u32[]{:S(2)}, u32[]{:S(2)}) async-start(bf16[16,80,384]{2,1,0:T(8,128)(2,1)} %broadcast_in_dim.10), calls=%async_computation | async-start | bytes 1966080 | tf_op jit(solution)/shard_map/all_to_all | solution.py:44
  25.5 1.1 reduce_sum.74
  26.6 1.1 fusion.5
  27.7 3.1 %psum.42 = f32[2,128]{1,0:T(2,128)S(1)} all-reduce(f32[2,128]{1,0:T(2,128)S(1)} %pad_maximum_fusion.4), channel_id=1, replica_groups=mesh['x'=4,'z'=16,'y'=4,'core'=2] {'core'}, use_global_device_ids=true, to_apply=%region_2.0 | all-reduce | flops 256 | bytes 2048 | tf_op jit(solution)/shard_map/psum | solution.py:22
  30.8 9.4 %psum.43 = f32[2,128]{1,0:T(2,128)S(1)} all-reduce(f32[2,128]{1,0:T(2,128)S(1)} %psum.42), channel_id=1, replica_groups=mesh['x'=4,'z'=16,'y'=4,'core'=2] {'y'}, use_global_device_ids=true, to_apply=%region_3.0 | all-reduce | flops 256 | bytes 2048 | tf_op jit(solution)/shard_map/psum | solution.py:22
  40.2 1.1 fusion.8
  41.3 0.7 collective-permute-start
  42.0 23.0 %all-gather = bf16[512,640]{1,0:T(8,128)(2,1)S(1)} all-gather(bf16[128,640]{1,0:T(8,128)(2,1)S(1)} %collective-permute-done), channel_id=2, replica_groups=mesh['x'=4,'z'=16,'y'=4,'core'=2] {'y'}, dimensions={0}, use_global_device_ids=true | all-gather | bytes 819200 | tf_op jit(solution)/shard_map/all_gather | solution.py:55
  65.0 0.1 fusion.23
  65.1 4.1 %all-gather.2 = bf16[4,128,640]{2,1,0:T(8,128)(2,1)S(1)} all-gather(bf16[2,128,640]{2,1,0:T(8,128)(2,1)S(1)} %bitcast.84), channel_id=4, replica_groups=mesh['x'=4,'z'=16,'y'=4,'core'=2] {'core'}, dimensions={0}, use_global_device_ids=true | all-gather | bytes 983040 | tf_op jit(solution)/shard_map/all_gather | solution.py:57
  69.2 2.3 %all-gather.1 = bf16[4,128,640]{2,1,0:T(8,128)(2,1)S(1)} all-gather(bf16[2,128,640]{2,1,0:T(8,128)(2,1)S(1)} %bitcast.83), channel_id=3, replica_groups=mesh['x'=4,'z'=16,'y'=4,'core'=2] {'core'}, dimensions={0}, use_global_device_ids=true | all-gather | bytes 983040 | tf_op jit(solution)/shard_map/all_gather | solution.py:57
  71.5 0.5 convolution_bitcast_fusion
  72.0 0.5 convolution_bitcast_fusion.1
  72.5 0.1 pad_maximum_fusion
  72.6 16.0 %all_to_all.25 = f32[4,128,384]{2,1,0:T(8,128)S(1)} all-to-all(f32[4,128,384]{2,1,0:T(8,128)S(1)} %pad_maximum_fusion), channel_id=1, replica_groups=mesh['x'=4,'z'=16,'y'=4,'core'=2] {'x'}, dimensions={0} | all-to-all | bytes 1572864 | tf_op jit(solution)/shard_map/all_to_all | solution.py:64
  88.5 13.5 %all-to-all-start.3 = ((f32[16,8,640]{2,1,0:T(8,128)}), f32[16,8,640]{2,1,0:T(8,128)S(1)}, u32[]{:S(2)}, u32[]{:S(2)}) async-start(f32[16,8,640]{2,1,0:T(8,128)} %bitcast.21), calls=%async_computation.3 | async-start | bytes 655360 | tf_op jit(solution)/shard_map/all_to_all | solution.py:41
  102.0 0.2 copy.21
  102.2 0.2 copy.24
  102.4 0.1 slice.65
  102.6 0.1 copy.20
  102.7 0.1 multiply_reduce_fusion.2
  102.8 4.2 %psum.44 = f32[128]{0:T(128)S(1)} all-reduce(f32[128]{0:T(128)S(1)} %multiply_reduce_fusion.2), channel_id=1, replica_groups=mesh['x'=4,'z'=16,'y'=4,'core'=2] {'core'}, use_global_device_ids=true, to_apply=%region_6.0 | all-reduce | flops 128 | bytes 1024 | tf_op jit(solution)/shard_map/psum | solution.py:22
  107.0 7.2 %psum.45 = f32[128]{0:T(128)S(1)} all-reduce(f32[128]{0:T(128)S(1)} %psum.44), channel_id=1, replica_groups=mesh['x'=4,'z'=16,'y'=4,'core'=2] {'y'}, use_global_device_ids=true, to_apply=%region_7.0 | all-reduce | flops 128 | bytes 1024 | tf_op jit(solution)/shard_map/psum | solution.py:22
  114.2 0.6 fusion.24
  114.8 0.4 convolution_multiply_fusion
  115.2 0.8 fusion.3
  116.0 0.1 copy.26
  116.1 0.7 convert_element_type.51
  116.8 12.0 %all-to-all-start.2 = ((bf16[16,8,384]{2,1,0:T(8,128)(2,1)}), bf16[16,8,384]{2,1,0:T(8,128)(2,1)S(1)}, u32[]{:S(2)}, u32[]{:S(2)}) async-start(bf16[16,8,384]{2,1,0:T(8,128)(2,1)} %convert_element_type.51), calls=%async_computation.2 | async-start | bytes 196608 | tf_op jit(solution)/shard_map/all_to_all | solution.py:82
  128.8 0.1 divide_subtract_fusion
  128.9 0.1 dynamic_slice.3
  129.0 12.2 %all-to-all-done.2 = bf16[16,8,384]{2,1,0:T(8,128)(2,1)S(1)} async-done(((bf16[16,8,384]{2,1,0:T(8,128)(2,1)}), bf16[16,8,384]{2,1,0:T(8,128)(2,1)S(1)}, u32[]{:S(2)}, u32[]{:S(2)}) %all-to-all-start.2) | async-done | bytes 98336 | tf_op jit(solution)/shard_map/all_to_all | solution.py:82
  141.2 0.1 multiply_reduce_fusion.1
  141.3 9.7 %all-gather.3 = f32[32,1024]{1,0:T(8,128)S(1)} all-gather(f32[8,1024]{1,0:T(8,128)S(1)} %pad_maximum_fusion.3), channel_id=5, replica_groups=mesh['x'=4,'z'=16,'y'=4,'core'=2] {'x'}, dimensions={0}, use_global_device_ids=true | all-gather | bytes 163840 | tf_op jit(solution)/shard_map/all_gather | solution.py:89
  151.1 19.9 %all_gather.38 = bf16[144,3072]{1,0:T(8,128)(2,1)S(1)} all-gather(bf16[144,384]{1,0:T(8,128)(2,1)S(1)} %pad_maximum_fusion.2), channel_id=1, replica_groups=mesh['x'=4,'z'=16,'y'=4,'core'=2] {'y','core'}, dimensions={1}, use_global_device_ids=true | all-gather | bytes 995328 | tf_op jit(solution)/shard_map/all_gather | solution.py:97
  171.0 3.0 %fusion.25 = f32[144,640]{1,0:T(8,128)S(1)} fusion(bf16[144,3072]{1,0:T(8,128)(2,1)S(1)} %all_gather.38, bf16[3072,640]{1,0:T(8,128)(2,1)} %all-gather.6.cloned.1.call-done), kind=kOutput, calls=%fused_computation.61 | convolution fusion | flops 566231040 | bytes 5185536 | tf_op jit(solution)/shard_map/dot_general | solution.py:98
  174.0 0.1 fusion.4
  174.1 0.1 pad_add_fusion.3
  174.5 0.2 multiply_reduce_fusion
  174.7 0.1 broadcast_in_dim.12
  174.8 18.0 %all_to_all.26 = f32[16,8,768]{2,1,0:T(8,128)S(1)} all-to-all(f32[16,8,768]{2,1,0:T(8,128)S(1)} %pad_maximum_fusion.1), channel_id=1, replica_groups=mesh['x'=4,'z'=16,'y'=4,'core'=2] {'z'}, dimensions={0} | all-to-all | bytes 786432 | tf_op jit(solution)/shard_map/all_to_all | solution.py:113
  192.9 0.6 slice_reduce_fusion
  193.5 12.1 %psum.46 = f32[]{:T(128)} all-reduce(f32[]{:T(128)} %slice_reduce_fusion), channel_id=1, replica_groups=mesh['x'=4,'z'=16,'y'=4,'core'=2] {'core'}, use_global_device_ids=true, to_apply=%region_13.14 | all-reduce | flops 1 | bytes 8 | tf_op jit(solution)/shard_map/psum | solution.py:22
  205.5 8.6 %psum.47 = f32[]{:T(128)} all-reduce(f32[]{:T(128)} %psum.46), channel_id=1, replica_groups=mesh['x'=4,'z'=16,'y'=4,'core'=2] {'y'}, use_global_device_ids=true, to_apply=%region_14.15 | all-reduce | flops 1 | bytes 8 | tf_op jit(solution)/shard_map/psum | solution.py:22
  214.8 0.7 slice_bitcast_fusion
  (33 shorter events, 0.4 us)
Async XLA Ops:
  7.2 163.9 %all-gather.6.cloned.1.call-start = ((), (), s32[]{:S(2)}) async-start(), calls=%async_computation.5 | async-start | bytes 3993600 | tf_op jit(solution)/shard_map/all_gather | solution.py:46
  9.8 61.7 %all-to-all-start = ((bf16[16,80,384]{2,1,0:T(8,128)(2,1)}), bf16[16,80,384]{2,1,0:T(8,128)(2,1)S(1)}, u32[]{:S(2)}, u32[]{:S(2)}) async-start(bf16[16,80,384]{2,1,0:T(8,128)(2,1)} %broadcast_in_dim.10), calls=%async_computation | async-start | bytes 1966080 | tf_op jit(solution)/shard_map/all_to_all | solution.py:44
  41.3 0.7 collective-permute-start
  71.5 30.6 %copy-start = (bf16[512,384]{1,0:T(8,128)(2,1)S(1)}, bf16[512,384]{1,0:T(8,128)(2,1)}, u32[]{:S(2)}) copy-start(bf16[512,384]{1,0:T(8,128)(2,1)} %param.10) | copy-start | bytes 1179652
  71.5 30.8 %copy-start.1 = (bf16[512,384]{1,0:T(8,128)(2,1)S(1)}, bf16[512,384]{1,0:T(8,128)(2,1)}, u32[]{:S(2)}) copy-start(bf16[512,384]{1,0:T(8,128)(2,1)} %param.11) | copy-start | bytes 1179652
  72.0 30.5 %copy-start.3 = (s32[64]{0:T(128)S(1)}, s32[64]{0:T(128)}, u32[]{:S(2)}) copy-start(s32[64]{0:T(128)} %param.9) | copy-start | bytes 772
  72.5 41.7 %copy-start.2 = (f32[384]{0:T(512)S(1)}, f32[384]{0:T(512)}, u32[]{:S(2)}) copy-start(f32[384]{0:T(512)} %param.13) | copy-start | bytes 4612
  88.5 28.3 %all-to-all-start.3 = ((f32[16,8,640]{2,1,0:T(8,128)}), f32[16,8,640]{2,1,0:T(8,128)S(1)}, u32[]{:S(2)}, u32[]{:S(2)}) async-start(f32[16,8,640]{2,1,0:T(8,128)} %bitcast.21), calls=%async_computation.3 | async-start | bytes 655360 | tf_op jit(solution)/shard_map/all_to_all | solution.py:41
  116.8 24.4 %all-to-all-start.2 = ((bf16[16,8,384]{2,1,0:T(8,128)(2,1)}), bf16[16,8,384]{2,1,0:T(8,128)(2,1)S(1)}, u32[]{:S(2)}, u32[]{:S(2)}) async-start(bf16[16,8,384]{2,1,0:T(8,128)(2,1)} %convert_element_type.51), calls=%async_computation.2 | async-start | bytes 196608 | tf_op jit(solution)/shard_map/all_to_all | solution.py:82
Sparse Core Ops, SparseCore 0:
  11.0 155.4 all-gather.5

commit v9 on v8

--- a/solution.py
+++ b/solution.py
@@ -28,6 +28,16 @@
     return lax.ppermute(value, ("x", "y"), pairs)
 
 
+def sum_over(terms, axis):
+    size, mine = lax.axis_size(axis), lax.axis_index(axis)
+    total = lax.dynamic_index_in_dim(terms, mine, 0, keepdims=False)
+    for shift in range(1, size):
+        pairs = [(at, (at + shift) % size) for at in range(size)]
+        term = lax.dynamic_index_in_dim(terms, (mine + shift) % size, 0, keepdims=False)
+        total = total + lax.ppermute(term, axis, pairs)
+    return total
+
+
 def on_device(trajectory, timesteps, context_keys, context_values, ln_gain, q_gain, w_query, w_out):
     latent = trajectory[0]
     token_count, block = latent.shape
@@ -38,12 +48,8 @@
     x_here = lax.axis_index("x")
     slice_tokens = token_count // z_size
 
-    rows_here = lax.all_to_all(latent.reshape(z_size, slice_tokens, block), "z", 0, 0)
-
     depth, cols = w_query.shape
     query_rows = lax.all_to_all(jnp.broadcast_to(w_query, (z_size, depth, cols)), "z", 0, 0)
-
-    out_rows = lax.all_gather(w_out, STEP, axis=0, tiled=True)
 
     sums = jnp.stack([jnp.sum(latent, axis=-1), jnp.sum(latent * latent, axis=-1)])
     sums = tp_sum(sums) / full_width
@@ -51,17 +57,25 @@
     row_var = row_square - row_mean * row_mean
     normed = ((latent - row_mean) * lax.rsqrt(row_var + epsilon) * ln_gain).astype(jnp.bfloat16)
 
+    w_out, normed = lax.optimization_barrier((w_out, normed))
+    out_rows = lax.all_gather(w_out, "x")
     flipped = transpose_plane(normed)
+    out_rows, flipped = lax.optimization_barrier((out_rows, flipped))
+    out_rows = lax.all_gather(out_rows, "z", axis=1).reshape(-1, block)
     gathered = lax.all_gather(flipped, "y")
     half = x_size // 2
     parts = [lax.all_gather(gathered[at * half : (at + 1) * half], "core") for at in range(2)]
+    latent, query_rows, parts = lax.optimization_barrier((latent, query_rows, parts))
+    rows_here = lax.all_to_all(latent.reshape(z_size, slice_tokens, block), "z", 0, 0)
     query_weights = query_rows.reshape(2, block, cols)
     partial = [
         jnp.einsum("cxtk,ckn->xtn", part, query_weights, preferred_element_type=jnp.float32)
         for part in parts
     ]
     partial = jnp.concatenate(partial)
-    query = jnp.sum(lax.all_to_all(partial, "x", 0, 0), axis=0)
+
+    query = sum_over(partial, "x")
+    query, rows_here = lax.optimization_barrier((query, rows_here))
     query_width = query.shape[1] * lax.axis_size(TP)
     square_sum = tp_sum(jnp.sum(query * query, axis=-1))
     query_scale = lax.rsqrt(square_sum / query_width + epsilon)[:, None]

time: 226 us -> 231 us (1.022)
  waiting for transfers between devices: 12.9 us -> 21.7 us
  blocking collectives: 138 us -> 132 us
    all_gather x0 -> x1, blocking collectives: none -> 17.4 us  [on_device(): out_rows = lax.all_gather(w_out, 'x')]
    all_to_all x1 -> x0, blocking collectives: 16 us -> none  [on_device(): query = jnp.sum(lax.all_to_all(partial, 'x', 0, 0), axis=0)]
    all_gather x1, blocking collectives: 23 us -> 11.6 us  [on_device(): gathered = lax.all_gather(flipped, 'y')]
    ppermute x0 -> x3, starting transfers between devices: none -> 9.06 us  [sum_over(): total = total + lax.ppermute(term, axis, pairs)]
    all_to_all x1, starting transfers between devices: 12 us -> 5.37 us  [on_device(): attended = lax.all_to_all(attended, 'z', 0, 0).reshape(token_count, -1)]
    ppermute x0 -> x3, waiting for transfers between devices: none -> 5.31 us  [sum_over(): total = total + lax.ppermute(term, axis, pairs)]
    all_to_all x1, waiting for transfers between devices: 0.01 us -> 4.6 us  [on_device(): lax.all_to_all(latent.reshape(z_size, slice_tokens, block), 'z', 0, 0)]
    all_to_all x1, blocking collectives: 18 us -> 22.5 us  [on_device(): got = lax.all_to_all(sent, 'z', 0, 0)]
  transfers between devices with their start and end apart: 5 -> 8, of which waited for: 1 -> 4; matrix products, arithmetic and copies ran while one was open for 4% -> 4% of each run, Pallas kernels for 0% -> 0%
where the time goes in v9:
time: 231 us; the launch traced here: 229 us
  blocking collectives  132 us (57%)
  starting transfers between devices  42.8 us (19%)
  waiting for transfers between devices  21.7 us (9%)
  between operations  16.2 us (7%)
  matrix products  5.65 us (2%)
  local copies, waits for them, and re-layouts  5.33 us (2%)
  other arithmetic  5.07 us (2%)
    psum x6, blocking collectives, tp_sum(): return lax.psum(lax.psum(value, 'core'), 'y')  42.3 us
    all_to_all x1, blocking collectives, on_device(): got = lax.all_to_all(sent, 'z', 0, 0)  22.5 us
    all_gather x1, blocking collectives, on_device(): rows = lax.all_gather(rows, TP, axis=1, tiled=True)  19.4 us
    all_gather x1, blocking collectives, on_device(): out_rows = lax.all_gather(w_out, 'x')  17.4 us
    all_to_all x1, starting transfers between devices, on_device(): lax.all_to_all(jnp.broadcast_to(w_query, (z_size, depth, cols)), 'z', 0, 0)  15.7 us
    all_to_all x1, starting transfers between devices, on_device(): lax.all_to_all(latent.reshape(z_size, slice_tokens, block), 'z', 0, 0)  11.9 us
    all_to_all x1, waiting for transfers between devices, on_device(): attended = lax.all_to_all(attended, 'z', 0, 0).reshape(token_count, -1)  11.7 us
    all_gather x1, blocking collectives, on_device(): gathered = lax.all_gather(flipped, 'y')  11.6 us
  transfers between devices with their start and end apart: 8, of which 4 were waited for; matrix products, arithmetic and copies ran while one was open for 4% of the time, Pallas kernels for 0%

profile of v9, /device:TPU:1, one launch (start us, length us, event | category | flops | bytes accessed | tf_op | source)
XLA Modules:
  0.0 229.0 jit_solution(17849620705756911494)
XLA Ops:
  7.2 1.9 broadcast_in_dim.10
  9.1 15.7 %all-to-all-start = ((bf16[16,80,384]{2,1,0:T(8,128)(2,1)}), bf16[16,80,384]{2,1,0:T(8,128)(2,1)S(1)}, u32[]{:S(2)}, u32[]{:S(2)}) async-start(bf16[16,80,384]{2,1,0:T(8,128)(2,1)} %broadcast_in_dim.10), calls=%async_computation | async-start | bytes 1966080 | tf_op jit(solution)/shard_map/all_to_all | solution.py:52
  24.9 1.1 multiply_reduce_fusion.1
  26.0 1.1 reduce_sum.63
  27.1 3.1 %psum.42 = f32[2,128]{1,0:T(2,128)S(1)} all-reduce(f32[2,128]{1,0:T(2,128)S(1)} %pad_maximum_fusion.3), channel_id=1, replica_groups=mesh['x'=4,'z'=16,'y'=4,'core'=2] {'core'}, use_global_device_ids=true, to_apply=%region_2.0 | all-reduce | flops 256 | bytes 2048 | tf_op jit(solution)/shard_map/psum | solution.py:22
  30.1 9.3 %psum.43 = f32[2,128]{1,0:T(2,128)S(1)} all-reduce(f32[2,128]{1,0:T(2,128)S(1)} %psum.42), channel_id=1, replica_groups=mesh['x'=4,'z'=16,'y'=4,'core'=2] {'y'}, use_global_device_ids=true, to_apply=%region_3.0 | all-reduce | flops 256 | bytes 2048 | tf_op jit(solution)/shard_map/psum | solution.py:22
  39.4 1.1 multiply_convert_fusion
  40.6 0.7 collective-permute-start
  41.3 17.4 %all-gather = bf16[192,640]{1,0:T(8,128)(2,1)} all-gather(bf16[48,640]{1,0:T(8,128)(2,1)S(1)} %copy-done.1), channel_id=2, replica_groups=mesh['x'=4,'z'=16,'y'=4,'core'=2] {'x'}, dimensions={0}, use_global_device_ids=true | all-gather | bytes 307200 | tf_op jit(solution)/shard_map/all_gather | solution.py:61
  58.7 11.6 %all-gather.1 = bf16[512,640]{1,0:T(8,128)(2,1)S(1)} all-gather(bf16[128,640]{1,0:T(8,128)(2,1)S(1)} %collective-permute-done), channel_id=3, replica_groups=mesh['x'=4,'z'=16,'y'=4,'core'=2] {'y'}, dimensions={0}, use_global_device_ids=true | all-gather | bytes 819200 | tf_op jit(solution)/shard_map/all_gather | solution.py:65
  70.3 6.7 %all-gather.2 = bf16[4,128,640]{2,1,0:T(8,128)(2,1)S(1)} all-gather(bf16[2,128,640]{2,1,0:T(8,128)(2,1)S(1)} %bitcast.94), channel_id=4, replica_groups=mesh['x'=4,'z'=16,'y'=4,'core'=2] {'core'}, dimensions={0}, use_global_device_ids=true | all-gather | bytes 983040 | tf_op jit(solution)/shard_map/all_gather | solution.py:67
  77.0 2.3 all-gather.3
  79.3 11.9 %all-to-all-start.1 = ((f32[16,8,640]{2,1,0:T(8,128)}), f32[16,8,640]{2,1,0:T(8,128)S(1)}, u32[]{:S(2)}, u32[]{:S(2)}) async-start(f32[16,8,640]{2,1,0:T(8,128)} %bitcast.21), calls=%async_computation.1 | async-start | bytes 655360 | tf_op jit(solution)/shard_map/all_to_all | solution.py:69
  91.2 0.5 convolution_bitcast_fusion
  91.7 0.5 convolution_bitcast_fusion.1
  92.2 0.1 fusion.13
  92.4 2.8 %collective-permute-start.1 = (f32[128,384]{1,0:T(8,128)S(1)}, f32[128,384]{1,0:T(8,128)S(1)}, u32[]{:S(2)}, u32[]{:S(2)}) collective-permute-start(f32[128,384]{1,0:T(8,128)S(1)} %get-tuple-element.26), channel_id=1, source_target_pairs={{0,128},{128,256},{256,384},{384,0},{1,129},{129,257},{257,385},{3... | collective-permute-start | bytes 589832 | tf_op jit(solution)/shard_map/ppermute | solution.py:37
  95.2 4.3 %collective-permute-start.2 = (f32[128,384]{1,0:T(8,128)S(1)}, f32[128,384]{1,0:T(8,128)S(1)}, u32[]{:S(2)}, u32[]{:S(2)}) collective-permute-start(f32[128,384]{1,0:T(8,128)S(1)} %get-tuple-element.27), channel_id=1, source_target_pairs={{0,256},{128,384},{256,0},{384,128},{1,257},{129,385},{257,1},{385... | collective-permute-start | bytes 589832 | tf_op jit(solution)/shard_map/ppermute | solution.py:37
  99.5 1.9 collective-permute-start.3
  101.5 0.2 copy.28
  101.7 1.2 copy.31
  102.9 3.2 %collective-permute-done.2 = f32[128,384]{1,0:T(8,128)S(1)} collective-permute-done((f32[128,384]{1,0:T(8,128)S(1)}, f32[128,384]{1,0:T(8,128)S(1)}, u32[]{:S(2)}, u32[]{:S(2)}) %collective-permute-start.2) | collective-permute-done | bytes 196640 | tf_op jit(solution)/shard_map/ppermute | solution.py:37
  106.1 2.1 collective-permute-done.3
  108.3 4.6 %all-to-all-done.1 = f32[16,8,640]{2,1,0:T(8,128)S(1)} async-done(((f32[16,8,640]{2,1,0:T(8,128)}), f32[16,8,640]{2,1,0:T(8,128)S(1)}, u32[]{:S(2)}, u32[]{:S(2)}) %all-to-all-start.1) | async-done | bytes 327712 | tf_op jit(solution)/shard_map/all_to_all | solution.py:69
  112.9 0.1 multiply_reduce_fusion.3
  113.0 6.9 %psum.44 = f32[128]{0:T(128)S(1)} all-reduce(f32[128]{0:T(128)S(1)} %multiply_reduce_fusion.3), channel_id=1, replica_groups=mesh['x'=4,'z'=16,'y'=4,'core'=2] {'core'}, use_global_device_ids=true, to_apply=%region_5.6 | all-reduce | flops 128 | bytes 1024 | tf_op jit(solution)/shard_map/psum | solution.py:22
  119.9 7.5 %psum.45 = f32[128]{0:T(128)S(1)} all-reduce(f32[128]{0:T(128)S(1)} %psum.44), channel_id=1, replica_groups=mesh['x'=4,'z'=16,'y'=4,'core'=2] {'y'}, use_global_device_ids=true, to_apply=%region_6.7 | all-reduce | flops 128 | bytes 1024 | tf_op jit(solution)/shard_map/psum | solution.py:22
  127.4 0.1 multiply_convert_fusion.1
  127.5 0.1 copy.27
  127.7 0.5 fusion.29
  128.2 0.3 convolution_multiply_fusion
  128.5 0.8 fusion.3
  129.3 0.1 copy.33
  129.4 0.7 convert_element_type.50
  130.2 5.4 %all-to-all-start.2 = ((bf16[16,8,384]{2,1,0:T(8,128)(2,1)}), bf16[16,8,384]{2,1,0:T(8,128)(2,1)S(1)}, u32[]{:S(2)}, u32[]{:S(2)}) async-start(bf16[16,8,384]{2,1,0:T(8,128)(2,1)} %convert_element_type.50), calls=%async_computation.2 | async-start | bytes 196608 | tf_op jit(solution)/shard_map/all_to_all | solution.py:96
  135.7 11.7 %all-to-all-done.2 = bf16[16,8,384]{2,1,0:T(8,128)(2,1)S(1)} async-done(((bf16[16,8,384]{2,1,0:T(8,128)(2,1)}), bf16[16,8,384]{2,1,0:T(8,128)(2,1)S(1)}, u32[]{:S(2)}, u32[]{:S(2)}) %all-to-all-start.2) | async-done | bytes 98336 | tf_op jit(solution)/shard_map/all_to_all | solution.py:96
  147.4 0.1 multiply_reduce_fusion.2
  147.5 10.3 %all-gather.4 = f32[32,1024]{1,0:T(8,128)S(1)} all-gather(f32[8,1024]{1,0:T(8,128)S(1)} %pad_maximum_fusion.2), channel_id=6, replica_groups=mesh['x'=4,'z'=16,'y'=4,'core'=2] {'x'}, dimensions={0}, use_global_device_ids=true | all-gather | bytes 163840 | tf_op jit(solution)/shard_map/all_gather | solution.py:103
  157.8 19.4 %all_gather.49 = bf16[144,3072]{1,0:T(8,128)(2,1)S(1)} all-gather(bf16[144,384]{1,0:T(8,128)(2,1)S(1)} %pad_maximum_fusion.1), channel_id=1, replica_groups=mesh['x'=4,'z'=16,'y'=4,'core'=2] {'y','core'}, dimensions={1}, use_global_device_ids=true | all-gather | bytes 995328 | tf_op jit(solution)/shard_map/all_gather | solution.py:111
  177.3 3.0 %fusion.30 = f32[144,640]{1,0:T(8,128)S(1)} fusion(bf16[144,3072]{1,0:T(8,128)(2,1)S(1)} %all_gather.49, bf16[3072,640]{1,0:T(8,128)(2,1)} %bitcast.88), kind=kOutput, calls=%fused_computation.73 | convolution fusion | flops 566231040 | bytes 5185536 | tf_op jit(solution)/shard_map/dot_general | solution.py:112
  180.3 0.1 fusion.4
  180.4 0.1 pad_add_fusion.3
  180.8 0.2 multiply_reduce_fusion
  181.1 22.5 %all_to_all.20 = f32[16,8,768]{2,1,0:T(8,128)S(1)} all-to-all(f32[16,8,768]{2,1,0:T(8,128)S(1)} %pad_maximum_fusion), channel_id=1, replica_groups=mesh['x'=4,'z'=16,'y'=4,'core'=2] {'z'}, dimensions={0} | all-to-all | bytes 786432 | tf_op jit(solution)/shard_map/all_to_all | solution.py:127
  203.6 0.6 slice_reduce_fusion
  204.2 8.8 %psum.46 = f32[]{:T(128)} all-reduce(f32[]{:T(128)} %slice_reduce_fusion), channel_id=1, replica_groups=mesh['x'=4,'z'=16,'y'=4,'core'=2] {'core'}, use_global_device_ids=true, to_apply=%region_12.13 | all-reduce | flops 1 | bytes 8 | tf_op jit(solution)/shard_map/psum | solution.py:22
  213.0 6.7 %psum.47 = f32[]{:T(128)} all-reduce(f32[]{:T(128)} %psum.46), channel_id=1, replica_groups=mesh['x'=4,'z'=16,'y'=4,'core'=2] {'y'}, use_global_device_ids=true, to_apply=%region_13.14 | all-reduce | flops 1 | bytes 8 | tf_op jit(solution)/shard_map/psum | solution.py:22
  220.3 0.7 slice_bitcast_fusion
  (40 shorter events, 0.8 us)
Async XLA Ops:
  7.2 34.1 %copy-start.1 = (bf16[48,640]{1,0:T(8,128)(2,1)S(1)}, bf16[48,640]{1,0:T(8,128)(2,1)}, u32[]{:S(2)}) copy-start(bf16[48,640]{1,0:T(8,128)(2,1)} %param.15) | copy-start | bytes 184324
  9.1 70.2 %all-to-all-start = ((bf16[16,80,384]{2,1,0:T(8,128)(2,1)}), bf16[16,80,384]{2,1,0:T(8,128)(2,1)S(1)}, u32[]{:S(2)}, u32[]{:S(2)}) async-start(bf16[16,80,384]{2,1,0:T(8,128)(2,1)} %broadcast_in_dim.10), calls=%async_computation | async-start | bytes 1966080 | tf_op jit(solution)/shard_map/all_to_all | solution.py:52
  24.8 152.5 %all-gather.8.cloned.1.call-start = ((), (), s32[]{:S(2)}) async-start(), calls=%async_computation.4 | async-start | bytes 4177920 | tf_op jit(solution)/shard_map/all_gather | solution.py:64
  40.6 18.1 %collective-permute-start = (bf16[128,640]{1,0:T(8,128)(2,1)S(1)}, bf16[128,640]{1,0:T(8,128)(2,1)S(1)}, u32[]{:S(2)}, u32[]{:S(2)}) collective-permute-start(bf16[128,640]{1,0:T(8,128)(2,1)S(1)} %multiply_convert_fusion), channel_id=1, source_target_pairs={{0,0},{2,128},{4,256},{6,384},{128,2},{130,130},{132,258},{134,386... | collective-permute-start | bytes 491528 | tf_op jit(solution)/shard_map/ppermute | solution.py:28
  70.3 31.1 %copy-start = (bf16[512,384]{1,0:T(8,128)(2,1)S(1)}, bf16[512,384]{1,0:T(8,128)(2,1)}, u32[]{:S(2)}) copy-start(bf16[512,384]{1,0:T(8,128)(2,1)} %param.10) | copy-start | bytes 1179652
  79.3 23.6 %copy-start.3 = (s32[64]{0:T(128)S(1)}, s32[64]{0:T(128)}, u32[]{:S(2)}) copy-start(s32[64]{0:T(128)} %param.9) | copy-start | bytes 772
  79.3 33.6 %all-to-all-start.1 = ((f32[16,8,640]{2,1,0:T(8,128)}), f32[16,8,640]{2,1,0:T(8,128)S(1)}, u32[]{:S(2)}, u32[]{:S(2)}) async-start(f32[16,8,640]{2,1,0:T(8,128)} %bitcast.21), calls=%async_computation.1 | async-start | bytes 655360 | tf_op jit(solution)/shard_map/all_to_all | solution.py:69
  91.2 36.2 %copy-start.2 = (f32[384]{0:T(512)S(1)}, f32[384]{0:T(512)}, u32[]{:S(2)}) copy-start(f32[384]{0:T(512)} %param.13) | copy-start | bytes 4612
  92.4 10.6 %collective-permute-start.1 = (f32[128,384]{1,0:T(8,128)S(1)}, f32[128,384]{1,0:T(8,128)S(1)}, u32[]{:S(2)}, u32[]{:S(2)}) collective-permute-start(f32[128,384]{1,0:T(8,128)S(1)} %get-tuple-element.26), channel_id=1, source_target_pairs={{0,128},{128,256},{256,384},{384,0},{1,129},{129,257},{257,385},{3... | collective-permute-start | bytes 589832 | tf_op jit(solution)/shard_map/ppermute | solution.py:37
  95.2 10.9 %collective-permute-start.2 = (f32[128,384]{1,0:T(8,128)S(1)}, f32[128,384]{1,0:T(8,128)S(1)}, u32[]{:S(2)}, u32[]{:S(2)}) collective-permute-start(f32[128,384]{1,0:T(8,128)S(1)} %get-tuple-element.27), channel_id=1, source_target_pairs={{0,256},{128,384},{256,0},{384,128},{1,257},{129,385},{257,1},{385... | collective-permute-start | bytes 589832 | tf_op jit(solution)/shard_map/ppermute | solution.py:37
  99.5 8.7 %collective-permute-start.3 = (f32[128,384]{1,0:T(8,128)S(1)}, f32[128,384]{1,0:T(8,128)S(1)}, u32[]{:S(2)}, u32[]{:S(2)}) collective-permute-start(f32[128,384]{1,0:T(8,128)S(1)} %get-tuple-element.28), channel_id=1, source_target_pairs={{0,384},{128,0},{256,128},{384,256},{1,385},{129,1},{257,129},{385... | collective-permute-start | bytes 589832 | tf_op jit(solution)/shard_map/ppermute | solution.py:37
  130.2 17.3 %all-to-all-start.2 = ((bf16[16,8,384]{2,1,0:T(8,128)(2,1)}), bf16[16,8,384]{2,1,0:T(8,128)(2,1)S(1)}, u32[]{:S(2)}, u32[]{:S(2)}) async-start(bf16[16,8,384]{2,1,0:T(8,128)(2,1)} %convert_element_type.50), calls=%async_computation.2 | async-start | bytes 196608 | tf_op jit(solution)/shard_map/all_to_all | solution.py:96
Sparse Core Ops, SparseCore 0:
  58.8 88.4 all-gather.7

commit v10 on v5

--- a/solution.py
+++ b/solution.py
@@ -38,13 +38,10 @@
     x_here = lax.axis_index("x")
     slice_tokens = token_count // z_size
 
-    rows_here = lax.all_to_all(latent.reshape(z_size, slice_tokens, block), "z", 0, 0)
-
     depth, cols = w_query.shape
     query_rows = lax.all_to_all(jnp.broadcast_to(w_query, (z_size, depth, cols)), "z", 0, 0)
 
-    out_depth = w_out.shape[0]
-    out_rows = lax.all_gather(jnp.pad(w_out, ((0, 16), (0, 0))), "z")
+    rows_here = lax.all_to_all(latent.reshape(z_size, slice_tokens, block), "z", 0, 0)
 
     sums = jnp.stack([jnp.sum(latent, axis=-1), jnp.sum(latent * latent, axis=-1)])
     sums = tp_sum(sums) / full_width
@@ -52,7 +49,11 @@
     row_var = row_square - row_mean * row_mean
     normed = ((latent - row_mean) * lax.rsqrt(row_var + epsilon) * ln_gain).astype(jnp.bfloat16)
 
+    w_out, normed = lax.optimization_barrier((w_out, normed))
+    out_rows = lax.all_gather(w_out, "x")
     flipped = transpose_plane(normed)
+    out_rows, flipped = lax.optimization_barrier((out_rows, flipped))
+    out_rows = lax.all_gather(out_rows, "z", axis=1).reshape(-1, block)
     gathered = lax.all_gather(flipped, "y")
     half = x_size // 2
     parts = [lax.all_gather(gathered[at * half : (at + 1) * half], "core") for at in range(2)]
@@ -63,10 +64,6 @@
     ]
     partial = jnp.concatenate(partial)
     query = jnp.sum(lax.all_to_all(partial, "x", 0, 0), axis=0)
-    out_rows, query = lax.optimization_barrier((out_rows, query))
-    out_rows = out_rows[:, :out_depth].reshape(-1, block)
-    out_rows = lax.all_gather(out_rows, "x", axis=0, tiled=True)
-
     query_width = query.shape[1] * lax.axis_size(TP)
     square_sum = tp_sum(jnp.sum(query * query, axis=-1))
     query_scale = lax.rsqrt(square_sum / query_width + epsilon)[:, None]

time: 240 us -> 254 us (1.058)
  waiting for transfers between devices: 29.1 us -> 49.8 us
  blocking collectives: 148 us -> 142 us
  local copies, waits for them, and re-layouts: 8.07 us -> 4.33 us
    all_to_all x1, waiting for transfers between devices: 0.01 us -> 30.1 us  [on_device(): lax.all_to_all(jnp.broadcast_to(w_query, (z_size, depth, cols)), 'z', 0, 0)]
    all_gather x0 -> x1, blocking collectives: none -> 17.9 us  [on_device(): out_rows = lax.all_gather(w_out, 'x')]
    all_gather x2 -> x1, waiting for transfers between devices: 17.3 us -> 0.01 us  [on_device(): out_rows = lax.all_gather(out_rows, 'z', axis=1).reshape(-1, block)]
    all_to_all x1 -> x0, blocking collectives: 16.2 us -> none  [on_device(): query = jnp.sum(lax.all_to_all(partial, 'x', 0, 0), axis=0)]
    all_gather x1, blocking collectives: 23 us -> 10.3 us  [on_device(): gathered = lax.all_gather(flipped, 'y')]
    all_to_all x0 -> x1, waiting for transfers between devices: none -> 7.94 us  [on_device(): query = jnp.sum(lax.all_to_all(partial, 'x', 0, 0), axis=0)]
    all_gather x2, blocking collectives: 6.4 us -> 11 us  [on_device(): lax.all_gather(gathered[at * half:(at + 1) * half], 'core')]
    all_to_all x1, starting transfers between devices: 15.7 us -> 11.4 us  [on_device(): lax.all_to_all(jnp.broadcast_to(w_query, (z_size, depth, cols)), 'z', 0, 0)]
  transfers between devices with their start and end apart: 6 -> 6, of which waited for: 2 -> 3; matrix products, arithmetic and copies ran while one was open for 5% -> 4% of each run, Pallas kernels for 0% -> 0%
where the time goes in v10:
time: 254 us; the launch traced here: 252 us
  blocking collectives  142 us (56%)
  waiting for transfers between devices  49.8 us (20%)
  starting transfers between devices  28.6 us (11%)
  between operations  16.1 us (6%)
  matrix products  5.7 us (2%)
  other arithmetic  5.5 us (2%)
  local copies, waits for them, and re-layouts  4.33 us (2%)
    psum x6, blocking collectives, tp_sum(): return lax.psum(lax.psum(value, 'core'), 'y')  50.9 us
    all_to_all x1, waiting for transfers between devices, on_device(): lax.all_to_all(jnp.broadcast_to(w_query, (z_size, depth, cols)), 'z', 0, 0)  30.1 us
    all_to_all x1, blocking collectives, on_device(): got = lax.all_to_all(sent, 'z', 0, 0)  26.2 us
    all_gather x1, blocking collectives, on_device(): out_rows = lax.all_gather(w_out, 'x')  17.9 us
    all_gather x1, blocking collectives, on_device(): attended_all = lax.all_gather(attended, TP, axis=1, tiled=True)  16.9 us
    all_to_all x1, waiting for transfers between devices, on_device(): attended = lax.all_to_all(attended, 'z', 0, 0).reshape(token_count, -1)  11.7 us
    all_to_all x1, starting transfers between devices, on_device(): lax.all_to_all(jnp.broadcast_to(w_query, (z_size, depth, cols)), 'z', 0, 0)  11.4 us
    all_gather x2, blocking collectives, on_device(): lax.all_gather(gathered[at * half:(at + 1) * half], 'core')  11 us
  transfers between devices with their start and end apart: 6, of which 3 were waited for; matrix products, arithmetic and copies ran while one was open for 4% of the time, Pallas kernels for 0%

profile of v10, /device:TPU:1, one launch (start us, length us, event | category | flops | bytes accessed | tf_op | source)
XLA Modules:
  0.0 252.2 jit_solution(8497338255307962170)
XLA Ops:
  7.2 0.0 all-gather.7.cloned.1.call-start
  7.2 1.1 fusion.5
  8.3 1.1 reduce_sum.65
  9.4 9.0 %psum.42 = f32[2,128]{1,0:T(2,128)S(1)} all-reduce(f32[2,128]{1,0:T(2,128)S(1)} %pad_maximum_fusion.2), channel_id=1, replica_groups=mesh['x'=4,'z'=16,'y'=4,'core'=2] {'core'}, use_global_device_ids=true, to_apply=%region_2.0 | all-reduce | flops 256 | bytes 2048 | tf_op jit(solution)/shard_map/psum | solution.py:22
  18.4 6.1 %psum.43 = f32[2,128]{1,0:T(2,128)S(1)} all-reduce(f32[2,128]{1,0:T(2,128)S(1)} %psum.42), channel_id=1, replica_groups=mesh['x'=4,'z'=16,'y'=4,'core'=2] {'y'}, use_global_device_ids=true, to_apply=%region_3.0 | all-reduce | flops 256 | bytes 2048 | tf_op jit(solution)/shard_map/psum | solution.py:22
  24.5 1.1 fusion.8
  25.6 0.7 collective-permute-start
  26.3 17.9 %all-gather = bf16[192,640]{1,0:T(8,128)(2,1)} all-gather(bf16[48,640]{1,0:T(8,128)(2,1)} %param.15), channel_id=2, replica_groups=mesh['x'=4,'z'=16,'y'=4,'core'=2] {'x'}, dimensions={0}, use_global_device_ids=true | all-gather | bytes 307200 | tf_op jit(solution)/shard_map/all_gather | solution.py:53
  44.1 0.0 all-gather.7.cloned.1.call-update
  44.2 1.9 broadcast_in_dim.12
  46.0 11.4 %all-to-all-start.1 = ((bf16[16,80,384]{2,1,0:T(8,128)(2,1)}), bf16[16,80,384]{2,1,0:T(8,128)(2,1)S(1)}, u32[]{:S(2)}, u32[]{:S(2)}) async-start(bf16[16,80,384]{2,1,0:T(8,128)(2,1)} %broadcast_in_dim.12), calls=%async_computation.1 | async-start | bytes 1966080 | tf_op jit(solution)/shard_map/all_to_all | solution.py:42
  57.4 10.3 %all-gather.1 = bf16[512,640]{1,0:T(8,128)(2,1)S(1)} all-gather(bf16[128,640]{1,0:T(8,128)(2,1)S(1)} %collective-permute-done), channel_id=3, replica_groups=mesh['x'=4,'z'=16,'y'=4,'core'=2] {'y'}, dimensions={0}, use_global_device_ids=true | all-gather | bytes 819200 | tf_op jit(solution)/shard_map/all_gather | solution.py:57
  67.7 0.1 fusion.19
  67.8 8.6 %all-gather.3 = bf16[4,128,640]{2,1,0:T(8,128)(2,1)S(1)} all-gather(bf16[2,128,640]{2,1,0:T(8,128)(2,1)S(1)} %bitcast.73), channel_id=5, replica_groups=mesh['x'=4,'z'=16,'y'=4,'core'=2] {'core'}, dimensions={0}, use_global_device_ids=true | all-gather | bytes 983040 | tf_op jit(solution)/shard_map/all_gather | solution.py:59
  76.4 2.4 all-gather.2
  78.8 30.1 %all-to-all-done.1 = bf16[16,80,384]{2,1,0:T(8,128)(2,1)S(1)} async-done(((bf16[16,80,384]{2,1,0:T(8,128)(2,1)}), bf16[16,80,384]{2,1,0:T(8,128)(2,1)S(1)}, u32[]{:S(2)}, u32[]{:S(2)}) %all-to-all-start.1) | async-done | bytes 983072 | tf_op jit(solution)/shard_map/all_to_all | solution.py:42
  108.8 0.5 convolution_bitcast_fusion
  109.4 0.5 convolution_bitcast_fusion.1
  109.9 0.9 pad_maximum_fusion
  110.8 3.5 %all-to-all-start.2 = ((f32[4,128,384]{2,1,0:T(8,128)}), f32[4,128,384]{2,1,0:T(8,128)S(1)}, u32[]{:S(2)}, u32[]{:S(2)}) async-start(f32[4,128,384]{2,1,0:T(8,128)} %pad_maximum_fusion), calls=%async_computation.2 | async-start | bytes 1572864 | tf_op jit(solution)/shard_map/all_to_all | solution.py:66
  114.3 0.2 copy.21
  114.5 0.2 copy.24
  114.7 7.9 %all-to-all-done.2 = f32[4,128,384]{2,1,0:T(8,128)S(1)} async-done(((f32[4,128,384]{2,1,0:T(8,128)}), f32[4,128,384]{2,1,0:T(8,128)S(1)}, u32[]{:S(2)}, u32[]{:S(2)}) %all-to-all-start.2) | async-done | bytes 786464 | tf_op jit(solution)/shard_map/all_to_all | solution.py:66
  122.7 0.1 copy.20
  122.8 0.1 multiply_reduce_fusion.1
  122.9 8.8 %psum.44 = f32[128]{0:T(128)S(1)} all-reduce(f32[128]{0:T(128)S(1)} %multiply_reduce_fusion.1), channel_id=1, replica_groups=mesh['x'=4,'z'=16,'y'=4,'core'=2] {'core'}, use_global_device_ids=true, to_apply=%region_6.0 | all-reduce | flops 128 | bytes 1024 | tf_op jit(solution)/shard_map/psum | solution.py:22
  131.7 8.3 %psum.45 = f32[128]{0:T(128)S(1)} all-reduce(f32[128]{0:T(128)S(1)} %psum.44), channel_id=1, replica_groups=mesh['x'=4,'z'=16,'y'=4,'core'=2] {'y'}, use_global_device_ids=true, to_apply=%region_7.0 | all-reduce | flops 128 | bytes 1024 | tf_op jit(solution)/shard_map/psum | solution.py:22
  140.1 0.6 fusion.20
  140.7 0.4 convolution_multiply_fusion
  141.1 0.8 fusion.3
  141.9 0.1 copy.26
  142.0 0.7 convert_element_type.42
  142.7 9.5 %all-to-all-start.3 = ((bf16[16,8,384]{2,1,0:T(8,128)(2,1)}), bf16[16,8,384]{2,1,0:T(8,128)(2,1)S(1)}, u32[]{:S(2)}, u32[]{:S(2)}) async-start(bf16[16,8,384]{2,1,0:T(8,128)(2,1)} %convert_element_type.42), calls=%async_computation.3 | async-start | bytes 196608 | tf_op jit(solution)/shard_map/all_to_all | solution.py:84
  152.2 0.1 slice.52
  152.3 0.1 divide_subtract_fusion
  152.4 0.1 dynamic_slice.3
  152.5 11.7 %all-to-all-done.3 = bf16[16,8,384]{2,1,0:T(8,128)(2,1)S(1)} async-done(((bf16[16,8,384]{2,1,0:T(8,128)(2,1)}), bf16[16,8,384]{2,1,0:T(8,128)(2,1)S(1)}, u32[]{:S(2)}, u32[]{:S(2)}) %all-to-all-start.3) | async-done | bytes 98336 | tf_op jit(solution)/shard_map/all_to_all | solution.py:84
  164.2 3.5 %all-to-all-start = ((f32[16,8,640]{2,1,0:T(8,128)}), f32[16,8,640]{2,1,0:T(8,128)S(1)}, u32[]{:S(2)}, u32[]{:S(2)}) async-start(f32[16,8,640]{2,1,0:T(8,128)} %bitcast), calls=%async_computation | async-start | bytes 655360 | tf_op jit(solution)/shard_map/all_to_all | solution.py:44
  167.8 16.9 %all_gather.45 = bf16[128,3072]{1,0:T(8,128)(2,1)S(1)} all-gather(bf16[128,384]{1,0:T(8,128)(2,1)S(1)} %bitcast.78), channel_id=1, replica_groups=mesh['x'=4,'z'=16,'y'=4,'core'=2] {'y','core'}, dimensions={1}, use_global_device_ids=true | all-gather | bytes 884736 | tf_op jit(solution)/shard_map/all_gather | solution.py:85
  184.7 2.9 %convolution_multiply_fusion.1 = f32[16,8,640]{2,1,0:T(8,128)S(1)} fusion(bf16[3072,640,1]{1,0,2:T(8,128)(2,1)} %bitcast.67, bf16[128,3072]{1,0:T(8,128)(2,1)S(1)} %all_gather.45, f32[16]{0:T(128)S(1)} %dynamic_slice.3), kind=kOutput, calls=%fused_computation.6 | convolution fusion | flops 503398400 | bytes 5046336 | tf_op jit(solution)/shard_map/dot_general | solution.py:86
  187.9 9.1 %all_gather.48 = f32[4,8,640]{2,1,0:T(8,128)S(1)} all-gather(f32[1,8,640]{2,1,0:T(8,128)S(1)} %slice_add_fusion), channel_id=1, replica_groups=mesh['x'=4,'z'=16,'y'=4,'core'=2] {'x'}, dimensions={0}, use_global_device_ids=true | all-gather | bytes 102400 | tf_op jit(solution)/shard_map/all_gather | solution.py:100
  197.1 0.2 broadcast_add_fusion
  197.3 0.1 broadcast_in_dim.13
  197.4 26.2 %all_to_all.25 = f32[16,8,768]{2,1,0:T(8,128)S(1)} all-to-all(f32[16,8,768]{2,1,0:T(8,128)S(1)} %pad_maximum_fusion.1), channel_id=1, replica_groups=mesh['x'=4,'z'=16,'y'=4,'core'=2] {'z'}, dimensions={0} | all-to-all | bytes 786432 | tf_op jit(solution)/shard_map/all_to_all | solution.py:107
  223.6 0.6 slice_reduce_fusion
  224.2 12.0 %psum.46 = f32[]{:T(128)} all-reduce(f32[]{:T(128)} %slice_reduce_fusion), channel_id=1, replica_groups=mesh['x'=4,'z'=16,'y'=4,'core'=2] {'core'}, use_global_device_ids=true, to_apply=%region_12.13 | all-reduce | flops 1 | bytes 8 | tf_op jit(solution)/shard_map/psum | solution.py:22
  236.2 6.7 %psum.47 = f32[]{:T(128)} all-reduce(f32[]{:T(128)} %psum.46), channel_id=1, replica_groups=mesh['x'=4,'z'=16,'y'=4,'core'=2] {'y'}, use_global_device_ids=true, to_apply=%region_13.14 | all-reduce | flops 1 | bytes 8 | tf_op jit(solution)/shard_map/psum | solution.py:22
  243.5 0.7 slice_bitcast_fusion
  (29 shorter events, 0.4 us)
Async XLA Ops:
  7.2 177.5 %all-gather.7.cloned.1.call-start = ((), (), s32[]{:S(2)}) async-start(), calls=%async_computation.5 | async-start | bytes 4177920 | tf_op jit(solution)/shard_map/all_gather | solution.py:56
  25.6 18.5 %collective-permute-start = (bf16[128,640]{1,0:T(8,128)(2,1)S(1)}, bf16[128,640]{1,0:T(8,128)(2,1)S(1)}, u32[]{:S(2)}, u32[]{:S(2)}) collective-permute-start(bf16[128,640]{1,0:T(8,128)(2,1)S(1)} %fusion.8), channel_id=1, source_target_pairs={{0,0},{2,128},{4,256},{6,384},{128,2},{130,130},{132,258},{134,386... | collective-permute-start | bytes 491528 | tf_op jit(solution)/shard_map/ppermute | solution.py:28
  46.0 62.8 %all-to-all-start.1 = ((bf16[16,80,384]{2,1,0:T(8,128)(2,1)}), bf16[16,80,384]{2,1,0:T(8,128)(2,1)S(1)}, u32[]{:S(2)}, u32[]{:S(2)}) async-start(bf16[16,80,384]{2,1,0:T(8,128)(2,1)} %broadcast_in_dim.12), calls=%async_computation.1 | async-start | bytes 1966080 | tf_op jit(solution)/shard_map/all_to_all | solution.py:42
  76.4 37.9 %copy-start = (bf16[512,384]{1,0:T(8,128)(2,1)S(1)}, bf16[512,384]{1,0:T(8,128)(2,1)}, u32[]{:S(2)}) copy-start(bf16[512,384]{1,0:T(8,128)(2,1)} %param.10) | copy-start | bytes 1179652
  108.8 5.7 %copy-start.1 = (bf16[512,384]{1,0:T(8,128)(2,1)S(1)}, bf16[512,384]{1,0:T(8,128)(2,1)}, u32[]{:S(2)}) copy-start(bf16[512,384]{1,0:T(8,128)(2,1)} %param.11) | copy-start | bytes 1179652
  109.3 30.7 %copy-start.2 = (f32[384]{0:T(512)S(1)}, f32[384]{0:T(512)}, u32[]{:S(2)}) copy-start(f32[384]{0:T(512)} %param.13) | copy-start | bytes 4612
  110.8 11.8 %all-to-all-start.2 = ((f32[4,128,384]{2,1,0:T(8,128)}), f32[4,128,384]{2,1,0:T(8,128)S(1)}, u32[]{:S(2)}, u32[]{:S(2)}) async-start(f32[4,128,384]{2,1,0:T(8,128)} %pad_maximum_fusion), calls=%async_computation.2 | async-start | bytes 1572864 | tf_op jit(solution)/shard_map/all_to_all | solution.py:66
  122.7 29.5 %copy-start.3 = (s32[64]{0:T(128)S(1)}, s32[64]{0:T(128)}, u32[]{:S(2)}) copy-start(s32[64]{0:T(128)} %param.9) | copy-start | bytes 772
  142.7 21.5 %all-to-all-start.3 = ((bf16[16,8,384]{2,1,0:T(8,128)(2,1)}), bf16[16,8,384]{2,1,0:T(8,128)(2,1)S(1)}, u32[]{:S(2)}, u32[]{:S(2)}) async-start(bf16[16,8,384]{2,1,0:T(8,128)(2,1)} %convert_element_type.42), calls=%async_computation.3 | async-start | bytes 196608 | tf_op jit(solution)/shard_map/all_to_all | solution.py:84
  164.2 23.7 %all-to-all-start = ((f32[16,8,640]{2,1,0:T(8,128)}), f32[16,8,640]{2,1,0:T(8,128)S(1)}, u32[]{:S(2)}, u32[]{:S(2)}) async-start(f32[16,8,640]{2,1,0:T(8,128)} %bitcast), calls=%async_computation | async-start | bytes 655360 | tf_op jit(solution)/shard_map/all_to_all | solution.py:44
Sparse Core Ops, SparseCore 0:
  44.3 107.3 all-gather.6

commit v11 on v10

--- a/solution.py
+++ b/solution.py
@@ -3,6 +3,7 @@
 import jax
 import jax.numpy as jnp
 from jax import lax
+from jax.experimental import pallas as pl
 from jax.sharding import Mesh
 from jax.sharding import PartitionSpec as P
 
@@ -26,6 +27,30 @@
     side = lax.axis_size("x")
     pairs = [(a * side + b, b * side + a) for a in range(side) for b in range(side)]
     return lax.ppermute(value, ("x", "y"), pairs)
+
+
+def attend_kernel(query, scale, gain, keys, values, attended):
+    normed = (query[...] * scale[...] * gain[...]).astype(jnp.bfloat16)
+    for head in range(normed.shape[1] // HD):
+        part = slice(head * HD, (head + 1) * HD)
+        scores = lax.dot_general(
+            normed[:, part],
+            keys[:, part],
+            (((1,), (1,)), ((), ())),
+            preferred_element_type=jnp.float32,
+        ) / math.sqrt(HD)
+        grown = jnp.exp(scores - jnp.max(scores, axis=-1, keepdims=True))
+        weights = (grown / jnp.sum(grown, axis=-1, keepdims=True)).astype(jnp.bfloat16)
+        got = jnp.dot(weights, values[:, part], preferred_element_type=jnp.float32)
+        attended[:, part] = got.astype(jnp.bfloat16)
+
+
+def attend(query, scale, gain, keys, values):
+    return pl.pallas_call(
+        attend_kernel,
+        out_shape=jax.ShapeDtypeStruct(query.shape, jnp.bfloat16),
+        cost_estimate=pl.CostEstimate(flops=20_000_000_000, bytes_accessed=2_000_000, transcendentals=0),
+    )(query, scale, gain[None], keys, values)
 
 
 def on_device(trajectory, timesteps, context_keys, context_values, ln_gain, q_gain, w_query, w_out):
@@ -67,19 +92,7 @@
     query_width = query.shape[1] * lax.axis_size(TP)
     square_sum = tp_sum(jnp.sum(query * query, axis=-1))
     query_scale = lax.rsqrt(square_sum / query_width + epsilon)[:, None]
-    q_normed = (query * query_scale * q_gain).astype(jnp.bfloat16)
-    local_heads = query.shape[1] // HD
-    q_heads = q_normed.reshape(token_count, local_heads, HD)
-    key_heads = context_keys.reshape(context_keys.shape[0], local_heads, HD)
-    value_heads = context_values.reshape(context_values.shape[0], local_heads, HD)
-    scores = jnp.einsum(
-        "thd,khd->htk", q_heads, key_heads, preferred_element_type=jnp.float32
-    ) / math.sqrt(HD)
-    soft_weights = jax.nn.softmax(scores, axis=-1).astype(jnp.bfloat16)
-    attended = jnp.einsum(
-        "htk,khd->thd", soft_weights, value_heads, preferred_element_type=jnp.float32
-    )
-    attended = attended.reshape(token_count, local_heads * HD).astype(jnp.bfloat16)
+    attended = attend(query, query_scale, q_gain, context_keys, context_values)
     attended = attended.reshape(z_size, slice_tokens, -1)
     attended = lax.all_to_all(attended, "z", 0, 0).reshape(token_count, -1)
     attended_all = lax.all_gather(attended, TP, axis=1, tiled=True)

time: 254 us -> 227 us (0.89)
  waiting for transfers between devices: 49.8 us -> 23.1 us
  blocking collectives: 142 us -> 134 us
  starting transfers between devices: 28.6 us -> 35.3 us
  Pallas kernels: 0 us -> 3.14 us
    all_to_all x1, waiting for transfers between devices: 30.1 us -> 0.01 us  [on_device(): lax.all_to_all(jnp.broadcast_to(w_query, (z_size, depth, cols)), 'z', 0, 0)]
    psum x6, blocking collectives: 50.9 us -> 43.6 us  [tp_sum(): return lax.psum(lax.psum(value, 'core'), 'y')]
    all_to_all x1, starting transfers between devices: 11.4 us -> 15.7 us  [on_device(): lax.all_to_all(jnp.broadcast_to(w_query, (z_size, depth, cols)), 'z', 0, 0)]
    all_to_all x1, waiting for transfers between devices: 7.94 us -> 11.4 us  [on_device(): query = jnp.sum(lax.all_to_all(partial, 'x', 0, 0), axis=0)]
    pallas_call x0 -> x1, Pallas kernels: none -> 3.14 us  [attend(): pl.pallas_call(attend_kernel, out_shape=jax.ShapeDtypeStruct(query.shape,...]
  transfers between devices with their start and end apart: 6 -> 6, of which waited for: 3 -> 2; matrix products, arithmetic and copies ran while one was open for 4% -> 4% of each run, Pallas kernels for 0% -> 1%
where the time goes in v11:
time: 227 us; the launch traced here: 225 us
  blocking collectives  134 us (59%)
  starting transfers between devices  35.3 us (16%)
  waiting for transfers between devices  23.1 us (10%)
  between operations  16.1 us (7%)
  other arithmetic  5.47 us (2%)
  local copies, waits for them, and re-layouts  4.34 us (2%)
  matrix products  3.9 us (2%)
  Pallas kernels  3.14 us (1%)
    psum x6, blocking collectives, tp_sum(): return lax.psum(lax.psum(value, 'core'), 'y')  43.6 us
    all_to_all x1, blocking collectives, on_device(): got = lax.all_to_all(sent, 'z', 0, 0)  26.1 us
    all_gather x1, blocking collectives, on_device(): out_rows = lax.all_gather(w_out, 'x')  17.4 us
    all_gather x1, blocking collectives, on_device(): attended_all = lax.all_gather(attended, TP, axis=1, tiled=True)  17 us
    all_to_all x1, starting transfers between devices, on_device(): lax.all_to_all(jnp.broadcast_to(w_query, (z_size, depth, cols)), 'z', 0, 0)  15.7 us
    all_to_all x1, waiting for transfers between devices, on_device(): attended = lax.all_to_all(attended, 'z', 0, 0).reshape(token_count, -1)  11.7 us
    all_gather x1, blocking collectives, on_device(): gathered = lax.all_gather(flipped, 'y')  11.6 us
    all_to_all x1, waiting for transfers between devices, on_device(): query = jnp.sum(lax.all_to_all(partial, 'x', 0, 0), axis=0)  11.4 us
  transfers between devices with their start and end apart: 6, of which 2 were waited for; matrix products, arithmetic and copies ran while one was open for 4% of the time, Pallas kernels for 1%

profile of v11, /device:TPU:1, one launch (start us, length us, event | category | flops | bytes accessed | tf_op | source)
XLA Modules:
  0.0 225.0 jit_solution(10036973007128231484)
XLA Ops:
  7.2 0.0 copy-start.1
  7.2 1.9 broadcast_in_dim.27
  9.1 15.7 %all-to-all-start.1 = ((bf16[16,80,384]{2,1,0:T(8,128)(2,1)}), bf16[16,80,384]{2,1,0:T(8,128)(2,1)S(1)}, u32[]{:S(2)}, u32[]{:S(2)}) async-start(bf16[16,80,384]{2,1,0:T(8,128)(2,1)} %broadcast_in_dim.27), calls=%async_computation.1 | async-start | bytes 1966080 | tf_op jit(solution)/shard_map/all_to_all | solution.py:67
  24.8 0.0 all-gather.7.cloned.1.call-start
  24.9 1.1 fusion.1
  26.0 1.1 reduce_sum.54
  27.1 3.1 %psum.42 = f32[2,128]{1,0:T(2,128)S(1)} all-reduce(f32[2,128]{1,0:T(2,128)S(1)} %pad_maximum_fusion.2), channel_id=1, replica_groups=mesh['x'=4,'z'=16,'y'=4,'core'=2] {'core'}, use_global_device_ids=true, to_apply=%region_2.0 | all-reduce | flops 256 | bytes 2048 | tf_op jit(solution)/shard_map/psum | solution.py:23
  30.1 9.3 %psum.43 = f32[2,128]{1,0:T(2,128)S(1)} all-reduce(f32[2,128]{1,0:T(2,128)S(1)} %psum.42), channel_id=1, replica_groups=mesh['x'=4,'z'=16,'y'=4,'core'=2] {'y'}, use_global_device_ids=true, to_apply=%region_3.0 | all-reduce | flops 256 | bytes 2048 | tf_op jit(solution)/shard_map/psum | solution.py:23
  39.4 1.1 fusion.4
  40.5 0.7 collective-permute-start
  41.2 0.0 copy-done.1
  41.2 17.4 %all-gather = bf16[192,640]{1,0:T(8,128)(2,1)} all-gather(bf16[48,640]{1,0:T(8,128)(2,1)S(1)} %copy-done.1), channel_id=2, replica_groups=mesh['x'=4,'z'=16,'y'=4,'core'=2] {'x'}, dimensions={0}, use_global_device_ids=true | all-gather | bytes 307200 | tf_op jit(solution)/shard_map/all_gather | solution.py:78
  58.7 0.0 collective-permute-done
  58.7 0.0 all-gather.7.cloned.1.call-update
  58.7 11.6 %all-gather.1 = bf16[512,640]{1,0:T(8,128)(2,1)S(1)} all-gather(bf16[128,640]{1,0:T(8,128)(2,1)S(1)} %collective-permute-done), channel_id=3, replica_groups=mesh['x'=4,'z'=16,'y'=4,'core'=2] {'y'}, dimensions={0}, use_global_device_ids=true | all-gather | bytes 819200 | tf_op jit(solution)/shard_map/all_gather | solution.py:82
  70.3 0.1 fusion.11
  70.3 6.5 %all-gather.3 = bf16[4,128,640]{2,1,0:T(8,128)(2,1)S(1)} all-gather(bf16[2,128,640]{2,1,0:T(8,128)(2,1)S(1)} %bitcast.64), channel_id=5, replica_groups=mesh['x'=4,'z'=16,'y'=4,'core'=2] {'core'}, dimensions={0}, use_global_device_ids=true | all-gather | bytes 983040 | tf_op jit(solution)/shard_map/all_gather | solution.py:84
  76.9 2.4 %all-gather.2 = bf16[4,128,640]{2,1,0:T(8,128)(2,1)S(1)} all-gather(bf16[2,128,640]{2,1,0:T(8,128)(2,1)S(1)} %bitcast.63), channel_id=4, replica_groups=mesh['x'=4,'z'=16,'y'=4,'core'=2] {'core'}, dimensions={0}, use_global_device_ids=true | all-gather | bytes 983040 | tf_op jit(solution)/shard_map/all_gather | solution.py:84
  79.2 0.0 all-to-all-done.1
  79.3 0.5 convolution_bitcast_fusion
  79.8 0.5 convolution_bitcast_fusion.1
  80.3 0.9 pad_maximum_fusion
  81.2 3.5 %all-to-all-start.2 = ((f32[4,128,384]{2,1,0:T(8,128)}), f32[4,128,384]{2,1,0:T(8,128)S(1)}, u32[]{:S(2)}, u32[]{:S(2)}) async-start(f32[4,128,384]{2,1,0:T(8,128)} %pad_maximum_fusion), calls=%async_computation.2 | async-start | bytes 1572864 | tf_op jit(solution)/shard_map/all_to_all | solution.py:91
  84.7 0.6 broadcast_in_dim.29.gain
  85.3 11.4 %all-to-all-done.2 = f32[4,128,384]{2,1,0:T(8,128)S(1)} async-done(((f32[4,128,384]{2,1,0:T(8,128)}), f32[4,128,384]{2,1,0:T(8,128)S(1)}, u32[]{:S(2)}, u32[]{:S(2)}) %all-to-all-start.2) | async-done | bytes 786464 | tf_op jit(solution)/shard_map/all_to_all | solution.py:91
  96.7 0.0 copy-start
  96.8 0.1 multiply_reduce_fusion.1
  96.9 3.3 %psum.44 = f32[128]{0:T(128)S(1)} all-reduce(f32[128]{0:T(128)S(1)} %multiply_reduce_fusion.1), channel_id=1, replica_groups=mesh['x'=4,'z'=16,'y'=4,'core'=2] {'core'}, use_global_device_ids=true, to_apply=%region_6.0 | all-reduce | flops 128 | bytes 1024 | tf_op jit(solution)/shard_map/psum | solution.py:23
  100.2 8.9 %psum.45 = f32[128]{0:T(128)S(1)} all-reduce(f32[128]{0:T(128)S(1)} %psum.44), channel_id=1, replica_groups=mesh['x'=4,'z'=16,'y'=4,'core'=2] {'y'}, use_global_device_ids=true, to_apply=%region_7.0 | all-reduce | flops 128 | bytes 1024 | tf_op jit(solution)/shard_map/psum | solution.py:23
  109.1 0.7 copy.14.scale
  109.8 3.1 %shard_map.95 = bf16[128,384]{1,0:T(8,128)(2,1)} custom-call(f32[128,384]{1,0:T(8,128)} %copy-done, f32[128,1]{1,0:T(8,128)} %copy.14.scale, f32[1,384]{1,0:T(1,128)} %broadcast_in_dim.29.gain, bf16[512,384]{1,0:T(8,128)(2,1)} %keys.1, bf16[512,384]{1,0:T(8,128)(2,1)} %values.1), custom_call_target="tpu_custom_call" | custom-call | flops 20000000000 | bytes 2000000 | tf_op jit(solution)/shard_map/pallas_call | solution.py:49
  113.0 11.3 %all-to-all-start.3 = ((bf16[16,8,384]{2,1,0:T(8,128)(2,1)}), bf16[16,8,384]{2,1,0:T(8,128)(2,1)S(1)}, u32[]{:S(2)}, u32[]{:S(2)}) async-start(bf16[16,8,384]{2,1,0:T(8,128)(2,1)} %bitcast.67), calls=%async_computation.3 | async-start | bytes 196608 | tf_op jit(solution)/shard_map/all_to_all | solution.py:97
  124.3 0.1 slice.52
  124.4 0.1 divide_subtract_fusion
  124.5 0.1 dynamic_slice.3
  124.6 11.7 %all-to-all-done.3 = bf16[16,8,384]{2,1,0:T(8,128)(2,1)S(1)} async-done(((bf16[16,8,384]{2,1,0:T(8,128)(2,1)}), bf16[16,8,384]{2,1,0:T(8,128)(2,1)S(1)}, u32[]{:S(2)}, u32[]{:S(2)}) %all-to-all-start.3) | async-done | bytes 98336 | tf_op jit(solution)/shard_map/all_to_all | solution.py:97
  136.2 4.0 %all-to-all-start = ((f32[16,8,640]{2,1,0:T(8,128)}), f32[16,8,640]{2,1,0:T(8,128)S(1)}, u32[]{:S(2)}, u32[]{:S(2)}) async-start(f32[16,8,640]{2,1,0:T(8,128)} %bitcast), calls=%async_computation | async-start | bytes 655360 | tf_op jit(solution)/shard_map/all_to_all | solution.py:69
  140.2 17.0 %all_gather.45 = bf16[128,3072]{1,0:T(8,128)(2,1)S(1)} all-gather(bf16[128,384]{1,0:T(8,128)(2,1)S(1)} %bitcast.66), channel_id=1, replica_groups=mesh['x'=4,'z'=16,'y'=4,'core'=2] {'y','core'}, dimensions={1}, use_global_device_ids=true | all-gather | bytes 884736 | tf_op jit(solution)/shard_map/all_gather | solution.py:98
  157.3 2.9 %convolution_multiply_fusion = f32[16,8,640]{2,1,0:T(8,128)S(1)} fusion(bf16[3072,640,1]{1,0,2:T(8,128)(2,1)} %bitcast.60, bf16[128,3072]{1,0:T(8,128)(2,1)S(1)} %all_gather.45, f32[16]{0:T(128)S(1)} %dynamic_slice.3), kind=kOutput, calls=%fused_computation.2 | convolution fusion | flops 503398400 | bytes 5046336 | tf_op jit(solution)/shard_map/dot_general | solution.py:99
  160.5 0.0 all-to-all-done
  160.5 9.0 %all_gather.48 = f32[4,8,640]{2,1,0:T(8,128)S(1)} all-gather(f32[1,8,640]{2,1,0:T(8,128)S(1)} %slice_add_fusion), channel_id=1, replica_groups=mesh['x'=4,'z'=16,'y'=4,'core'=2] {'x'}, dimensions={0}, use_global_device_ids=true | all-gather | bytes 102400 | tf_op jit(solution)/shard_map/all_gather | solution.py:113
  169.5 0.2 broadcast_add_fusion
  169.7 0.1 broadcast_in_dim.30
  169.8 26.1 %all_to_all.25 = f32[16,8,768]{2,1,0:T(8,128)S(1)} all-to-all(f32[16,8,768]{2,1,0:T(8,128)S(1)} %pad_maximum_fusion.1), channel_id=1, replica_groups=mesh['x'=4,'z'=16,'y'=4,'core'=2] {'z'}, dimensions={0} | all-to-all | bytes 786432 | tf_op jit(solution)/shard_map/all_to_all | solution.py:120
  196.0 0.6 slice_reduce_fusion
  196.6 12.1 %psum.46 = f32[]{:T(128)} all-reduce(f32[]{:T(128)} %slice_reduce_fusion), channel_id=1, replica_groups=mesh['x'=4,'z'=16,'y'=4,'core'=2] {'core'}, use_global_device_ids=true, to_apply=%region_10.11 | all-reduce | flops 1 | bytes 8 | tf_op jit(solution)/shard_map/psum | solution.py:23
  208.7 6.9 %psum.47 = f32[]{:T(128)} all-reduce(f32[]{:T(128)} %psum.46), channel_id=1, replica_groups=mesh['x'=4,'z'=16,'y'=4,'core'=2] {'y'}, use_global_device_ids=true, to_apply=%region_11.12 | all-reduce | flops 1 | bytes 8 | tf_op jit(solution)/shard_map/psum | solution.py:23
  216.2 0.7 slice_bitcast_fusion
  (24 shorter events, 0.4 us)
Async XLA Ops:
  7.2 34.1 %copy-start.1 = (bf16[48,640]{1,0:T(8,128)(2,1)S(1)}, bf16[48,640]{1,0:T(8,128)(2,1)}, u32[]{:S(2)}) copy-start(bf16[48,640]{1,0:T(8,128)(2,1)} %param.15) | copy-start | bytes 184324
  9.1 70.2 %all-to-all-start.1 = ((bf16[16,80,384]{2,1,0:T(8,128)(2,1)}), bf16[16,80,384]{2,1,0:T(8,128)(2,1)S(1)}, u32[]{:S(2)}, u32[]{:S(2)}) async-start(bf16[16,80,384]{2,1,0:T(8,128)(2,1)} %broadcast_in_dim.27), calls=%async_computation.1 | async-start | bytes 1966080 | tf_op jit(solution)/shard_map/all_to_all | solution.py:67
  24.8 132.4 %all-gather.7.cloned.1.call-start = ((), (), s32[]{:S(2)}) async-start(), calls=%async_computation.5 | async-start | bytes 4177920 | tf_op jit(solution)/shard_map/all_gather | solution.py:81
  40.5 18.1 %collective-permute-start = (bf16[128,640]{1,0:T(8,128)(2,1)S(1)}, bf16[128,640]{1,0:T(8,128)(2,1)S(1)}, u32[]{:S(2)}, u32[]{:S(2)}) collective-permute-start(bf16[128,640]{1,0:T(8,128)(2,1)S(1)} %fusion.4), channel_id=1, source_target_pairs={{0,0},{2,128},{4,256},{6,384},{128,2},{130,130},{132,258},{134,386... | collective-permute-start | bytes 491528 | tf_op jit(solution)/shard_map/ppermute | solution.py:29
  76.9 7.8 %copy-start.2 = (f32[384]{0:T(512)S(1)}, f32[384]{0:T(512)}, u32[]{:S(2)}) copy-start(f32[384]{0:T(512)} %param.13) | copy-start | bytes 4612
  81.2 15.5 %all-to-all-start.2 = ((f32[4,128,384]{2,1,0:T(8,128)}), f32[4,128,384]{2,1,0:T(8,128)S(1)}, u32[]{:S(2)}, u32[]{:S(2)}) async-start(f32[4,128,384]{2,1,0:T(8,128)} %pad_maximum_fusion), calls=%async_computation.2 | async-start | bytes 1572864 | tf_op jit(solution)/shard_map/all_to_all | solution.py:91
  96.7 13.1 %copy-start = (f32[128,384]{1,0:T(8,128)}, f32[128,384]{1,0:T(8,128)S(1)}, u32[]{:S(2)}) copy-start(f32[128,384]{1,0:T(8,128)S(1)} %reduce_sum.56.query) | copy-start | bytes 589828
  109.8 14.5 %copy-start.3 = (s32[64]{0:T(128)S(1)}, s32[64]{0:T(128)}, u32[]{:S(2)}) copy-start(s32[64]{0:T(128)} %param.9) | copy-start | bytes 772
  113.0 23.3 %all-to-all-start.3 = ((bf16[16,8,384]{2,1,0:T(8,128)(2,1)}), bf16[16,8,384]{2,1,0:T(8,128)(2,1)S(1)}, u32[]{:S(2)}, u32[]{:S(2)}) async-start(bf16[16,8,384]{2,1,0:T(8,128)(2,1)} %bitcast.67), calls=%async_computation.3 | async-start | bytes 196608 | tf_op jit(solution)/shard_map/all_to_all | solution.py:97
  136.2 24.2 %all-to-all-start = ((f32[16,8,640]{2,1,0:T(8,128)}), f32[16,8,640]{2,1,0:T(8,128)S(1)}, u32[]{:S(2)}, u32[]{:S(2)}) async-start(f32[16,8,640]{2,1,0:T(8,128)} %bitcast), calls=%async_computation | async-start | bytes 655360 | tf_op jit(solution)/shard_map/all_to_all | solution.py:69
Sparse Core Ops, SparseCore 0:
  58.8 74.3 all-gather.6

commit v12 on v10

--- a/solution.py
+++ b/solution.py
@@ -39,9 +39,11 @@
     slice_tokens = token_count // z_size
 
     depth, cols = w_query.shape
-    query_rows = lax.all_to_all(jnp.broadcast_to(w_query, (z_size, depth, cols)), "z", 0, 0)
+    both = jnp.concatenate([jnp.pad(w_query, ((0, 0), (0, block - cols))), w_out])
+    both = lax.all_gather(both, "z")
 
     rows_here = lax.all_to_all(latent.reshape(z_size, slice_tokens, block), "z", 0, 0)
+    latent = rows_here.reshape(token_count, block)
 
     sums = jnp.stack([jnp.sum(latent, axis=-1), jnp.sum(latent * latent, axis=-1)])
     sums = tp_sum(sums) / full_width
@@ -49,15 +51,14 @@
     row_var = row_square - row_mean * row_mean
     normed = ((latent - row_mean) * lax.rsqrt(row_var + epsilon) * ln_gain).astype(jnp.bfloat16)
 
-    w_out, normed = lax.optimization_barrier((w_out, normed))
-    out_rows = lax.all_gather(w_out, "x")
     flipped = transpose_plane(normed)
-    out_rows, flipped = lax.optimization_barrier((out_rows, flipped))
-    out_rows = lax.all_gather(out_rows, "z", axis=1).reshape(-1, block)
     gathered = lax.all_gather(flipped, "y")
     half = x_size // 2
     parts = [lax.all_gather(gathered[at * half : (at + 1) * half], "core") for at in range(2)]
-    query_weights = query_rows.reshape(2, block, cols)
+    both, parts = lax.optimization_barrier((both, parts))
+    query_weights = both[:, :depth, :cols].reshape(2, block, cols)
+    out_rows = both[:, depth:].reshape(-1, block)
+    out_rows = lax.all_gather(out_rows, "x", axis=0, tiled=True)
     partial = [
         jnp.einsum("cxtk,ckn->xtn", part, query_weights, preferred_element_type=jnp.float32)
         for part in parts
@@ -80,8 +81,6 @@
         "htk,khd->thd", soft_weights, value_heads, preferred_element_type=jnp.float32
     )
     attended = attended.reshape(token_count, local_heads * HD).astype(jnp.bfloat16)
-    attended = attended.reshape(z_size, slice_tokens, -1)
-    attended = lax.all_to_all(attended, "z", 0, 0).reshape(token_count, -1)
     attended_all = lax.all_gather(attended, TP, axis=1, tiled=True)
     velocity = jnp.dot(attended_all, out_rows, preferred_element_type=jnp.float32)
     velocity = velocity.reshape(z_size, slice_tokens, block)

time: 254 us -> 220 us (0.87)
  waiting for transfers between devices: 49.8 us -> 14 us
  blocking collectives: 142 us -> 165 us
  starting transfers between devices: 28.6 us -> 7.27 us
    all_to_all x3 -> x0, waiting for transfers between devices: 41.8 us -> none  [the longest x1 30.1 us: on_device(): lax.all_to_all(jnp.broadcast_to(w_query, (z_size, depth, cols)), 'z', 0, 0)]
    all_to_all x0 -> x1, blocking collectives: none -> 31 us  [on_device(): lax.all_to_all(latent.reshape(z_size, slice_tokens, block), 'z', 0, 0)]
    all_to_all x3 -> x0, starting transfers between devices: 24.4 us -> none  [the longest x1 11.4 us: on_device(): lax.all_to_all(jnp.broadcast_to(w_query, (z_size, depth, cols)), 'z', 0, 0)]
    all_gather x1 -> x0, blocking collectives: 17.9 us -> none  [on_device(): out_rows = lax.all_gather(w_out, 'x')]
    all_gather x1, blocking collectives: 10.3 us -> 22.3 us  [on_device(): gathered = lax.all_gather(flipped, 'y')]
    psum x6, blocking collectives: 50.9 us -> 55.7 us  [tp_sum(): return lax.psum(lax.psum(value, 'core'), 'y')]
    all_gather x1 -> x2, waiting for transfers between devices: 0.01 us -> 4.62 us  [the longest x1 4.62 us: on_device(): out_rows = lax.all_gather(out_rows, 'x', axis=0, tiled=True)]
    all_gather x2, blocking collectives: 11 us -> 6.78 us  [on_device(): lax.all_gather(gathered[at * half:(at + 1) * half], 'core')]
  transfers between devices with their start and end apart: 6 -> 4, of which waited for: 3 -> 2; matrix products, arithmetic and copies ran while one was open for 4% -> 3% of each run, Pallas kernels for 0% -> 0%
where the time goes in v12:
time: 220 us; the launch traced here: 218 us
  blocking collectives  165 us (75%)
  between operations  16.1 us (7%)
  waiting for transfers between devices  14 us (6%)
  starting transfers between devices  7.27 us (3%)
  matrix products  5.75 us (3%)
  local copies, waits for them, and re-layouts  5.4 us (2%)
  other arithmetic  4.69 us (2%)
    psum x6, blocking collectives, tp_sum(): return lax.psum(lax.psum(value, 'core'), 'y')  55.7 us
    all_to_all x1, blocking collectives, on_device(): lax.all_to_all(latent.reshape(z_size, slice_tokens, block), 'z', 0, 0)  31 us
    all_to_all x1, blocking collectives, on_device(): got = lax.all_to_all(sent, 'z', 0, 0)  25.5 us
    all_gather x1, blocking collectives, on_device(): gathered = lax.all_gather(flipped, 'y')  22.3 us
    all_gather x1, blocking collectives, on_device(): attended_all = lax.all_gather(attended, TP, axis=1, tiled=True)  14.8 us
    all_to_all x1, waiting for transfers between devices, on_device(): query = jnp.sum(lax.all_to_all(partial, 'x', 0, 0), axis=0)  9.33 us
    all_gather x1, blocking collectives, on_device(): totals = lax.all_gather(running[-1] + start, 'x')  9.01 us
    all_gather x2, blocking collectives, on_device(): lax.all_gather(gathered[at * half:(at + 1) * half], 'core')  6.78 us
  transfers between devices with their start and end apart: 4, of which 2 were waited for; matrix products, arithmetic and copies ran while one was open for 3% of the time, Pallas kernels for 0%

profile of v12, /device:TPU:1, one launch (start us, length us, event | category | flops | bytes accessed | tf_op | source)
XLA Modules:
  0.0 218.3 jit_solution(16207010083100429030)
XLA Ops:
  7.2 0.0 all-gather.9.cloned.1.call-start
  7.2 1.5 fusion.8
  8.7 0.0 all-gather.9.cloned.1.call-update
  8.8 0.0 all-gather.7.cloned.1.call-start
  8.8 31.0 %all_to_all.15 = f32[16,8,640]{2,1,0:T(8,128)S(1)} all-to-all(f32[16,8,640]{2,1,0:T(8,128)} %bitcast.74), channel_id=1, replica_groups=mesh['x'=4,'z'=16,'y'=4,'core'=2] {'z'}, dimensions={0} | all-to-all | bytes 655360 | tf_op jit(solution)/shard_map/all_to_all | solution.py:45
  39.8 0.1 fusion.19
  39.9 0.1 stack.10
  40.0 0.1 stack.9
  40.1 11.3 %psum.42 = f32[2,128]{1,0:T(2,128)S(1)} all-reduce(f32[2,128]{1,0:T(2,128)S(1)} %pad_maximum_fusion.2), channel_id=1, replica_groups=mesh['x'=4,'z'=16,'y'=4,'core'=2] {'core'}, use_global_device_ids=true, to_apply=%region_2.3 | all-reduce | flops 256 | bytes 2048 | tf_op jit(solution)/shard_map/psum | solution.py:22
  51.5 9.9 %psum.43 = f32[2,128]{1,0:T(2,128)S(1)} all-reduce(f32[2,128]{1,0:T(2,128)S(1)} %psum.42), channel_id=1, replica_groups=mesh['x'=4,'z'=16,'y'=4,'core'=2] {'y'}, use_global_device_ids=true, to_apply=%region_3.4 | all-reduce | flops 256 | bytes 2048 | tf_op jit(solution)/shard_map/psum | solution.py:22
  61.3 0.8 fusion.6
  62.1 0.7 collective-permute-start
  62.8 22.3 %all-gather.1 = bf16[512,640]{1,0:T(8,128)(2,1)S(1)} all-gather(bf16[128,640]{1,0:T(8,128)(2,1)S(1)} %collective-permute-done), channel_id=3, replica_groups=mesh['x'=4,'z'=16,'y'=4,'core'=2] {'y'}, dimensions={0}, use_global_device_ids=true | all-gather | bytes 819200 | tf_op jit(solution)/shard_map/all_gather | solution.py:55
  85.1 0.1 fusion.20
  85.2 4.5 %all-gather.2 = bf16[4,128,640]{2,1,0:T(8,128)(2,1)S(1)} all-gather(bf16[2,128,640]{2,1,0:T(8,128)(2,1)S(1)} %bitcast.70), channel_id=4, replica_groups=mesh['x'=4,'z'=16,'y'=4,'core'=2] {'core'}, dimensions={0}, use_global_device_ids=true | all-gather | bytes 983040 | tf_op jit(solution)/shard_map/all_gather | solution.py:57
  89.7 2.3 %all-gather.3 = bf16[4,128,640]{2,1,0:T(8,128)(2,1)S(1)} all-gather(bf16[2,128,640]{2,1,0:T(8,128)(2,1)S(1)} %bitcast.69), channel_id=5, replica_groups=mesh['x'=4,'z'=16,'y'=4,'core'=2] {'core'}, dimensions={0}, use_global_device_ids=true | all-gather | bytes 983040 | tf_op jit(solution)/shard_map/all_gather | solution.py:57
  92.0 2.3 %slice.64 = bf16[16,48,640]{2,1,0:T(8,128)(2,1)} slice(bf16[16,128,640]{2,1,0:T(8,128)(2,1)} %bitcast.67), slice={[0:16], [80:128], [0:640]} | slice | bytes 1966080 | tf_op jit(solution)/shard_map/slice | solution.py:60
  94.2 0.0 all-gather.7.cloned.1.call-update
  94.3 1.3 slice.63
  95.6 0.0 copy-start
  95.6 0.5 convolution_bitcast_fusion.1
  96.2 0.5 convolution_bitcast_fusion
  96.7 0.9 pad_maximum_fusion
  97.6 6.5 %all-to-all-start.1 = ((f32[4,128,384]{2,1,0:T(8,128)}), f32[4,128,384]{2,1,0:T(8,128)S(1)}, u32[]{:S(2)}, u32[]{:S(2)}) async-start(f32[4,128,384]{2,1,0:T(8,128)} %pad_maximum_fusion), calls=%async_computation.1 | async-start | bytes 1572864 | tf_op jit(solution)/shard_map/all_to_all | solution.py:67
  104.1 0.2 copy.19
  104.3 0.2 copy.22
  104.5 0.1 slice.58
  104.6 0.1 divide_subtract_fusion
  104.7 0.1 dynamic_slice.3
  104.8 9.3 %all-to-all-done.1 = f32[4,128,384]{2,1,0:T(8,128)S(1)} async-done(((f32[4,128,384]{2,1,0:T(8,128)}), f32[4,128,384]{2,1,0:T(8,128)S(1)}, u32[]{:S(2)}, u32[]{:S(2)}) %all-to-all-start.1) | async-done | bytes 786464 | tf_op jit(solution)/shard_map/all_to_all | solution.py:67
  114.1 0.1 copy.18
  114.3 0.1 multiply_reduce_fusion.2
  114.4 6.3 %psum.44 = f32[128]{0:T(128)S(1)} all-reduce(f32[128]{0:T(128)S(1)} %multiply_reduce_fusion.2), channel_id=1, replica_groups=mesh['x'=4,'z'=16,'y'=4,'core'=2] {'core'}, use_global_device_ids=true, to_apply=%region_6.7 | all-reduce | flops 128 | bytes 1024 | tf_op jit(solution)/shard_map/psum | solution.py:22
  120.6 7.0 %psum.45 = f32[128]{0:T(128)S(1)} all-reduce(f32[128]{0:T(128)S(1)} %psum.44), channel_id=1, replica_groups=mesh['x'=4,'z'=16,'y'=4,'core'=2] {'y'}, use_global_device_ids=true, to_apply=%region_7.8 | all-reduce | flops 128 | bytes 1024 | tf_op jit(solution)/shard_map/psum | solution.py:22
  127.7 0.6 fusion.21
  128.2 0.4 convolution_multiply_fusion
  128.6 0.9 convolution_convert_fusion
  129.5 14.8 %all_gather.42 = bf16[128,3072]{0,1:T(8,128)(2,1)S(1)} all-gather(bf16[128,384]{0,1:T(8,128)(2,1)S(1)} %bitcast.75), channel_id=1, replica_groups=mesh['x'=4,'z'=16,'y'=4,'core'=2] {'y','core'}, dimensions={1}, use_global_device_ids=true | all-gather | bytes 884736 | tf_op jit(solution)/shard_map/all_gather | solution.py:84
  144.3 4.6 %all-gather.7.cloned.1.call-done = bf16[3072,640]{1,0:T(8,128)(2,1)} async-done(((bf16[768,640]{1,0:T(8,128)(2,1)}), bf16[3072,640]{1,0:T(8,128)(2,1)}) %all-gather.7.cloned.1.call-update) | async-done | bytes 3932176 | tf_op jit(solution)/shard_map/all_gather | solution.py:61
  148.9 2.9 %fusion.3 = f32[16,8,640]{2,1,0:T(8,128)S(1)} fusion(bf16[128,3072]{0,1:T(8,128)(2,1)S(1)} %all_gather.42, bf16[3072,640]{1,0:T(8,128)(2,1)} %all-gather.7.cloned.1.call-done, f32[16]{0:T(128)S(1)} %dynamic_slice.3), kind=kOutput, calls=%fused_computation.7 | convolution fusion | flops 503398400 | bytes 5046336 | tf_op jit(solution)/shard_map/dot_general | solution.py:85
  152.1 9.0 %all_gather.44 = f32[4,8,640]{2,1,0:T(8,128)S(1)} all-gather(f32[1,8,640]{2,1,0:T(8,128)S(1)} %slice_add_fusion), channel_id=1, replica_groups=mesh['x'=4,'z'=16,'y'=4,'core'=2] {'x'}, dimensions={0}, use_global_device_ids=true | all-gather | bytes 102400 | tf_op jit(solution)/shard_map/all_gather | solution.py:99
  161.2 0.2 broadcast_add_fusion
  161.4 0.1 broadcast_in_dim.10
  161.5 25.5 %all_to_all.16 = f32[16,8,768]{2,1,0:T(8,128)S(1)} all-to-all(f32[16,8,768]{2,1,0:T(8,128)S(1)} %pad_maximum_fusion.1), channel_id=1, replica_groups=mesh['x'=4,'z'=16,'y'=4,'core'=2] {'z'}, dimensions={0} | all-to-all | bytes 786432 | tf_op jit(solution)/shard_map/all_to_all | solution.py:106
  187.0 0.6 slice_reduce_fusion
  187.6 12.2 %psum.46 = f32[]{:T(128)} all-reduce(f32[]{:T(128)} %slice_reduce_fusion), channel_id=1, replica_groups=mesh['x'=4,'z'=16,'y'=4,'core'=2] {'core'}, use_global_device_ids=true, to_apply=%region_12.13 | all-reduce | flops 1 | bytes 8 | tf_op jit(solution)/shard_map/psum | solution.py:22
  199.8 9.1 %psum.47 = f32[]{:T(128)} all-reduce(f32[]{:T(128)} %psum.46), channel_id=1, replica_groups=mesh['x'=4,'z'=16,'y'=4,'core'=2] {'y'}, use_global_device_ids=true, to_apply=%region_13.14 | all-reduce | flops 1 | bytes 8 | tf_op jit(solution)/shard_map/psum | solution.py:22
  209.6 0.7 slice_bitcast_fusion
  (27 shorter events, 0.4 us)
Async XLA Ops:
  7.2 84.8 %all-gather.9.cloned.1.call-start = ((), (), s32[]{:S(2)}) async-start(), calls=%async_computation.4 | async-start | bytes 2785280 | tf_op jit(solution)/shard_map/all_gather | solution.py:43
  8.8 140.1 %all-gather.7.cloned.1.call-start = ((), (), s32[]{:S(2)}) async-start(), calls=%async_computation.3 | async-start | bytes 4915200 | tf_op jit(solution)/shard_map/all_gather | solution.py:61
  62.1 0.7 collective-permute-start
  95.6 8.5 %copy-start = (bf16[512,384]{1,0:T(8,128)(2,1)S(1)}, bf16[512,384]{1,0:T(8,128)(2,1)}, u32[]{:S(2)}) copy-start(bf16[512,384]{1,0:T(8,128)(2,1)} %param.10) | copy-start | bytes 1179652
  95.6 8.7 %copy-start.1 = (bf16[512,384]{1,0:T(8,128)(2,1)S(1)}, bf16[512,384]{1,0:T(8,128)(2,1)}, u32[]{:S(2)}) copy-start(bf16[512,384]{1,0:T(8,128)(2,1)} %param.11) | copy-start | bytes 1179652
  95.6 8.9 %copy-start.3 = (s32[64]{0:T(128)S(1)}, s32[64]{0:T(128)}, u32[]{:S(2)}) copy-start(s32[64]{0:T(128)} %param.9) | copy-start | bytes 772
  96.1 31.5 %copy-start.2 = (f32[384]{0:T(512)S(1)}, f32[384]{0:T(512)}, u32[]{:S(2)}) copy-start(f32[384]{0:T(512)} %param.13) | copy-start | bytes 4612
  97.6 16.5 %all-to-all-start.1 = ((f32[4,128,384]{2,1,0:T(8,128)}), f32[4,128,384]{2,1,0:T(8,128)S(1)}, u32[]{:S(2)}, u32[]{:S(2)}) async-start(f32[4,128,384]{2,1,0:T(8,128)} %pad_maximum_fusion), calls=%async_computation.1 | async-start | bytes 1572864 | tf_op jit(solution)/shard_map/all_to_all | solution.py:67
Sparse Core Ops, SparseCore 0:
  10.7 77.4 all-gather.8
  94.4 54.4 all-gather.6

commit v13 on v8

--- a/solution.py
+++ b/solution.py
@@ -38,12 +38,12 @@
     x_here = lax.axis_index("x")
     slice_tokens = token_count // z_size
 
+    depth, cols = w_query.shape
+    both = jnp.concatenate([jnp.pad(w_query, ((0, 0), (0, block - cols))), w_out])
+    both = lax.all_gather(both, "z")
+
     rows_here = lax.all_to_all(latent.reshape(z_size, slice_tokens, block), "z", 0, 0)
-
-    depth, cols = w_query.shape
-    query_rows = lax.all_to_all(jnp.broadcast_to(w_query, (z_size, depth, cols)), "z", 0, 0)
-
-    out_rows = lax.all_gather(w_out, STEP, axis=0, tiled=True)
+    latent = rows_here.reshape(token_count, block)
 
     sums = jnp.stack([jnp.sum(latent, axis=-1), jnp.sum(latent * latent, axis=-1)])
     sums = tp_sum(sums) / full_width
@@ -55,12 +55,16 @@
     gathered = lax.all_gather(flipped, "y")
     half = x_size // 2
     parts = [lax.all_gather(gathered[at * half : (at + 1) * half], "core") for at in range(2)]
-    query_weights = query_rows.reshape(2, block, cols)
+    both, parts = lax.optimization_barrier((both, parts))
+    query_weights = both[:, :depth, :cols].reshape(2, block, cols)
     partial = [
         jnp.einsum("cxtk,ckn->xtn", part, query_weights, preferred_element_type=jnp.float32)
         for part in parts
     ]
     partial = jnp.concatenate(partial)
+    both, partial = lax.optimization_barrier((both, partial))
+    out_rows = both[:, depth:].reshape(-1, block)
+    out_rows = lax.all_gather(out_rows, "x", axis=0, tiled=True)
     query = jnp.sum(lax.all_to_all(partial, "x", 0, 0), axis=0)
     query_width = query.shape[1] * lax.axis_size(TP)
     square_sum = tp_sum(jnp.sum(query * query, axis=-1))
@@ -78,8 +82,6 @@
         "htk,khd->thd", soft_weights, value_heads, preferred_element_type=jnp.float32
     )
     attended = attended.reshape(token_count, local_heads * HD).astype(jnp.bfloat16)
-    attended = attended.reshape(z_size, slice_tokens, -1)
-    attended = lax.all_to_all(attended, "z", 0, 0).reshape(token_count, -1)
     later = jnp.concatenate([timesteps[1:], jnp.zeros((1,), timesteps.dtype)])
     step_sizes = sigma_of(later) - sigma_of(timesteps)
     step_sizes = lax.dynamic_slice_in_dim(step_sizes, x_here * z_size, z_size)[:, None, None]
@@ -107,12 +109,10 @@
         running = running + jnp.pad(running[:-reach], ((reach, 0), (0, 0), (0, 0)))
         reach *= 2
     change = start + jnp.pad(running[:-1], ((1, 0), (0, 0), (0, 0))) - rows_here
-    change_sum = jnp.sum(change * change, axis=(1, 2), keepdims=True)
-    change_sum = jnp.broadcast_to(change_sum, (z_size, slice_tokens, HD))
-    sent = jnp.concatenate([start + running, change_sum], axis=2)
-    got = lax.all_to_all(sent, "z", 0, 0)
-    new_rows = got[:, :, :block].reshape(token_count, block)
-    change_sum = tp_sum(jnp.sum(got[:, 0, block]))
+    change_sum = tp_sum(jnp.sum(change * change, axis=(1, 2)))
+    change_sum = lax.all_gather(change_sum, "z")
+    change_sum = jnp.sum(change_sum, axis=0)[lax.axis_index("z")]
+    new_rows = lax.all_to_all(start + running, "z", 0, 0).reshape(token_count, block)
     error_value = change_sum / (token_count * full_width)
     return (new_rows[None], error_value.reshape(1))
 

time: 226 us -> 221 us (0.978)
  the two profiles are of different devices: /device:TPU:1 before, /device:TPU:2 now
where the time goes in v13:
time: 221 us; the launch traced here: 220 us
  blocking collectives  150 us (68%)
  waiting for transfers between devices  22.2 us (10%)
  between operations  16.1 us (7%)
  starting transfers between devices  13.6 us (6%)
  local copies, waits for them, and re-layouts  6.53 us (3%)
  matrix products  5.88 us (3%)
  other arithmetic  5.18 us (2%)
    all_to_all x1, blocking collectives, on_device(): lax.all_to_all(latent.reshape(z_size, slice_tokens, block), 'z', 0, 0)  38.8 us
    psum x6, blocking collectives, tp_sum(): return lax.psum(lax.psum(value, 'core'), 'y')  38 us
    all_gather x1, blocking collectives, on_device(): change_sum = lax.all_gather(change_sum, 'z')  29.4 us
    all_gather x1, blocking collectives, on_device(): rows = lax.all_gather(rows, TP, axis=1, tiled=True)  14.8 us
    all_gather x1, blocking collectives, on_device(): gathered = lax.all_gather(flipped, 'y')  13 us
    all_gather x1, blocking collectives, on_device(): lax.all_gather(jnp.concatenate([weighted, rows_here[0]], axis=1), 'x')  11.8 us
    ppermute x1, waiting for transfers between devices, transpose_plane(): return lax.ppermute(value, ('x', 'y'), pairs)  9.31 us
    all_to_all x1, waiting for transfers between devices, on_device(): query = jnp.sum(lax.all_to_all(partial, 'x', 0, 0), axis=0)  9.1 us
  transfers between devices with their start and end apart: 5, of which 3 were waited for; matrix products, arithmetic and copies ran while one was open for 3% of the time, Pallas kernels for 0%

profile of v13, /device:TPU:2, one launch (start us, length us, event | category | flops | bytes accessed | tf_op | source)
XLA Modules:
  0.0 219.9 jit_solution(10620923142408357420)
XLA Ops:
  7.2 1.5 fusion.8
  8.8 38.8 %all_to_all.15 = f32[16,8,640]{2,1,0:T(8,128)S(1)} all-to-all(f32[16,8,640]{2,1,0:T(8,128)} %bitcast.90), channel_id=1, replica_groups=mesh['x'=4,'z'=16,'y'=4,'core'=2] {'z'}, dimensions={0} | all-to-all | bytes 655360 | tf_op jit(solution)/shard_map/all_to_all | solution.py:45
  47.6 0.1 fusion.22
  47.8 0.1 stack.10
  47.9 2.5 %psum.42 = f32[2,128]{1,0:T(2,128)S(1)} all-reduce(f32[2,128]{1,0:T(2,128)S(1)} %pad_maximum_fusion.3), channel_id=1, replica_groups=mesh['x'=4,'z'=16,'y'=4,'core'=2] {'core'}, use_global_device_ids=true, to_apply=%region_2.3 | all-reduce | flops 256 | bytes 2048 | tf_op jit(solution)/shard_map/psum | solution.py:22
  50.4 11.1 %psum.43 = f32[2,128]{1,0:T(2,128)S(1)} all-reduce(f32[2,128]{1,0:T(2,128)S(1)} %psum.42), channel_id=1, replica_groups=mesh['x'=4,'z'=16,'y'=4,'core'=2] {'y'}, use_global_device_ids=true, to_apply=%region_3.4 | all-reduce | flops 256 | bytes 2048 | tf_op jit(solution)/shard_map/psum | solution.py:22
  61.5 0.8 fusion.6
  62.3 1.9 collective-permute-start
  64.2 9.3 %collective-permute-done = bf16[128,640]{1,0:T(8,128)(2,1)S(1)} collective-permute-done((bf16[128,640]{1,0:T(8,128)(2,1)S(1)}, bf16[128,640]{1,0:T(8,128)(2,1)S(1)}, u32[]{:S(2)}, u32[]{:S(2)}) %collective-permute-start) | collective-permute-done | bytes 163872 | tf_op jit(solution)/shard_map/ppermute | solution.py:28
  73.5 13.0 %all-gather.1 = bf16[512,640]{1,0:T(8,128)(2,1)S(1)} all-gather(bf16[128,640]{1,0:T(8,128)(2,1)S(1)} %collective-permute-done), channel_id=3, replica_groups=mesh['x'=4,'z'=16,'y'=4,'core'=2] {'y'}, dimensions={0}, use_global_device_ids=true | all-gather | bytes 819200 | tf_op jit(solution)/shard_map/all_gather | solution.py:55
  86.6 2.3 %all-gather.2 = bf16[4,128,640]{2,1,0:T(8,128)(2,1)S(1)} all-gather(bf16[2,128,640]{2,1,0:T(8,128)(2,1)S(1)} %bitcast.86), channel_id=4, replica_groups=mesh['x'=4,'z'=16,'y'=4,'core'=2] {'core'}, dimensions={0}, use_global_device_ids=true | all-gather | bytes 983040 | tf_op jit(solution)/shard_map/all_gather | solution.py:57
  88.9 2.3 %all-gather.3 = bf16[4,128,640]{2,1,0:T(8,128)(2,1)S(1)} all-gather(bf16[2,128,640]{2,1,0:T(8,128)(2,1)S(1)} %bitcast.85), channel_id=5, replica_groups=mesh['x'=4,'z'=16,'y'=4,'core'=2] {'core'}, dimensions={0}, use_global_device_ids=true | all-gather | bytes 983040 | tf_op jit(solution)/shard_map/all_gather | solution.py:57
  91.1 3.8 %all-gather.11.cloned.1.call-done = bf16[2048,640]{1,0:T(8,128)(2,1)} async-done(((bf16[128,640]{1,0:T(8,128)(2,1)}), bf16[2048,640]{1,0:T(8,128)(2,1)}) %all-gather.11.cloned.1.call-update) | async-done | bytes 2621456 | tf_op jit(solution)/shard_map/all_gather | solution.py:43
  94.9 1.3 slice.70
  96.2 0.5 convolution_bitcast_fusion
  96.7 0.5 convolution_bitcast_fusion.1
  97.2 1.0 pad_maximum_fusion
  98.2 2.3 %slice.76 = bf16[16,48,640]{2,1,0:T(8,128)(2,1)} slice(bf16[16,128,640]{2,1,0:T(8,128)(2,1)} %bitcast.83), slice={[0:16], [80:128], [0:640]} | slice | bytes 1966080 | tf_op jit(solution)/shard_map/slice | solution.py:66
  100.6 4.7 %all-to-all-start.1 = ((f32[4,128,384]{2,1,0:T(8,128)}), f32[4,128,384]{2,1,0:T(8,128)S(1)}, u32[]{:S(2)}, u32[]{:S(2)}) async-start(f32[4,128,384]{2,1,0:T(8,128)} %pad_maximum_fusion), calls=%async_computation.1 | async-start | bytes 1572864 | tf_op jit(solution)/shard_map/all_to_all | solution.py:68
  105.3 0.2 copy.24
  105.5 0.2 copy.27
  105.9 9.1 %all-to-all-done.1 = f32[4,128,384]{2,1,0:T(8,128)S(1)} async-done(((f32[4,128,384]{2,1,0:T(8,128)}), f32[4,128,384]{2,1,0:T(8,128)S(1)}, u32[]{:S(2)}, u32[]{:S(2)}) %all-to-all-start.1) | async-done | bytes 786464 | tf_op jit(solution)/shard_map/all_to_all | solution.py:68
  115.0 0.1 copy.23
  115.2 0.1 multiply_reduce_fusion.3
  115.3 2.5 %psum.44 = f32[128]{0:T(128)S(1)} all-reduce(f32[128]{0:T(128)S(1)} %multiply_reduce_fusion.3), channel_id=1, replica_groups=mesh['x'=4,'z'=16,'y'=4,'core'=2] {'core'}, use_global_device_ids=true, to_apply=%region_6.7 | all-reduce | flops 128 | bytes 1024 | tf_op jit(solution)/shard_map/psum | solution.py:22
  117.8 9.1 %psum.45 = f32[128]{0:T(128)S(1)} all-reduce(f32[128]{0:T(128)S(1)} %psum.44), channel_id=1, replica_groups=mesh['x'=4,'z'=16,'y'=4,'core'=2] {'y'}, use_global_device_ids=true, to_apply=%region_7.8 | all-reduce | flops 128 | bytes 1024 | tf_op jit(solution)/shard_map/psum | solution.py:22
  126.9 0.6 fusion.25
  127.4 0.4 convolution_multiply_fusion
  127.8 0.9 bitcast_convert_fusion
  128.7 0.1 copy.28
  128.9 0.1 reshape.99
  129.0 0.1 multiply_reduce_fusion.2
  129.1 11.8 %all-gather.4 = f32[32,1024]{1,0:T(8,128)S(1)} all-gather(f32[8,1024]{1,0:T(8,128)S(1)} %pad_maximum_fusion.2), channel_id=6, replica_groups=mesh['x'=4,'z'=16,'y'=4,'core'=2] {'x'}, dimensions={0}, use_global_device_ids=true | all-gather | bytes 163840 | tf_op jit(solution)/shard_map/all_gather | solution.py:91
  140.9 0.2 copy.30
  141.1 0.2 copy.29
  141.2 0.1 pad_maximum_fusion.1
  141.4 14.8 %all_gather.52 = bf16[144,3072]{0,1:T(8,128)(2,1)S(1)} all-gather(bf16[144,384]{0,1:T(8,128)(2,1)S(1)} %pad_maximum_fusion.1), channel_id=1, replica_groups=mesh['x'=4,'z'=16,'y'=4,'core'=2] {'y','core'}, dimensions={1}, use_global_device_ids=true | all-gather | bytes 995328 | tf_op jit(solution)/shard_map/all_gather | solution.py:99
  156.2 3.0 %fusion.26 = f32[144,640]{1,0:T(8,128)S(1)} fusion(bf16[144,3072]{0,1:T(8,128)(2,1)S(1)} %all_gather.52, bf16[3072,640]{1,0:T(8,128)(2,1)} %all-gather.9.cloned.1.call-done), kind=kOutput, calls=%fused_computation.61 | convolution fusion | flops 566231040 | bytes 5185536 | tf_op jit(solution)/shard_map/dot_general | solution.py:100
  159.2 0.1 fusion.3
  159.4 0.1 pad_add_fusion.3
  159.6 0.8 broadcast_add_fusion
  160.4 6.9 %all-to-all-start.2 = ((f32[16,8,640]{2,1,0:T(8,128)}), f32[16,8,640]{2,1,0:T(8,128)S(1)}, u32[]{:S(2)}, u32[]{:S(2)}) async-start(f32[16,8,640]{2,1,0:T(8,128)} %get-tuple-element.14), calls=%async_computation.2 | async-start | bytes 655360 | tf_op jit(solution)/shard_map/all_to_all | solution.py:115
  167.4 0.2 multiply_reduce_fusion
  167.6 2.4 %psum.46 = f32[16]{0:T(128)S(1)} all-reduce(f32[16]{0:T(128)S(1)} %multiply_reduce_fusion), channel_id=1, replica_groups=mesh['x'=4,'z'=16,'y'=4,'core'=2] {'core'}, use_global_device_ids=true, to_apply=%region_12.13 | all-reduce | flops 16 | bytes 128 | tf_op jit(solution)/shard_map/psum | solution.py:22
  170.0 10.4 %psum.47 = f32[1,16]{1,0:T(1,128)S(1)} all-reduce(f32[1,16]{1,0:T(1,128)S(1)} %bitcast.97), channel_id=1, replica_groups=mesh['x'=4,'z'=16,'y'=4,'core'=2] {'y'}, use_global_device_ids=true, to_apply=%region_13.14 | all-reduce | flops 16 | bytes 128 | tf_op jit(solution)/shard_map/psum | solution.py:22
  180.5 29.4 %all-gather.5 = f32[16,1,16]{2,1,0:T(1,128)S(1)} all-gather(f32[1,1,16]{2,1,0:T(1,128)S(1)} %bitcast.96), channel_id=1, replica_groups=mesh['x'=4,'z'=16,'y'=4,'core'=2] {'z'}, dimensions={0}, use_global_device_ids=true | all-gather | bytes 1088 | tf_op jit(solution)/shard_map/all_gather | solution.py:113
  209.9 0.6 dynamic_slice.7
  211.2 0.7 copy.35
  (38 shorter events, 0.8 us)
Async XLA Ops:
  7.2 87.7 %all-gather.11.cloned.1.call-start = ((), (), s32[]{:S(2)}) async-start(), calls=%async_computation.4 | async-start | bytes 2785280 | tf_op jit(solution)/shard_map/all_gather | solution.py:43
  8.8 147.4 %all-gather.9.cloned.1.call-start = ((), (), s32[]{:S(2)}) async-start(), calls=%async_computation.3 | async-start | bytes 4915200 | tf_op jit(solution)/shard_map/all_gather | solution.py:67
  62.3 11.2 %collective-permute-start = (bf16[128,640]{1,0:T(8,128)(2,1)S(1)}, bf16[128,640]{1,0:T(8,128)(2,1)S(1)}, u32[]{:S(2)}, u32[]{:S(2)}) collective-permute-start(bf16[128,640]{1,0:T(8,128)(2,1)S(1)} %fusion.6), channel_id=1, source_target_pairs={{0,0},{2,128},{4,256},{6,384},{128,2},{130,130},{132,258},{134,386... | collective-permute-start | bytes 491528 | tf_op jit(solution)/shard_map/ppermute | solution.py:28
  98.2 7.1 %copy-start.3 = (s32[64]{0:T(128)S(1)}, s32[64]{0:T(128)}, u32[]{:S(2)}) copy-start(s32[64]{0:T(128)} %param.9) | copy-start | bytes 772
  98.2 7.1 %copy-start = (bf16[512,384]{1,0:T(8,128)(2,1)S(1)}, bf16[512,384]{1,0:T(8,128)(2,1)}, u32[]{:S(2)}) copy-start(bf16[512,384]{1,0:T(8,128)(2,1)} %param.10) | copy-start | bytes 1179652
  98.2 7.3 %copy-start.1 = (bf16[512,384]{1,0:T(8,128)(2,1)S(1)}, bf16[512,384]{1,0:T(8,128)(2,1)}, u32[]{:S(2)}) copy-start(bf16[512,384]{1,0:T(8,128)(2,1)} %param.11) | copy-start | bytes 1179652
  100.6 26.3 %copy-start.2 = (f32[384]{0:T(512)S(1)}, f32[384]{0:T(512)}, u32[]{:S(2)}) copy-start(f32[384]{0:T(512)} %param.13) | copy-start | bytes 4612
  100.6 14.4 %all-to-all-start.1 = ((f32[4,128,384]{2,1,0:T(8,128)}), f32[4,128,384]{2,1,0:T(8,128)S(1)}, u32[]{:S(2)}, u32[]{:S(2)}) async-start(f32[4,128,384]{2,1,0:T(8,128)} %pad_maximum_fusion), calls=%async_computation.1 | async-start | bytes 1572864 | tf_op jit(solution)/shard_map/all_to_all | solution.py:68
  160.4 50.7 %all-to-all-start.2 = ((f32[16,8,640]{2,1,0:T(8,128)}), f32[16,8,640]{2,1,0:T(8,128)S(1)}, u32[]{:S(2)}, u32[]{:S(2)}) async-start(f32[16,8,640]{2,1,0:T(8,128)} %get-tuple-element.14), calls=%async_computation.2 | async-start | bytes 655360 | tf_op jit(solution)/shard_map/all_to_all | solution.py:115
Sparse Core Ops, SparseCore 0:
  10.7 84.2 all-gather.10
  100.7 50.0 all-gather.8

commit v14 on v13

--- a/solution.py
+++ b/solution.py
@@ -110,9 +110,10 @@
         reach *= 2
     change = start + jnp.pad(running[:-1], ((1, 0), (0, 0), (0, 0))) - rows_here
     change_sum = tp_sum(jnp.sum(change * change, axis=(1, 2)))
-    change_sum = lax.all_gather(change_sum, "z")
-    change_sum = jnp.sum(change_sum, axis=0)[lax.axis_index("z")]
     new_rows = lax.all_to_all(start + running, "z", 0, 0).reshape(token_count, block)
+    change_sum, new_rows = lax.optimization_barrier((change_sum, new_rows))
+    change_sum = jnp.broadcast_to(change_sum[:, None, None], (z_size, 1, HD))
+    change_sum = jnp.sum(lax.all_to_all(change_sum, "z", 0, 0)[:, 0, 0])
     error_value = change_sum / (token_count * full_width)
     return (new_rows[None], error_value.reshape(1))
 

time: 221 us -> 219 us (level)
  the two profiles are of different devices: /device:TPU:2 before, /device:TPU:1 now
where the time goes in v14:
time: 219 us
  blocking collectives  134 us (61%)
  starting transfers between devices  25.3 us (12%)
  waiting for transfers between devices  24.9 us (11%)
  between operations  16.1 us (7%)
  local copies, waits for them, and re-layouts  6.62 us (3%)
  matrix products  5.87 us (3%)
  other arithmetic  5.76 us (3%)
    psum x6, blocking collectives, tp_sum(): return lax.psum(lax.psum(value, 'core'), 'y')  45.4 us
    all_to_all x1, blocking collectives, on_device(): lax.all_to_all(latent.reshape(z_size, slice_tokens, block), 'z', 0, 0)  31 us
    all_gather x1, blocking collectives, on_device(): gathered = lax.all_gather(flipped, 'y')  22.3 us
    all_gather x1, blocking collectives, on_device(): rows = lax.all_gather(rows, TP, axis=1, tiled=True)  17.8 us
    all_to_all x1, starting transfers between devices, on_device(): change_sum = jnp.sum(lax.all_to_all(change_sum, 'z', 0, 0)[:, 0, 0])  11.6 us
    all_to_all x1, waiting for transfers between devices, on_device(): change_sum = jnp.sum(lax.all_to_all(change_sum, 'z', 0, 0)[:, 0, 0])  11.2 us
    all_gather x1, blocking collectives, on_device(): lax.all_gather(jnp.concatenate([weighted, rows_here[0]], axis=1), 'x')  10.7 us
    all_to_all x1, waiting for transfers between devices, on_device(): query = jnp.sum(lax.all_to_all(partial, 'x', 0, 0), axis=0)  9.34 us
  transfers between devices with their start and end apart: 6, of which 3 were waited for; matrix products, arithmetic and copies ran while one was open for 2% of the time, Pallas kernels for 0%

profile of v14, /device:TPU:1, one launch (start us, length us, event | category | flops | bytes accessed | tf_op | source)
XLA Modules:
  0.0 218.7 jit_solution(937745826374985325)
XLA Ops:
  7.2 1.5 fusion.8
  8.8 31.0 %all_to_all.20 = f32[16,8,640]{2,1,0:T(8,128)S(1)} all-to-all(f32[16,8,640]{2,1,0:T(8,128)} %bitcast.90), channel_id=1, replica_groups=mesh['x'=4,'z'=16,'y'=4,'core'=2] {'z'}, dimensions={0} | all-to-all | bytes 655360 | tf_op jit(solution)/shard_map/all_to_all | solution.py:45
  39.8 0.1 fusion.22
  40.0 0.1 stack.10
  40.1 11.3 %psum.42 = f32[2,128]{1,0:T(2,128)S(1)} all-reduce(f32[2,128]{1,0:T(2,128)S(1)} %pad_maximum_fusion.3), channel_id=1, replica_groups=mesh['x'=4,'z'=16,'y'=4,'core'=2] {'core'}, use_global_device_ids=true, to_apply=%region_2.3 | all-reduce | flops 256 | bytes 2048 | tf_op jit(solution)/shard_map/psum | solution.py:22
  51.5 9.9 %psum.43 = f32[2,128]{1,0:T(2,128)S(1)} all-reduce(f32[2,128]{1,0:T(2,128)S(1)} %psum.42), channel_id=1, replica_groups=mesh['x'=4,'z'=16,'y'=4,'core'=2] {'y'}, use_global_device_ids=true, to_apply=%region_3.4 | all-reduce | flops 256 | bytes 2048 | tf_op jit(solution)/shard_map/psum | solution.py:22
  61.3 0.8 fusion.6
  62.1 0.7 collective-permute-start
  62.8 22.3 %all-gather.1 = bf16[512,640]{1,0:T(8,128)(2,1)S(1)} all-gather(bf16[128,640]{1,0:T(8,128)(2,1)S(1)} %collective-permute-done), channel_id=3, replica_groups=mesh['x'=4,'z'=16,'y'=4,'core'=2] {'y'}, dimensions={0}, use_global_device_ids=true | all-gather | bytes 819200 | tf_op jit(solution)/shard_map/all_gather | solution.py:55
  85.2 4.5 %all-gather.2 = bf16[4,128,640]{2,1,0:T(8,128)(2,1)S(1)} all-gather(bf16[2,128,640]{2,1,0:T(8,128)(2,1)S(1)} %bitcast.86), channel_id=4, replica_groups=mesh['x'=4,'z'=16,'y'=4,'core'=2] {'core'}, dimensions={0}, use_global_device_ids=true | all-gather | bytes 983040 | tf_op jit(solution)/shard_map/all_gather | solution.py:57
  89.7 2.3 %all-gather.3 = bf16[4,128,640]{2,1,0:T(8,128)(2,1)S(1)} all-gather(bf16[2,128,640]{2,1,0:T(8,128)(2,1)S(1)} %bitcast.85), channel_id=5, replica_groups=mesh['x'=4,'z'=16,'y'=4,'core'=2] {'core'}, dimensions={0}, use_global_device_ids=true | all-gather | bytes 983040 | tf_op jit(solution)/shard_map/all_gather | solution.py:57
  92.0 1.3 slice.73
  93.3 0.5 convolution_bitcast_fusion
  93.8 0.5 convolution_bitcast_fusion.1
  94.3 1.0 pad_maximum_fusion
  95.3 2.3 %slice.79 = bf16[16,48,640]{2,1,0:T(8,128)(2,1)} slice(bf16[16,128,640]{2,1,0:T(8,128)(2,1)} %bitcast.83), slice={[0:16], [80:128], [0:640]} | slice | bytes 1966080 | tf_op jit(solution)/shard_map/slice | solution.py:66
  97.7 6.5 %all-to-all-start.1 = ((f32[4,128,384]{2,1,0:T(8,128)}), f32[4,128,384]{2,1,0:T(8,128)S(1)}, u32[]{:S(2)}, u32[]{:S(2)}) async-start(f32[4,128,384]{2,1,0:T(8,128)} %pad_maximum_fusion), calls=%async_computation.1 | async-start | bytes 1572864 | tf_op jit(solution)/shard_map/all_to_all | solution.py:68
  104.3 0.2 copy.40
  104.5 0.2 copy.43
  104.8 9.3 %all-to-all-done.1 = f32[4,128,384]{2,1,0:T(8,128)S(1)} async-done(((f32[4,128,384]{2,1,0:T(8,128)}), f32[4,128,384]{2,1,0:T(8,128)S(1)}, u32[]{:S(2)}, u32[]{:S(2)}) %all-to-all-start.1) | async-done | bytes 786464 | tf_op jit(solution)/shard_map/all_to_all | solution.py:68
  114.2 0.1 copy.39
  114.3 0.1 multiply_reduce_fusion.3
  114.4 5.4 %psum.44 = f32[128]{0:T(128)S(1)} all-reduce(f32[128]{0:T(128)S(1)} %multiply_reduce_fusion.3), channel_id=1, replica_groups=mesh['x'=4,'z'=16,'y'=4,'core'=2] {'core'}, use_global_device_ids=true, to_apply=%region_6.7 | all-reduce | flops 128 | bytes 1024 | tf_op jit(solution)/shard_map/psum | solution.py:22
  119.8 7.9 %psum.45 = f32[128]{0:T(128)S(1)} all-reduce(f32[128]{0:T(128)S(1)} %psum.44), channel_id=1, replica_groups=mesh['x'=4,'z'=16,'y'=4,'core'=2] {'y'}, use_global_device_ids=true, to_apply=%region_7.8 | all-reduce | flops 128 | bytes 1024 | tf_op jit(solution)/shard_map/psum | solution.py:22
  127.7 0.6 fusion.25
  128.3 0.4 convolution_multiply_fusion
  128.7 0.9 bitcast_convert_fusion
  129.6 0.1 copy.44
  129.7 0.1 reshape.106
  129.9 10.7 %all-gather.4 = f32[32,1024]{1,0:T(8,128)S(1)} all-gather(f32[8,1024]{1,0:T(8,128)S(1)} %pad_maximum_fusion.2), channel_id=6, replica_groups=mesh['x'=4,'z'=16,'y'=4,'core'=2] {'x'}, dimensions={0}, use_global_device_ids=true | all-gather | bytes 163840 | tf_op jit(solution)/shard_map/all_gather | solution.py:91
  140.7 0.2 copy.46
  140.9 0.2 copy.45
  141.0 0.1 pad_maximum_fusion.1
  141.1 17.8 %all_gather.46 = bf16[144,3072]{0,1:T(8,128)(2,1)S(1)} all-gather(bf16[144,384]{0,1:T(8,128)(2,1)S(1)} %pad_maximum_fusion.1), channel_id=1, replica_groups=mesh['x'=4,'z'=16,'y'=4,'core'=2] {'y','core'}, dimensions={1}, use_global_device_ids=true | all-gather | bytes 995328 | tf_op jit(solution)/shard_map/all_gather | solution.py:99
  159.0 3.0 %fusion.26 = f32[144,640]{1,0:T(8,128)S(1)} fusion(bf16[144,3072]{0,1:T(8,128)(2,1)S(1)} %all_gather.46, bf16[3072,640]{1,0:T(8,128)(2,1)} %all-gather.8.cloned.1.call-done), kind=kOutput, calls=%fused_computation.62 | convolution fusion | flops 566231040 | bytes 5185536 | tf_op jit(solution)/shard_map/dot_general | solution.py:100
  162.1 0.1 fusion.3
  162.2 0.1 pad_add_fusion.3
  162.5 0.8 broadcast_add_fusion
  163.2 6.4 %all-to-all-start.2 = ((f32[16,8,640]{2,1,0:T(8,128)}), f32[16,8,640]{2,1,0:T(8,128)S(1)}, u32[]{:S(2)}, u32[]{:S(2)}) async-start(f32[16,8,640]{2,1,0:T(8,128)} %get-tuple-element.18), calls=%async_computation.2 | async-start | bytes 655360 | tf_op jit(solution)/shard_map/all_to_all | solution.py:113
  169.7 0.2 multiply_reduce_fusion
  169.9 2.5 %psum.46 = f32[16]{0:T(128)S(1)} all-reduce(f32[16]{0:T(128)S(1)} %multiply_reduce_fusion), channel_id=1, replica_groups=mesh['x'=4,'z'=16,'y'=4,'core'=2] {'core'}, use_global_device_ids=true, to_apply=%region_12.13 | all-reduce | flops 16 | bytes 128 | tf_op jit(solution)/shard_map/psum | solution.py:22
  172.4 8.4 %psum.47 = f32[16]{0:T(128)S(1)} all-reduce(f32[16]{0:T(128)S(1)} %psum.46), channel_id=1, replica_groups=mesh['x'=4,'z'=16,'y'=4,'core'=2] {'y'}, use_global_device_ids=true, to_apply=%region_13.14 | all-reduce | flops 16 | bytes 128 | tf_op jit(solution)/shard_map/psum | solution.py:22
  180.9 4.3 %all-to-all-done.2 = f32[16,8,640]{2,1,0:T(8,128)S(1)} async-done(((f32[16,8,640]{2,1,0:T(8,128)}), f32[16,8,640]{2,1,0:T(8,128)S(1)}, u32[]{:S(2)}, u32[]{:S(2)}) %all-to-all-start.2) | async-done | bytes 327712 | tf_op jit(solution)/shard_map/all_to_all | solution.py:113
  185.2 0.7 broadcast_in_dim.12
  185.9 11.6 %all-to-all-start.3 = ((f32[16,1,128]{2,1,0:T(1,128)}), f32[16,1,128]{2,1,0:T(1,128)S(1)}, u32[]{:S(2)}, u32[]{:S(2)}) async-start(f32[16,1,128]{2,1,0:T(1,128)} %broadcast_in_dim.12), calls=%async_computation.3 | async-start | bytes 16384 | tf_op jit(solution)/shard_map/all_to_all | solution.py:116
  197.5 11.2 %all-to-all-done.3 = f32[16,1,128]{2,1,0:T(1,128)S(1)} async-done(((f32[16,1,128]{2,1,0:T(1,128)}), f32[16,1,128]{2,1,0:T(1,128)S(1)}, u32[]{:S(2)}, u32[]{:S(2)}) %all-to-all-start.3) | async-done | bytes 8224 | tf_op jit(solution)/shard_map/all_to_all | solution.py:116
  208.7 0.6 slice_reduce_fusion
  210.0 0.7 copy.53
  (39 shorter events, 0.9 us)
Async XLA Ops:
  7.2 84.8 %all-gather.10.cloned.1.call-start = ((), (), s32[]{:S(2)}) async-start(), calls=%async_computation.5 | async-start | bytes 2785280 | tf_op jit(solution)/shard_map/all_gather | solution.py:43
  8.8 150.2 %all-gather.8.cloned.1.call-start = ((), (), s32[]{:S(2)}) async-start(), calls=%async_computation.4 | async-start | bytes 4915200 | tf_op jit(solution)/shard_map/all_gather | solution.py:67
  62.1 0.7 collective-permute-start
  95.3 8.9 %copy-start.3 = (s32[64]{0:T(128)S(1)}, s32[64]{0:T(128)}, u32[]{:S(2)}) copy-start(s32[64]{0:T(128)} %param.9) | copy-start | bytes 772
  95.3 9.0 %copy-start = (bf16[512,384]{1,0:T(8,128)(2,1)S(1)}, bf16[512,384]{1,0:T(8,128)(2,1)}, u32[]{:S(2)}) copy-start(bf16[512,384]{1,0:T(8,128)(2,1)} %param.10) | copy-start | bytes 1179652
  95.3 9.2 %copy-start.1 = (bf16[512,384]{1,0:T(8,128)(2,1)S(1)}, bf16[512,384]{1,0:T(8,128)(2,1)}, u32[]{:S(2)}) copy-start(bf16[512,384]{1,0:T(8,128)(2,1)} %param.11) | copy-start | bytes 1179652
  97.6 30.1 %copy-start.2 = (f32[384]{0:T(512)S(1)}, f32[384]{0:T(512)}, u32[]{:S(2)}) copy-start(f32[384]{0:T(512)} %param.13) | copy-start | bytes 4612
  97.7 16.5 %all-to-all-start.1 = ((f32[4,128,384]{2,1,0:T(8,128)}), f32[4,128,384]{2,1,0:T(8,128)S(1)}, u32[]{:S(2)}, u32[]{:S(2)}) async-start(f32[4,128,384]{2,1,0:T(8,128)} %pad_maximum_fusion), calls=%async_computation.1 | async-start | bytes 1572864 | tf_op jit(solution)/shard_map/all_to_all | solution.py:68
  163.2 22.0 %all-to-all-start.2 = ((f32[16,8,640]{2,1,0:T(8,128)}), f32[16,8,640]{2,1,0:T(8,128)S(1)}, u32[]{:S(2)}, u32[]{:S(2)}) async-start(f32[16,8,640]{2,1,0:T(8,128)} %get-tuple-element.18), calls=%async_computation.2 | async-start | bytes 655360 | tf_op jit(solution)/shard_map/all_to_all | solution.py:113
  185.9 22.8 %all-to-all-start.3 = ((f32[16,1,128]{2,1,0:T(1,128)}), f32[16,1,128]{2,1,0:T(1,128)S(1)}, u32[]{:S(2)}, u32[]{:S(2)}) async-start(f32[16,1,128]{2,1,0:T(1,128)} %broadcast_in_dim.12), calls=%async_computation.3 | async-start | bytes 16384 | tf_op jit(solution)/shard_map/all_to_all | solution.py:116
Sparse Core Ops, SparseCore 0:
  10.7 77.4 all-gather.9
  97.8 54.4 all-gather.7

commit v15 on v13

--- a/solution.py
+++ b/solution.py
@@ -3,6 +3,7 @@
 import jax
 import jax.numpy as jnp
 from jax import lax
+from jax.experimental import pallas as pl
 from jax.sharding import Mesh
 from jax.sharding import PartitionSpec as P
 
@@ -26,6 +27,22 @@
     side = lax.axis_size("x")
     pairs = [(a * side + b, b * side + a) for a in range(side) for b in range(side)]
     return lax.ppermute(value, ("x", "y"), pairs)
+
+
+def side_kernel(sizes, attended, first, side):
+    rows, width = first.shape[0], attended.shape[1]
+    weighted = sizes[...] * attended[...].astype(jnp.float32)
+    side[:, :width] = jnp.sum(weighted.reshape(-1, rows, width), axis=0)
+    side[:, width:] = first[...]
+
+
+def weighted_side(sizes, attended, first):
+    shape = (first.shape[0], attended.shape[1] + first.shape[1])
+    return pl.pallas_call(
+        side_kernel,
+        out_shape=jax.ShapeDtypeStruct(shape, jnp.float32),
+        cost_estimate=pl.CostEstimate(flops=50_000_000_000, bytes_accessed=1_000_000, transcendentals=0),
+    )(sizes, attended, first)
 
 
 def on_device(trajectory, timesteps, context_keys, context_values, ln_gain, q_gain, w_query, w_out):
@@ -86,10 +103,10 @@
     step_sizes = sigma_of(later) - sigma_of(timesteps)
     step_sizes = lax.dynamic_slice_in_dim(step_sizes, x_here * z_size, z_size)[:, None, None]
 
-    weighted = jnp.sum(step_sizes * attended.reshape(z_size, slice_tokens, -1), axis=0)
-    width = weighted.shape[1]
-    sides = lax.all_gather(jnp.concatenate([weighted, rows_here[0]], axis=1), "x")
-    weighted = jnp.zeros_like(weighted)
+    width = attended.shape[1]
+    row_sizes = jnp.broadcast_to(step_sizes, (z_size, slice_tokens, 1)).reshape(token_count, 1)
+    sides = lax.all_gather(weighted_side(row_sizes, attended, rows_here[0]), "x")
+    weighted = jnp.zeros((slice_tokens, width), jnp.float32)
     for at in range(x_size - 1):
         weighted = weighted + jnp.where(at < x_here, sides[at, :, :width], 0.0)
     high = lax.reduce_precision(weighted, 8, 7)
@@ -109,10 +126,12 @@
         running = running + jnp.pad(running[:-reach], ((reach, 0), (0, 0), (0, 0)))
         reach *= 2
     change = start + jnp.pad(running[:-1], ((1, 0), (0, 0), (0, 0))) - rows_here
-    change_sum = tp_sum(jnp.sum(change * change, axis=(1, 2)))
-    change_sum = lax.all_gather(change_sum, "z")
-    change_sum = jnp.sum(change_sum, axis=0)[lax.axis_index("z")]
-    new_rows = lax.all_to_all(start + running, "z", 0, 0).reshape(token_count, block)
+    change_sum = jnp.sum(change * change, axis=(1, 2), keepdims=True)
+    change_sum = jnp.broadcast_to(change_sum, (z_size, slice_tokens, HD))
+    sent = jnp.concatenate([start + running, change_sum], axis=2)
+    got = lax.all_to_all(sent, "z", 0, 0)
+    new_rows = got[:, :, :block].reshape(token_count, block)
+    change_sum = tp_sum(jnp.sum(got[:, 0, block]))
     error_value = change_sum / (token_count * full_width)
     return (new_rows[None], error_value.reshape(1))
 

time: 221 us -> 222 us (level)
  the two profiles are of different devices: /device:TPU:2 before, /device:TPU:1 now
where the time goes in v15:
time: 222 us; the launch traced here: 221 us
  blocking collectives  172 us (77%)
  between operations  16.1 us (7%)
  local copies, waits for them, and re-layouts  7.86 us (4%)
  starting transfers between devices  7.06 us (3%)
  matrix products  5.88 us (3%)
  waiting for transfers between devices  5.75 us (3%)
  other arithmetic  4.97 us (2%)
    psum x6, blocking collectives, tp_sum(): return lax.psum(lax.psum(value, 'core'), 'y')  52.4 us
    all_to_all x1, blocking collectives, on_device(): lax.all_to_all(latent.reshape(z_size, slice_tokens, block), 'z', 0, 0)  31 us
    all_to_all x1, blocking collectives, on_device(): got = lax.all_to_all(sent, 'z', 0, 0)  29.8 us
    all_gather x1, blocking collectives, on_device(): gathered = lax.all_gather(flipped, 'y')  22.3 us
    all_gather x1, blocking collectives, on_device(): rows = lax.all_gather(rows, TP, axis=1, tiled=True)  18.3 us
    all_gather x1, blocking collectives, on_device(): lax.all_gather(weighted_side(row_sizes, attended, rows_here[0]), 'x')  11.1 us
    all_gather x2, blocking collectives, on_device(): lax.all_gather(gathered[at * half:(at + 1) * half], 'core')  6.99 us
    all_to_all x1, starting transfers between devices, on_device(): query = jnp.sum(lax.all_to_all(partial, 'x', 0, 0), axis=0)  6.35 us
  transfers between devices with their start and end apart: 4, of which 2 were waited for; matrix products, arithmetic and copies ran while one was open for 4% of the time, Pallas kernels for 1%

profile of v15, /device:TPU:1, one launch (start us, length us, event | category | flops | bytes accessed | tf_op | source)
XLA Modules:
  0.0 221.1 jit_solution(10826395828806138316)
XLA Ops:
  7.2 1.5 fusion.8
  8.8 31.0 %all_to_all.15 = f32[16,8,640]{2,1,0:T(8,128)S(1)} all-to-all(f32[16,8,640]{2,1,0:T(8,128)} %bitcast.90), channel_id=1, replica_groups=mesh['x'=4,'z'=16,'y'=4,'core'=2] {'z'}, dimensions={0} | all-to-all | bytes 655360 | tf_op jit(solution)/shard_map/all_to_all | solution.py:62
  39.8 0.1 fusion.22
  39.9 0.1 stack.9
  40.0 0.1 stack.10
  40.1 11.3 %psum.42 = f32[2,128]{1,0:T(2,128)S(1)} all-reduce(f32[2,128]{1,0:T(2,128)S(1)} %pad_maximum_fusion.3), channel_id=1, replica_groups=mesh['x'=4,'z'=16,'y'=4,'core'=2] {'core'}, use_global_device_ids=true, to_apply=%region_2.3 | all-reduce | flops 256 | bytes 2048 | tf_op jit(solution)/shard_map/psum | solution.py:23
  51.3 9.9 %psum.43 = f32[2,128]{1,0:T(2,128)S(1)} all-reduce(f32[2,128]{1,0:T(2,128)S(1)} %psum.42), channel_id=1, replica_groups=mesh['x'=4,'z'=16,'y'=4,'core'=2] {'y'}, use_global_device_ids=true, to_apply=%region_3.4 | all-reduce | flops 256 | bytes 2048 | tf_op jit(solution)/shard_map/psum | solution.py:23
  61.3 0.8 fusion.6
  62.1 0.7 collective-permute-start
  62.8 22.3 %all-gather.1 = bf16[512,640]{1,0:T(8,128)(2,1)S(1)} all-gather(bf16[128,640]{1,0:T(8,128)(2,1)S(1)} %collective-permute-done), channel_id=3, replica_groups=mesh['x'=4,'z'=16,'y'=4,'core'=2] {'y'}, dimensions={0}, use_global_device_ids=true | all-gather | bytes 819200 | tf_op jit(solution)/shard_map/all_gather | solution.py:72
  85.1 4.7 %all-gather.2 = bf16[4,128,640]{2,1,0:T(8,128)(2,1)S(1)} all-gather(bf16[2,128,640]{2,1,0:T(8,128)(2,1)S(1)} %bitcast.84), channel_id=4, replica_groups=mesh['x'=4,'z'=16,'y'=4,'core'=2] {'core'}, dimensions={0}, use_global_device_ids=true | all-gather | bytes 983040 | tf_op jit(solution)/shard_map/all_gather | solution.py:74
  89.8 2.3 %all-gather.3 = bf16[4,128,640]{2,1,0:T(8,128)(2,1)S(1)} all-gather(bf16[2,128,640]{2,1,0:T(8,128)(2,1)S(1)} %bitcast.83), channel_id=5, replica_groups=mesh['x'=4,'z'=16,'y'=4,'core'=2] {'core'}, dimensions={0}, use_global_device_ids=true | all-gather | bytes 983040 | tf_op jit(solution)/shard_map/all_gather | solution.py:74
  92.1 1.3 slice.76
  93.4 0.5 convolution_bitcast_fusion
  94.0 0.5 convolution_bitcast_fusion.1
  94.5 1.0 pad_maximum_fusion
  95.4 6.3 %all-to-all-start.1 = ((f32[4,128,384]{2,1,0:T(8,128)}), f32[4,128,384]{2,1,0:T(8,128)S(1)}, u32[]{:S(2)}, u32[]{:S(2)}) async-start(f32[4,128,384]{2,1,0:T(8,128)} %pad_maximum_fusion), calls=%async_computation.1 | async-start | bytes 1572864 | tf_op jit(solution)/shard_map/all_to_all | solution.py:85
  101.8 0.1 divide_subtract_fusion
  102.1 0.7 broadcast_in_dim.16.sizes
  102.8 0.2 copy.25
  103.0 0.2 copy.28
  103.2 0.6 slice_bitcast_fusion.2.first
  103.8 2.2 %slice.82 = bf16[16,48,640]{2,1,0:T(8,128)(2,1)} slice(bf16[16,128,640]{2,1,0:T(8,128)(2,1)} %bitcast.82), slice={[0:16], [80:128], [0:640]} | slice | bytes 1966080 | tf_op jit(solution)/shard_map/slice | solution.py:83
  106.1 5.4 %all-to-all-done.1 = f32[4,128,384]{2,1,0:T(8,128)S(1)} async-done(((f32[4,128,384]{2,1,0:T(8,128)}), f32[4,128,384]{2,1,0:T(8,128)S(1)}, u32[]{:S(2)}, u32[]{:S(2)}) %all-to-all-start.1) | async-done | bytes 786464 | tf_op jit(solution)/shard_map/all_to_all | solution.py:85
  111.5 0.1 multiply_reduce_fusion.2
  111.7 0.1 copy.24
  111.8 5.6 %psum.44 = f32[128]{0:T(128)S(1)} all-reduce(f32[128]{0:T(128)S(1)} %multiply_reduce_fusion.2), channel_id=1, replica_groups=mesh['x'=4,'z'=16,'y'=4,'core'=2] {'core'}, use_global_device_ids=true, to_apply=%region_6.7 | all-reduce | flops 128 | bytes 1024 | tf_op jit(solution)/shard_map/psum | solution.py:23
  117.4 7.2 %psum.45 = f32[128]{0:T(128)S(1)} all-reduce(f32[128]{0:T(128)S(1)} %psum.44), channel_id=1, replica_groups=mesh['x'=4,'z'=16,'y'=4,'core'=2] {'y'}, use_global_device_ids=true, to_apply=%region_7.8 | all-reduce | flops 128 | bytes 1024 | tf_op jit(solution)/shard_map/psum | solution.py:23
  124.7 0.6 fusion.25
  125.2 0.4 convolution_multiply_fusion
  125.6 0.9 convolution_convert_fusion
  126.5 0.8 copy.30.attended
  127.3 1.6 shard_map.95
  128.8 11.1 %all-gather.4 = f32[32,1024]{1,0:T(8,128)S(1)} all-gather(f32[8,1024]{1,0:T(8,128)} %shard_map.95), channel_id=6, replica_groups=mesh['x'=4,'z'=16,'y'=4,'core'=2] {'x'}, dimensions={0}, use_global_device_ids=true | all-gather | bytes 163840 | tf_op jit(solution)/shard_map/all_gather | solution.py:108
  140.0 0.2 copy.32
  140.2 0.2 copy.31
  140.3 0.1 pad_maximum_fusion.2
  140.4 18.3 %all_gather.46 = bf16[144,3072]{0,1:T(8,128)(2,1)S(1)} all-gather(bf16[144,384]{0,1:T(8,128)(2,1)S(1)} %pad_maximum_fusion.2), channel_id=1, replica_groups=mesh['x'=4,'z'=16,'y'=4,'core'=2] {'y','core'}, dimensions={1}, use_global_device_ids=true | all-gather | bytes 995328 | tf_op jit(solution)/shard_map/all_gather | solution.py:116
  158.8 0.3 all-gather.8.cloned.1.call-done
  159.0 3.1 %fusion.26 = f32[144,640]{1,0:T(8,128)S(1)} fusion(bf16[144,3072]{0,1:T(8,128)(2,1)S(1)} %all_gather.46, bf16[3072,640]{1,0:T(8,128)(2,1)} %all-gather.8.cloned.1.call-done), kind=kOutput, calls=%fused_computation.61 | convolution fusion | flops 566231040 | bytes 5185536 | tf_op jit(solution)/shard_map/dot_general | solution.py:117
  162.1 0.1 fusion.3
  162.2 0.1 pad_add_fusion.3
  162.6 0.2 multiply_reduce_fusion
  162.9 29.8 %all_to_all.16 = f32[16,8,768]{2,1,0:T(8,128)S(1)} all-to-all(f32[16,8,768]{2,1,0:T(8,128)S(1)} %pad_maximum_fusion.1), channel_id=1, replica_groups=mesh['x'=4,'z'=16,'y'=4,'core'=2] {'z'}, dimensions={0} | all-to-all | bytes 786432 | tf_op jit(solution)/shard_map/all_to_all | solution.py:132
  192.7 0.6 slice_reduce_fusion
  193.4 9.4 %psum.46 = f32[]{:T(128)} all-reduce(f32[]{:T(128)} %slice_reduce_fusion), channel_id=1, replica_groups=mesh['x'=4,'z'=16,'y'=4,'core'=2] {'core'}, use_global_device_ids=true, to_apply=%region_12.13 | all-reduce | flops 1 | bytes 8 | tf_op jit(solution)/shard_map/psum | solution.py:23
  202.8 8.9 %psum.47 = f32[]{:T(128)} all-reduce(f32[]{:T(128)} %psum.46), channel_id=1, replica_groups=mesh['x'=4,'z'=16,'y'=4,'core'=2] {'y'}, use_global_device_ids=true, to_apply=%region_13.14 | all-reduce | flops 1 | bytes 8 | tf_op jit(solution)/shard_map/psum | solution.py:23
  212.3 0.7 slice_bitcast_fusion
  (37 shorter events, 0.8 us)
Async XLA Ops:
  7.2 84.9 %all-gather.10.cloned.1.call-start = ((), (), s32[]{:S(2)}) async-start(), calls=%async_computation.4 | async-start | bytes 2785280 | tf_op jit(solution)/shard_map/all_gather | solution.py:60
  62.1 0.7 collective-permute-start
  93.9 7.9 %copy-start.3 = (s32[64]{0:T(128)S(1)}, s32[64]{0:T(128)}, u32[]{:S(2)}) copy-start(s32[64]{0:T(128)} %param.9) | copy-start | bytes 772
  93.9 8.9 %copy-start = (bf16[512,384]{1,0:T(8,128)(2,1)S(1)}, bf16[512,384]{1,0:T(8,128)(2,1)}, u32[]{:S(2)}) copy-start(bf16[512,384]{1,0:T(8,128)(2,1)} %param.10) | copy-start | bytes 1179652
  93.9 9.0 %copy-start.1 = (bf16[512,384]{1,0:T(8,128)(2,1)S(1)}, bf16[512,384]{1,0:T(8,128)(2,1)}, u32[]{:S(2)}) copy-start(bf16[512,384]{1,0:T(8,128)(2,1)} %param.11) | copy-start | bytes 1179652
  95.4 16.1 %all-to-all-start.1 = ((f32[4,128,384]{2,1,0:T(8,128)}), f32[4,128,384]{2,1,0:T(8,128)S(1)}, u32[]{:S(2)}, u32[]{:S(2)}) async-start(f32[4,128,384]{2,1,0:T(8,128)} %pad_maximum_fusion), calls=%async_computation.1 | async-start | bytes 1572864 | tf_op jit(solution)/shard_map/all_to_all | solution.py:85
  101.8 57.3 %all-gather.8.cloned.1.call-start = ((), (), s32[]{:S(2)}) async-start(), calls=%async_computation.3 | async-start | bytes 4915200 | tf_op jit(solution)/shard_map/all_gather | solution.py:84
  103.0 21.7 %copy-start.2 = (f32[384]{0:T(512)S(1)}, f32[384]{0:T(512)}, u32[]{:S(2)}) copy-start(f32[384]{0:T(512)} %param.13) | copy-start | bytes 4612
Sparse Core Ops, SparseCore 0:
  10.7 77.7 all-gather.9
  106.2 52.8 all-gather.7

commit v16 on v8

--- a/solution.py
+++ b/solution.py
@@ -38,12 +38,12 @@
     x_here = lax.axis_index("x")
     slice_tokens = token_count // z_size
 
+    depth, cols = w_query.shape
+    both = jnp.concatenate([jnp.pad(w_query, ((0, 0), (0, block - cols))), w_out])
+    both = lax.all_gather(both, "z")
+
     rows_here = lax.all_to_all(latent.reshape(z_size, slice_tokens, block), "z", 0, 0)
-
-    depth, cols = w_query.shape
-    query_rows = lax.all_to_all(jnp.broadcast_to(w_query, (z_size, depth, cols)), "z", 0, 0)
-
-    out_rows = lax.all_gather(w_out, STEP, axis=0, tiled=True)
+    latent = rows_here.reshape(token_count, block)
 
     sums = jnp.stack([jnp.sum(latent, axis=-1), jnp.sum(latent * latent, axis=-1)])
     sums = tp_sum(sums) / full_width
@@ -55,7 +55,10 @@
     gathered = lax.all_gather(flipped, "y")
     half = x_size // 2
     parts = [lax.all_gather(gathered[at * half : (at + 1) * half], "core") for at in range(2)]
-    query_weights = query_rows.reshape(2, block, cols)
+    both, parts = lax.optimization_barrier((both, parts))
+    query_weights = both[:, :depth, :cols].reshape(2, block, cols)
+    out_rows = both[:, depth:].reshape(-1, block)
+    out_rows = lax.all_gather(out_rows, "x", axis=0, tiled=True)
     partial = [
         jnp.einsum("cxtk,ckn->xtn", part, query_weights, preferred_element_type=jnp.float32)
         for part in parts
@@ -78,8 +81,6 @@
         "htk,khd->thd", soft_weights, value_heads, preferred_element_type=jnp.float32
     )
     attended = attended.reshape(token_count, local_heads * HD).astype(jnp.bfloat16)
-    attended = attended.reshape(z_size, slice_tokens, -1)
-    attended = lax.all_to_all(attended, "z", 0, 0).reshape(token_count, -1)
     later = jnp.concatenate([timesteps[1:], jnp.zeros((1,), timesteps.dtype)])
     step_sizes = sigma_of(later) - sigma_of(timesteps)
     step_sizes = lax.dynamic_slice_in_dim(step_sizes, x_here * z_size, z_size)[:, None, None]

time: 226 us -> 215 us (0.951)
  starting transfers between devices: 42 us -> 7.4 us
  blocking collectives: 138 us -> 165 us
  waiting for transfers between devices: 12.9 us -> 9.36 us
    all_to_all x3 -> x1, starting transfers between devices: 41.2 us -> 6.65 us  [on_device(): query = jnp.sum(lax.all_to_all(partial, 'x', 0, 0), axis=0)]
    all_to_all x1, blocking collectives: 16 us -> 31 us  [on_device(): lax.all_to_all(latent.reshape(z_size, slice_tokens, block), 'z', 0, 0)]
    all_to_all x1, blocking collectives: 18 us -> 25.2 us  [on_device(): got = lax.all_to_all(sent, 'z', 0, 0)]
    psum x6, blocking collectives: 44.5 us -> 50.6 us  [tp_sum(): return lax.psum(lax.psum(value, 'core'), 'y')]
    slice x0 -> x2, local copies, waits for them, and re-layouts: none -> 3.58 us  [the longest x1 2.26 us: on_device(): out_rows = both[:, depth:].reshape(-1, block)]
    all_to_all x3 -> x1, waiting for transfers between devices: 12.2 us -> 9.32 us  [on_device(): query = jnp.sum(lax.all_to_all(partial, 'x', 0, 0), axis=0)]
  transfers between devices with their start and end apart: 5 -> 4, of which waited for: 1 -> 1; matrix products, arithmetic and copies ran while one was open for 4% -> 4% of each run, Pallas kernels for 0% -> 0%
where the time goes in v16:
time: 215 us; the launch traced here: 214 us
  blocking collectives  165 us (77%)
  between operations  16.1 us (7%)
  waiting for transfers between devices  9.36 us (4%)
  starting transfers between devices  7.4 us (3%)
  local copies, waits for them, and re-layouts  5.98 us (3%)
  matrix products  5.88 us (3%)
  other arithmetic  5.05 us (2%)
    psum x6, blocking collectives, tp_sum(): return lax.psum(lax.psum(value, 'core'), 'y')  50.6 us
    all_to_all x1, blocking collectives, on_device(): lax.all_to_all(latent.reshape(z_size, slice_tokens, block), 'z', 0, 0)  31 us
    all_to_all x1, blocking collectives, on_device(): got = lax.all_to_all(sent, 'z', 0, 0)  25.2 us
    all_gather x1, blocking collectives, on_device(): gathered = lax.all_gather(flipped, 'y')  22.3 us
    all_gather x1, blocking collectives, on_device(): rows = lax.all_gather(rows, TP, axis=1, tiled=True)  18 us
    all_gather x1, blocking collectives, on_device(): lax.all_gather(jnp.concatenate([weighted, rows_here[0]], axis=1), 'x')  10.7 us
    all_to_all x1, waiting for transfers between devices, on_device(): query = jnp.sum(lax.all_to_all(partial, 'x', 0, 0), axis=0)  9.32 us
    all_gather x2, blocking collectives, on_device(): lax.all_gather(gathered[at * half:(at + 1) * half], 'core')  6.78 us
  transfers between devices with their start and end apart: 4, of which 1 were waited for; matrix products, arithmetic and copies ran while one was open for 4% of the time, Pallas kernels for 0%

profile of v16, /device:TPU:1, one launch (start us, length us, event | category | flops | bytes accessed | tf_op | source)
XLA Modules:
  0.0 214.3 jit_solution(16211652381268766128)
XLA Ops:
  7.2 1.5 fusion.8
  8.8 31.0 %all_to_all.15 = f32[16,8,640]{2,1,0:T(8,128)S(1)} all-to-all(f32[16,8,640]{2,1,0:T(8,128)} %bitcast.89), channel_id=1, replica_groups=mesh['x'=4,'z'=16,'y'=4,'core'=2] {'z'}, dimensions={0} | all-to-all | bytes 655360 | tf_op jit(solution)/shard_map/all_to_all | solution.py:45
  39.8 0.1 fusion.22
  39.9 0.1 stack.10
  40.0 0.1 stack.9
  40.1 11.3 %psum.42 = f32[2,128]{1,0:T(2,128)S(1)} all-reduce(f32[2,128]{1,0:T(2,128)S(1)} %pad_maximum_fusion.4), channel_id=1, replica_groups=mesh['x'=4,'z'=16,'y'=4,'core'=2] {'core'}, use_global_device_ids=true, to_apply=%region_2.3 | all-reduce | flops 256 | bytes 2048 | tf_op jit(solution)/shard_map/psum | solution.py:22
  51.5 9.9 %psum.43 = f32[2,128]{1,0:T(2,128)S(1)} all-reduce(f32[2,128]{1,0:T(2,128)S(1)} %psum.42), channel_id=1, replica_groups=mesh['x'=4,'z'=16,'y'=4,'core'=2] {'y'}, use_global_device_ids=true, to_apply=%region_3.4 | all-reduce | flops 256 | bytes 2048 | tf_op jit(solution)/shard_map/psum | solution.py:22
  61.3 0.8 fusion.6
  62.1 0.7 collective-permute-start
  62.8 22.3 %all-gather.1 = bf16[512,640]{1,0:T(8,128)(2,1)S(1)} all-gather(bf16[128,640]{1,0:T(8,128)(2,1)S(1)} %collective-permute-done), channel_id=3, replica_groups=mesh['x'=4,'z'=16,'y'=4,'core'=2] {'y'}, dimensions={0}, use_global_device_ids=true | all-gather | bytes 819200 | tf_op jit(solution)/shard_map/all_gather | solution.py:55
  85.2 4.5 %all-gather.2 = bf16[4,128,640]{2,1,0:T(8,128)(2,1)S(1)} all-gather(bf16[2,128,640]{2,1,0:T(8,128)(2,1)S(1)} %bitcast.85), channel_id=4, replica_groups=mesh['x'=4,'z'=16,'y'=4,'core'=2] {'core'}, dimensions={0}, use_global_device_ids=true | all-gather | bytes 983040 | tf_op jit(solution)/shard_map/all_gather | solution.py:57
  89.7 2.3 %all-gather.3 = bf16[4,128,640]{2,1,0:T(8,128)(2,1)S(1)} all-gather(bf16[2,128,640]{2,1,0:T(8,128)(2,1)S(1)} %bitcast.84), channel_id=5, replica_groups=mesh['x'=4,'z'=16,'y'=4,'core'=2] {'core'}, dimensions={0}, use_global_device_ids=true | all-gather | bytes 983040 | tf_op jit(solution)/shard_map/all_gather | solution.py:57
  92.0 2.3 %slice.82 = bf16[16,48,640]{2,1,0:T(8,128)(2,1)} slice(bf16[16,128,640]{2,1,0:T(8,128)(2,1)} %bitcast.82), slice={[0:16], [80:128], [0:640]} | slice | bytes 1966080 | tf_op jit(solution)/shard_map/slice | solution.py:60
  94.3 1.3 slice.76
  95.6 0.5 convolution_bitcast_fusion.1
  96.1 0.5 convolution_bitcast_fusion
  96.6 0.9 pad_maximum_fusion
  97.6 6.7 %all-to-all-start.1 = ((f32[4,128,384]{2,1,0:T(8,128)}), f32[4,128,384]{2,1,0:T(8,128)S(1)}, u32[]{:S(2)}, u32[]{:S(2)}) async-start(f32[4,128,384]{2,1,0:T(8,128)} %pad_maximum_fusion), calls=%async_computation.1 | async-start | bytes 1572864 | tf_op jit(solution)/shard_map/all_to_all | solution.py:67
  104.2 0.2 copy.24
  104.4 0.2 copy.27
  104.7 0.1 divide_subtract_fusion
  104.8 0.1 dynamic_slice.3
  104.9 9.3 %all-to-all-done.1 = f32[4,128,384]{2,1,0:T(8,128)S(1)} async-done(((f32[4,128,384]{2,1,0:T(8,128)}), f32[4,128,384]{2,1,0:T(8,128)S(1)}, u32[]{:S(2)}, u32[]{:S(2)}) %all-to-all-start.1) | async-done | bytes 786464 | tf_op jit(solution)/shard_map/all_to_all | solution.py:67
  114.3 0.1 copy.23
  114.4 0.1 multiply_reduce_fusion.3
  114.5 6.5 %psum.44 = f32[128]{0:T(128)S(1)} all-reduce(f32[128]{0:T(128)S(1)} %multiply_reduce_fusion.3), channel_id=1, replica_groups=mesh['x'=4,'z'=16,'y'=4,'core'=2] {'core'}, use_global_device_ids=true, to_apply=%region_6.7 | all-reduce | flops 128 | bytes 1024 | tf_op jit(solution)/shard_map/psum | solution.py:22
  121.0 6.8 %psum.45 = f32[128]{0:T(128)S(1)} all-reduce(f32[128]{0:T(128)S(1)} %psum.44), channel_id=1, replica_groups=mesh['x'=4,'z'=16,'y'=4,'core'=2] {'y'}, use_global_device_ids=true, to_apply=%region_7.8 | all-reduce | flops 128 | bytes 1024 | tf_op jit(solution)/shard_map/psum | solution.py:22
  127.8 0.6 fusion.25
  128.4 0.4 convolution_multiply_fusion
  128.8 0.9 bitcast_convert_fusion
  129.6 0.1 copy.28
  129.8 0.1 reshape.100
  129.9 0.1 multiply_reduce_fusion.2
  130.0 10.7 %all-gather.4 = f32[32,1024]{1,0:T(8,128)S(1)} all-gather(f32[8,1024]{1,0:T(8,128)S(1)} %pad_maximum_fusion.3), channel_id=6, replica_groups=mesh['x'=4,'z'=16,'y'=4,'core'=2] {'x'}, dimensions={0}, use_global_device_ids=true | all-gather | bytes 163840 | tf_op jit(solution)/shard_map/all_gather | solution.py:90
  140.8 0.2 copy.30
  140.9 0.2 copy.29
  141.1 0.1 pad_maximum_fusion.2
  141.2 18.0 %all_gather.46 = bf16[144,3072]{0,1:T(8,128)(2,1)S(1)} all-gather(bf16[144,384]{0,1:T(8,128)(2,1)S(1)} %pad_maximum_fusion.2), channel_id=1, replica_groups=mesh['x'=4,'z'=16,'y'=4,'core'=2] {'y','core'}, dimensions={1}, use_global_device_ids=true | all-gather | bytes 995328 | tf_op jit(solution)/shard_map/all_gather | solution.py:98
  159.2 3.0 %fusion.26 = f32[144,640]{1,0:T(8,128)S(1)} fusion(bf16[144,3072]{0,1:T(8,128)(2,1)S(1)} %all_gather.46, bf16[3072,640]{1,0:T(8,128)(2,1)} %all-gather.8.cloned.1.call-done), kind=kOutput, calls=%fused_computation.64 | convolution fusion | flops 566231040 | bytes 5185536 | tf_op jit(solution)/shard_map/dot_general | solution.py:99
  162.2 0.1 fusion.3
  162.4 0.1 pad_add_fusion.3
  162.7 0.2 multiply_reduce_fusion
  162.9 0.1 broadcast_in_dim.9
  163.1 25.2 %all_to_all.16 = f32[16,8,768]{2,1,0:T(8,128)S(1)} all-to-all(f32[16,8,768]{2,1,0:T(8,128)S(1)} %pad_maximum_fusion.1), channel_id=1, replica_groups=mesh['x'=4,'z'=16,'y'=4,'core'=2] {'z'}, dimensions={0} | all-to-all | bytes 786432 | tf_op jit(solution)/shard_map/all_to_all | solution.py:114
  188.2 0.6 slice_reduce_fusion
  188.9 8.8 %psum.46 = f32[]{:T(128)} all-reduce(f32[]{:T(128)} %slice_reduce_fusion), channel_id=1, replica_groups=mesh['x'=4,'z'=16,'y'=4,'core'=2] {'core'}, use_global_device_ids=true, to_apply=%region_13.14 | all-reduce | flops 1 | bytes 8 | tf_op jit(solution)/shard_map/psum | solution.py:22
  197.6 7.3 %psum.47 = f32[]{:T(128)} all-reduce(f32[]{:T(128)} %psum.46), channel_id=1, replica_groups=mesh['x'=4,'z'=16,'y'=4,'core'=2] {'y'}, use_global_device_ids=true, to_apply=%region_14.15 | all-reduce | flops 1 | bytes 8 | tf_op jit(solution)/shard_map/psum | solution.py:22
  205.6 0.7 slice_bitcast_fusion
  (37 shorter events, 0.6 us)
Async XLA Ops:
  7.2 84.8 %all-gather.10.cloned.1.call-start = ((), (), s32[]{:S(2)}) async-start(), calls=%async_computation.4 | async-start | bytes 2785280 | tf_op jit(solution)/shard_map/all_gather | solution.py:43
  8.8 150.4 %all-gather.8.cloned.1.call-start = ((), (), s32[]{:S(2)}) async-start(), calls=%async_computation.3 | async-start | bytes 4915200 | tf_op jit(solution)/shard_map/all_gather | solution.py:61
  62.1 0.7 collective-permute-start
  96.1 8.1 %copy-start = (bf16[512,384]{1,0:T(8,128)(2,1)S(1)}, bf16[512,384]{1,0:T(8,128)(2,1)}, u32[]{:S(2)}) copy-start(bf16[512,384]{1,0:T(8,128)(2,1)} %param.10) | copy-start | bytes 1179652
  96.1 8.3 %copy-start.1 = (bf16[512,384]{1,0:T(8,128)(2,1)S(1)}, bf16[512,384]{1,0:T(8,128)(2,1)}, u32[]{:S(2)}) copy-start(bf16[512,384]{1,0:T(8,128)(2,1)} %param.11) | copy-start | bytes 1179652
  96.6 8.0 %copy-start.3 = (s32[64]{0:T(128)S(1)}, s32[64]{0:T(128)}, u32[]{:S(2)}) copy-start(s32[64]{0:T(128)} %param.9) | copy-start | bytes 772
  97.6 30.2 %copy-start.2 = (f32[384]{0:T(512)S(1)}, f32[384]{0:T(512)}, u32[]{:S(2)}) copy-start(f32[384]{0:T(512)} %param.13) | copy-start | bytes 4612
  97.6 16.6 %all-to-all-start.1 = ((f32[4,128,384]{2,1,0:T(8,128)}), f32[4,128,384]{2,1,0:T(8,128)S(1)}, u32[]{:S(2)}, u32[]{:S(2)}) async-start(f32[4,128,384]{2,1,0:T(8,128)} %pad_maximum_fusion), calls=%async_computation.1 | async-start | bytes 1572864 | tf_op jit(solution)/shard_map/all_to_all | solution.py:67
Sparse Core Ops, SparseCore 0:
  10.7 77.4 all-gather.9
  94.4 55.6 all-gather.7

commit v17 on v16

--- a/solution.py
+++ b/solution.py
@@ -81,6 +81,8 @@
         "htk,khd->thd", soft_weights, value_heads, preferred_element_type=jnp.float32
     )
     attended = attended.reshape(token_count, local_heads * HD).astype(jnp.bfloat16)
+    attended = lax.optimization_barrier(attended)
+
     later = jnp.concatenate([timesteps[1:], jnp.zeros((1,), timesteps.dtype)])
     step_sizes = sigma_of(later) - sigma_of(timesteps)
     step_sizes = lax.dynamic_slice_in_dim(step_sizes, x_here * z_size, z_size)[:, None, None]

time: 215 us -> 215 us (level)
  no operation moved by 1% of the time
where the time goes in v17:
time: 215 us; the launch traced here: 214 us
  blocking collectives  165 us (77%)
  between operations  16.1 us (7%)
  waiting for transfers between devices  9.36 us (4%)
  starting transfers between devices  7.4 us (3%)
  matrix products  5.88 us (3%)
  local copies, waits for them, and re-layouts  5.85 us (3%)
  other arithmetic  5.05 us (2%)
    psum x6, blocking collectives, tp_sum(): return lax.psum(lax.psum(value, 'core'), 'y')  50.6 us
    all_to_all x1, blocking collectives, on_device(): lax.all_to_all(latent.reshape(z_size, slice_tokens, block), 'z', 0, 0)  31 us
    all_to_all x1, blocking collectives, on_device(): got = lax.all_to_all(sent, 'z', 0, 0)  25.2 us
    all_gather x1, blocking collectives, on_device(): gathered = lax.all_gather(flipped, 'y')  22.3 us
    all_gather x1, blocking collectives, on_device(): rows = lax.all_gather(rows, TP, axis=1, tiled=True)  18 us
    all_gather x1, blocking collectives, on_device(): lax.all_gather(jnp.concatenate([weighted, rows_here[0]], axis=1), 'x')  10.7 us
    all_to_all x1, waiting for transfers between devices, on_device(): query = jnp.sum(lax.all_to_all(partial, 'x', 0, 0), axis=0)  9.32 us
    all_gather x2, blocking collectives, on_device(): lax.all_gather(gathered[at * half:(at + 1) * half], 'core')  6.78 us
  transfers between devices with their start and end apart: 4, of which 1 were waited for; matrix products, arithmetic and copies ran while one was open for 4% of the time, Pallas kernels for 0%

profile of v17, /device:TPU:1, one launch (start us, length us, event | category | flops | bytes accessed | tf_op | source)
XLA Modules:
  0.0 214.2 jit_solution(10002514322678028580)
XLA Ops:
  7.2 1.5 fusion.9
  8.8 31.0 %all_to_all.15 = f32[16,8,640]{2,1,0:T(8,128)S(1)} all-to-all(f32[16,8,640]{2,1,0:T(8,128)} %bitcast.93), channel_id=1, replica_groups=mesh['x'=4,'z'=16,'y'=4,'core'=2] {'z'}, dimensions={0} | all-to-all | bytes 655360 | tf_op jit(solution)/shard_map/all_to_all | solution.py:45
  39.8 0.1 fusion.23
  39.9 0.1 stack.10
  40.0 0.1 stack.9
  40.1 11.3 %psum.42 = f32[2,128]{1,0:T(2,128)S(1)} all-reduce(f32[2,128]{1,0:T(2,128)S(1)} %pad_maximum_fusion.4), channel_id=1, replica_groups=mesh['x'=4,'z'=16,'y'=4,'core'=2] {'core'}, use_global_device_ids=true, to_apply=%region_2.3 | all-reduce | flops 256 | bytes 2048 | tf_op jit(solution)/shard_map/psum | solution.py:22
  51.5 9.9 %psum.43 = f32[2,128]{1,0:T(2,128)S(1)} all-reduce(f32[2,128]{1,0:T(2,128)S(1)} %psum.42), channel_id=1, replica_groups=mesh['x'=4,'z'=16,'y'=4,'core'=2] {'y'}, use_global_device_ids=true, to_apply=%region_3.4 | all-reduce | flops 256 | bytes 2048 | tf_op jit(solution)/shard_map/psum | solution.py:22
  61.3 0.8 fusion.6
  62.1 0.7 collective-permute-start
  62.8 22.3 %all-gather.1 = bf16[512,640]{1,0:T(8,128)(2,1)S(1)} all-gather(bf16[128,640]{1,0:T(8,128)(2,1)S(1)} %collective-permute-done), channel_id=3, replica_groups=mesh['x'=4,'z'=16,'y'=4,'core'=2] {'y'}, dimensions={0}, use_global_device_ids=true | all-gather | bytes 819200 | tf_op jit(solution)/shard_map/all_gather | solution.py:55
  85.2 4.5 %all-gather.2 = bf16[4,128,640]{2,1,0:T(8,128)(2,1)S(1)} all-gather(bf16[2,128,640]{2,1,0:T(8,128)(2,1)S(1)} %bitcast.87), channel_id=4, replica_groups=mesh['x'=4,'z'=16,'y'=4,'core'=2] {'core'}, dimensions={0}, use_global_device_ids=true | all-gather | bytes 983040 | tf_op jit(solution)/shard_map/all_gather | solution.py:57
  89.7 2.3 %all-gather.3 = bf16[4,128,640]{2,1,0:T(8,128)(2,1)S(1)} all-gather(bf16[2,128,640]{2,1,0:T(8,128)(2,1)S(1)} %bitcast.86), channel_id=5, replica_groups=mesh['x'=4,'z'=16,'y'=4,'core'=2] {'core'}, dimensions={0}, use_global_device_ids=true | all-gather | bytes 983040 | tf_op jit(solution)/shard_map/all_gather | solution.py:57
  92.0 2.3 %slice.82 = bf16[16,48,640]{2,1,0:T(8,128)(2,1)} slice(bf16[16,128,640]{2,1,0:T(8,128)(2,1)} %bitcast.84), slice={[0:16], [80:128], [0:640]} | slice | bytes 1966080 | tf_op jit(solution)/shard_map/slice | solution.py:60
  94.3 1.3 slice.76
  95.6 0.5 convolution_bitcast_fusion.1
  96.1 0.5 convolution_bitcast_fusion
  96.6 0.9 pad_maximum_fusion
  97.6 6.7 %all-to-all-start.1 = ((f32[4,128,384]{2,1,0:T(8,128)}), f32[4,128,384]{2,1,0:T(8,128)S(1)}, u32[]{:S(2)}, u32[]{:S(2)}) async-start(f32[4,128,384]{2,1,0:T(8,128)} %pad_maximum_fusion), calls=%async_computation.1 | async-start | bytes 1572864 | tf_op jit(solution)/shard_map/all_to_all | solution.py:67
  104.2 0.2 copy.24
  104.4 0.2 copy.27
  104.7 0.1 slice.71
  104.7 0.1 divide_subtract_fusion
  104.8 0.1 dynamic_slice.3
  104.9 9.3 %all-to-all-done.1 = f32[4,128,384]{2,1,0:T(8,128)S(1)} async-done(((f32[4,128,384]{2,1,0:T(8,128)}), f32[4,128,384]{2,1,0:T(8,128)S(1)}, u32[]{:S(2)}, u32[]{:S(2)}) %all-to-all-start.1) | async-done | bytes 786464 | tf_op jit(solution)/shard_map/all_to_all | solution.py:67
  114.3 0.1 copy.23
  114.4 0.1 multiply_reduce_fusion.2
  114.5 6.5 %psum.44 = f32[128]{0:T(128)S(1)} all-reduce(f32[128]{0:T(128)S(1)} %multiply_reduce_fusion.2), channel_id=1, replica_groups=mesh['x'=4,'z'=16,'y'=4,'core'=2] {'core'}, use_global_device_ids=true, to_apply=%region_6.7 | all-reduce | flops 128 | bytes 1024 | tf_op jit(solution)/shard_map/psum | solution.py:22
  121.0 6.8 %psum.45 = f32[128]{0:T(128)S(1)} all-reduce(f32[128]{0:T(128)S(1)} %psum.44), channel_id=1, replica_groups=mesh['x'=4,'z'=16,'y'=4,'core'=2] {'y'}, use_global_device_ids=true, to_apply=%region_7.8 | all-reduce | flops 128 | bytes 1024 | tf_op jit(solution)/shard_map/psum | solution.py:22
  127.8 0.6 fusion.26
  128.4 0.4 convolution_multiply_fusion
  128.8 0.9 convolution_convert_fusion
  129.6 0.1 copy.28
  129.8 0.1 fusion.8
  129.9 10.7 %all-gather.4 = f32[32,1024]{1,0:T(8,128)S(1)} all-gather(f32[8,1024]{1,0:T(8,128)S(1)} %pad_maximum_fusion.3), channel_id=6, replica_groups=mesh['x'=4,'z'=16,'y'=4,'core'=2] {'x'}, dimensions={0}, use_global_device_ids=true | all-gather | bytes 163840 | tf_op jit(solution)/shard_map/all_gather | solution.py:92
  140.7 0.2 copy.30
  140.8 0.2 copy.29
  141.0 0.1 pad_maximum_fusion.2
  141.1 18.0 %all_gather.46 = bf16[144,3072]{0,1:T(8,128)(2,1)S(1)} all-gather(bf16[144,384]{0,1:T(8,128)(2,1)S(1)} %pad_maximum_fusion.2), channel_id=1, replica_groups=mesh['x'=4,'z'=16,'y'=4,'core'=2] {'y','core'}, dimensions={1}, use_global_device_ids=true | all-gather | bytes 995328 | tf_op jit(solution)/shard_map/all_gather | solution.py:100
  159.1 3.0 %fusion.27 = f32[144,640]{1,0:T(8,128)S(1)} fusion(bf16[144,3072]{0,1:T(8,128)(2,1)S(1)} %all_gather.46, bf16[3072,640]{1,0:T(8,128)(2,1)} %all-gather.8.cloned.1.call-done), kind=kOutput, calls=%fused_computation.64 | convolution fusion | flops 566231040 | bytes 5185536 | tf_op jit(solution)/shard_map/dot_general | solution.py:101
  162.1 0.1 fusion.3
  162.3 0.1 pad_add_fusion.3
  162.6 0.2 multiply_reduce_fusion
  162.8 0.1 broadcast_in_dim.9
  162.9 25.2 %all_to_all.16 = f32[16,8,768]{2,1,0:T(8,128)S(1)} all-to-all(f32[16,8,768]{2,1,0:T(8,128)S(1)} %pad_maximum_fusion.1), channel_id=1, replica_groups=mesh['x'=4,'z'=16,'y'=4,'core'=2] {'z'}, dimensions={0} | all-to-all | bytes 786432 | tf_op jit(solution)/shard_map/all_to_all | solution.py:116
  188.1 0.6 slice_reduce_fusion
  188.7 8.8 %psum.46 = f32[]{:T(128)} all-reduce(f32[]{:T(128)} %slice_reduce_fusion), channel_id=1, replica_groups=mesh['x'=4,'z'=16,'y'=4,'core'=2] {'core'}, use_global_device_ids=true, to_apply=%region_13.14 | all-reduce | flops 1 | bytes 8 | tf_op jit(solution)/shard_map/psum | solution.py:22
  197.5 7.4 %psum.47 = f32[]{:T(128)} all-reduce(f32[]{:T(128)} %psum.46), channel_id=1, replica_groups=mesh['x'=4,'z'=16,'y'=4,'core'=2] {'y'}, use_global_device_ids=true, to_apply=%region_14.15 | all-reduce | flops 1 | bytes 8 | tf_op jit(solution)/shard_map/psum | solution.py:22
  205.5 0.7 slice_bitcast_fusion
  (36 shorter events, 0.5 us)
Async XLA Ops:
  7.2 84.8 %all-gather.10.cloned.1.call-start = ((), (), s32[]{:S(2)}) async-start(), calls=%async_computation.4 | async-start | bytes 2785280 | tf_op jit(solution)/shard_map/all_gather | solution.py:43
  8.8 150.3 %all-gather.8.cloned.1.call-start = ((), (), s32[]{:S(2)}) async-start(), calls=%async_computation.3 | async-start | bytes 4915200 | tf_op jit(solution)/shard_map/all_gather | solution.py:61
  62.1 0.7 collective-permute-start
  96.1 8.1 %copy-start = (bf16[512,384]{1,0:T(8,128)(2,1)S(1)}, bf16[512,384]{1,0:T(8,128)(2,1)}, u32[]{:S(2)}) copy-start(bf16[512,384]{1,0:T(8,128)(2,1)} %param.10) | copy-start | bytes 1179652
  96.1 8.3 %copy-start.1 = (bf16[512,384]{1,0:T(8,128)(2,1)S(1)}, bf16[512,384]{1,0:T(8,128)(2,1)}, u32[]{:S(2)}) copy-start(bf16[512,384]{1,0:T(8,128)(2,1)} %param.11) | copy-start | bytes 1179652
  96.6 8.0 %copy-start.3 = (s32[64]{0:T(128)S(1)}, s32[64]{0:T(128)}, u32[]{:S(2)}) copy-start(s32[64]{0:T(128)} %param.9) | copy-start | bytes 772
  97.6 30.2 %copy-start.2 = (f32[384]{0:T(512)S(1)}, f32[384]{0:T(512)}, u32[]{:S(2)}) copy-start(f32[384]{0:T(512)} %param.13) | copy-start | bytes 4612
  97.6 16.6 %all-to-all-start.1 = ((f32[4,128,384]{2,1,0:T(8,128)}), f32[4,128,384]{2,1,0:T(8,128)S(1)}, u32[]{:S(2)}, u32[]{:S(2)}) async-start(f32[4,128,384]{2,1,0:T(8,128)} %pad_maximum_fusion), calls=%async_computation.1 | async-start | bytes 1572864 | tf_op jit(solution)/shard_map/all_to_all | solution.py:67
Sparse Core Ops, SparseCore 0:
  10.7 77.4 all-gather.9
  94.4 55.6 all-gather.7

commit v18 on v17

--- a/solution.py
+++ b/solution.py
@@ -53,17 +53,14 @@
 
     flipped = transpose_plane(normed)
     gathered = lax.all_gather(flipped, "y")
-    half = x_size // 2
-    parts = [lax.all_gather(gathered[at * half : (at + 1) * half], "core") for at in range(2)]
+    parts = [lax.all_gather(gathered[:, :, :cols], "core"), lax.all_gather(gathered[:, :, cols:], "core")]
     both, parts = lax.optimization_barrier((both, parts))
     query_weights = both[:, :depth, :cols].reshape(2, block, cols)
     out_rows = both[:, depth:].reshape(-1, block)
     out_rows = lax.all_gather(out_rows, "x", axis=0, tiled=True)
-    partial = [
-        jnp.einsum("cxtk,ckn->xtn", part, query_weights, preferred_element_type=jnp.float32)
-        for part in parts
-    ]
-    partial = jnp.concatenate(partial)
+    partial = 0.0
+    for part, weights in zip(parts, (query_weights[:, :cols], query_weights[:, cols:])):
+        partial += jnp.einsum("cxtk,ckn->xtn", part, weights, preferred_element_type=jnp.float32)
     query = jnp.sum(lax.all_to_all(partial, "x", 0, 0), axis=0)
     query_width = query.shape[1] * lax.axis_size(TP)
     square_sum = tp_sum(jnp.sum(query * query, axis=-1))

time: 215 us -> 215 us (level)
  no operation moved by 1% of the time
where the time goes in v18:
time: 215 us; the launch traced here: 214 us
  blocking collectives  165 us (77%)
  between operations  16.1 us (7%)
  waiting for transfers between devices  9.37 us (4%)
  starting transfers between devices  7.4 us (3%)
  matrix products  6.77 us (3%)
  local copies, waits for them, and re-layouts  5.85 us (3%)
  other arithmetic  4.12 us (2%)
    psum x6, blocking collectives, tp_sum(): return lax.psum(lax.psum(value, 'core'), 'y')  50.6 us
    all_to_all x1, blocking collectives, on_device(): lax.all_to_all(latent.reshape(z_size, slice_tokens, block), 'z', 0, 0)  31 us
    all_to_all x1, blocking collectives, on_device(): got = lax.all_to_all(sent, 'z', 0, 0)  25.2 us
    all_gather x1, blocking collectives, on_device(): gathered = lax.all_gather(flipped, 'y')  22.3 us
    all_gather x1, blocking collectives, on_device(): rows = lax.all_gather(rows, TP, axis=1, tiled=True)  18 us
    all_gather x1, blocking collectives, on_device(): lax.all_gather(jnp.concatenate([weighted, rows_here[0]], axis=1), 'x')  10.7 us
    all_to_all x1, waiting for transfers between devices, on_device(): query = jnp.sum(lax.all_to_all(partial, 'x', 0, 0), axis=0)  9.33 us
    all_to_all x1, starting transfers between devices, on_device(): query = jnp.sum(lax.all_to_all(partial, 'x', 0, 0), axis=0)  6.65 us
  transfers between devices with their start and end apart: 4, of which 1 were waited for; matrix products, arithmetic and copies ran while one was open for 4% of the time, Pallas kernels for 0%

profile of v18, /device:TPU:1, one launch (start us, length us, event | category | flops | bytes accessed | tf_op | source)
XLA Modules:
  0.0 214.2 jit_solution(3511833128832678201)
XLA Ops:
  7.2 1.5 fusion.10
  8.8 0.0 all-gather.8.cloned.1.call-start
  8.8 31.0 %all_to_all.15 = f32[16,8,640]{2,1,0:T(8,128)S(1)} all-to-all(f32[16,8,640]{2,1,0:T(8,128)} %bitcast.98), channel_id=1, replica_groups=mesh['x'=4,'z'=16,'y'=4,'core'=2] {'z'}, dimensions={0} | all-to-all | bytes 655360 | tf_op jit(solution)/shard_map/all_to_all | solution.py:45
  39.8 0.1 fusion.24
  39.9 0.1 stack.10
  40.0 0.1 stack.9
  40.1 11.3 %psum.42 = f32[2,128]{1,0:T(2,128)S(1)} all-reduce(f32[2,128]{1,0:T(2,128)S(1)} %pad_maximum_fusion.3), channel_id=1, replica_groups=mesh['x'=4,'z'=16,'y'=4,'core'=2] {'core'}, use_global_device_ids=true, to_apply=%region_2.3 | all-reduce | flops 256 | bytes 2048 | tf_op jit(solution)/shard_map/psum | solution.py:22
  51.5 9.9 %psum.43 = f32[2,128]{1,0:T(2,128)S(1)} all-reduce(f32[2,128]{1,0:T(2,128)S(1)} %psum.42), channel_id=1, replica_groups=mesh['x'=4,'z'=16,'y'=4,'core'=2] {'y'}, use_global_device_ids=true, to_apply=%region_3.4 | all-reduce | flops 256 | bytes 2048 | tf_op jit(solution)/shard_map/psum | solution.py:22
  61.3 0.8 fusion.7
  62.1 0.7 collective-permute-start
  62.8 22.3 %all-gather.1 = bf16[512,640]{1,0:T(8,128)(2,1)S(1)} all-gather(bf16[128,640]{1,0:T(8,128)(2,1)S(1)} %collective-permute-done), channel_id=3, replica_groups=mesh['x'=4,'z'=16,'y'=4,'core'=2] {'y'}, dimensions={0}, use_global_device_ids=true | all-gather | bytes 819200 | tf_op jit(solution)/shard_map/all_gather | solution.py:55
  85.2 4.4 %all-gather.3 = bf16[8,128,256]{2,1,0:T(8,128)(2,1)S(1)} all-gather(bf16[4,128,256]{2,1,0:T(8,128)(2,1)S(1)} %slice.102), channel_id=5, replica_groups=mesh['x'=4,'z'=16,'y'=4,'core'=2] {'core'}, dimensions={0}, use_global_device_ids=true | all-gather | bytes 786432 | tf_op jit(solution)/shard_map/all_gather | solution.py:56
  89.6 2.4 %all-gather.2 = bf16[8,128,384]{2,1,0:T(8,128)(2,1)S(1)} all-gather(bf16[4,128,384]{2,1,0:T(8,128)(2,1)S(1)} %slice.101), channel_id=4, replica_groups=mesh['x'=4,'z'=16,'y'=4,'core'=2] {'core'}, dimensions={0}, use_global_device_ids=true | all-gather | bytes 1179648 | tf_op jit(solution)/shard_map/all_gather | solution.py:56
  92.0 2.3 %slice.90 = bf16[16,48,640]{2,1,0:T(8,128)(2,1)} slice(bf16[16,128,640]{2,1,0:T(8,128)(2,1)} %bitcast.91), slice={[0:16], [80:128], [0:640]} | slice | bytes 1966080 | tf_op jit(solution)/shard_map/slice | solution.py:59
  94.3 1.3 slice.82
  95.6 0.4 convolution_bitcast_fusion
  96.1 1.5 fusion.3
  97.6 6.7 %all-to-all-start.1 = ((f32[4,128,384]{2,1,0:T(8,128)}), f32[4,128,384]{2,1,0:T(8,128)S(1)}, u32[]{:S(2)}, u32[]{:S(2)}) async-start(f32[4,128,384]{2,1,0:T(8,128)} %fusion.3), calls=%async_computation.1 | async-start | bytes 1572864 | tf_op jit(solution)/shard_map/all_to_all | solution.py:64
  104.2 0.2 copy.24
  104.4 0.2 copy.27
  104.6 0.1 slice.77
  104.7 0.1 divide_subtract_fusion
  104.8 0.1 dynamic_slice.3
  104.9 9.3 %all-to-all-done.1 = f32[4,128,384]{2,1,0:T(8,128)S(1)} async-done(((f32[4,128,384]{2,1,0:T(8,128)}), f32[4,128,384]{2,1,0:T(8,128)S(1)}, u32[]{:S(2)}, u32[]{:S(2)}) %all-to-all-start.1) | async-done | bytes 786464 | tf_op jit(solution)/shard_map/all_to_all | solution.py:64
  114.2 0.1 copy.23
  114.4 0.1 multiply_reduce_fusion.2
  114.5 6.4 %psum.44 = f32[128]{0:T(128)S(1)} all-reduce(f32[128]{0:T(128)S(1)} %multiply_reduce_fusion.2), channel_id=1, replica_groups=mesh['x'=4,'z'=16,'y'=4,'core'=2] {'core'}, use_global_device_ids=true, to_apply=%region_6.7 | all-reduce | flops 128 | bytes 1024 | tf_op jit(solution)/shard_map/psum | solution.py:22
  120.9 6.8 %psum.45 = f32[128]{0:T(128)S(1)} all-reduce(f32[128]{0:T(128)S(1)} %psum.44), channel_id=1, replica_groups=mesh['x'=4,'z'=16,'y'=4,'core'=2] {'y'}, use_global_device_ids=true, to_apply=%region_7.8 | all-reduce | flops 128 | bytes 1024 | tf_op jit(solution)/shard_map/psum | solution.py:22
  127.7 0.6 fusion.26
  128.3 0.4 convolution_multiply_fusion
  128.7 0.9 convolution_convert_fusion
  129.6 0.1 copy.28
  129.7 0.1 fusion.9
  129.8 10.7 %all-gather.4 = f32[32,1024]{1,0:T(8,128)S(1)} all-gather(f32[8,1024]{1,0:T(8,128)S(1)} %pad_maximum_fusion.2), channel_id=6, replica_groups=mesh['x'=4,'z'=16,'y'=4,'core'=2] {'x'}, dimensions={0}, use_global_device_ids=true | all-gather | bytes 163840 | tf_op jit(solution)/shard_map/all_gather | solution.py:89
  140.6 0.2 copy.30
  140.7 0.2 copy.29
  140.9 0.1 pad_maximum_fusion.1
  141.0 18.0 %all_gather.46 = bf16[144,3072]{0,1:T(8,128)(2,1)S(1)} all-gather(bf16[144,384]{0,1:T(8,128)(2,1)S(1)} %pad_maximum_fusion.1), channel_id=1, replica_groups=mesh['x'=4,'z'=16,'y'=4,'core'=2] {'y','core'}, dimensions={1}, use_global_device_ids=true | all-gather | bytes 995328 | tf_op jit(solution)/shard_map/all_gather | solution.py:97
  159.0 3.1 %fusion.27 = f32[144,640]{1,0:T(8,128)S(1)} fusion(bf16[144,3072]{0,1:T(8,128)(2,1)S(1)} %all_gather.46, bf16[3072,640]{1,0:T(8,128)(2,1)} %all-gather.8.cloned.1.call-done), kind=kOutput, calls=%fused_computation.65 | convolution fusion | flops 566231040 | bytes 5185536 | tf_op jit(solution)/shard_map/dot_general | solution.py:98
  162.1 0.1 fusion.4
  162.2 0.1 pad_add_fusion.3
  162.6 0.2 multiply_reduce_fusion
  162.8 0.1 broadcast_in_dim.9
  162.9 25.2 %all_to_all.16 = f32[16,8,768]{2,1,0:T(8,128)S(1)} all-to-all(f32[16,8,768]{2,1,0:T(8,128)S(1)} %pad_maximum_fusion), channel_id=1, replica_groups=mesh['x'=4,'z'=16,'y'=4,'core'=2] {'z'}, dimensions={0} | all-to-all | bytes 786432 | tf_op jit(solution)/shard_map/all_to_all | solution.py:113
  188.1 0.6 slice_reduce_fusion
  188.7 8.8 %psum.46 = f32[]{:T(128)} all-reduce(f32[]{:T(128)} %slice_reduce_fusion), channel_id=1, replica_groups=mesh['x'=4,'z'=16,'y'=4,'core'=2] {'core'}, use_global_device_ids=true, to_apply=%region_13.14 | all-reduce | flops 1 | bytes 8 | tf_op jit(solution)/shard_map/psum | solution.py:22
  197.5 7.4 %psum.47 = f32[]{:T(128)} all-reduce(f32[]{:T(128)} %psum.46), channel_id=1, replica_groups=mesh['x'=4,'z'=16,'y'=4,'core'=2] {'y'}, use_global_device_ids=true, to_apply=%region_14.15 | all-reduce | flops 1 | bytes 8 | tf_op jit(solution)/shard_map/psum | solution.py:22
  205.5 0.7 slice_bitcast_fusion.4
  (36 shorter events, 0.5 us)
Async XLA Ops:
  7.2 84.8 %all-gather.10.cloned.1.call-start = ((), (), s32[]{:S(2)}) async-start(), calls=%async_computation.4 | async-start | bytes 2785280 | tf_op jit(solution)/shard_map/all_gather | solution.py:43
  8.8 150.2 %all-gather.8.cloned.1.call-start = ((), (), s32[]{:S(2)}) async-start(), calls=%async_computation.3 | async-start | bytes 4915200 | tf_op jit(solution)/shard_map/all_gather | solution.py:60
  62.1 0.7 collective-permute-start
  96.1 8.2 %copy-start = (bf16[512,384]{1,0:T(8,128)(2,1)S(1)}, bf16[512,384]{1,0:T(8,128)(2,1)}, u32[]{:S(2)}) copy-start(bf16[512,384]{1,0:T(8,128)(2,1)} %param.10) | copy-start | bytes 1179652
  96.1 8.3 %copy-start.1 = (bf16[512,384]{1,0:T(8,128)(2,1)S(1)}, bf16[512,384]{1,0:T(8,128)(2,1)}, u32[]{:S(2)}) copy-start(bf16[512,384]{1,0:T(8,128)(2,1)} %param.11) | copy-start | bytes 1179652
  96.1 8.5 %copy-start.3 = (s32[64]{0:T(128)S(1)}, s32[64]{0:T(128)}, u32[]{:S(2)}) copy-start(s32[64]{0:T(128)} %param.9) | copy-start | bytes 772
  97.5 30.2 %copy-start.2 = (f32[384]{0:T(512)S(1)}, f32[384]{0:T(512)}, u32[]{:S(2)}) copy-start(f32[384]{0:T(512)} %param.13) | copy-start | bytes 4612
  97.6 16.6 %all-to-all-start.1 = ((f32[4,128,384]{2,1,0:T(8,128)}), f32[4,128,384]{2,1,0:T(8,128)S(1)}, u32[]{:S(2)}, u32[]{:S(2)}) async-start(f32[4,128,384]{2,1,0:T(8,128)} %fusion.3), calls=%async_computation.1 | async-start | bytes 1572864 | tf_op jit(solution)/shard_map/all_to_all | solution.py:64
Sparse Core Ops, SparseCore 0:
  10.7 77.4 all-gather.9
  94.4 55.5 all-gather.7

commit v19 on v18

--- a/solution.py
+++ b/solution.py
@@ -94,8 +94,9 @@
     terms = [high.astype(jnp.bfloat16), (weighted - high).astype(jnp.bfloat16)]
     rows = jnp.concatenate([attended, *terms])
 
-    rows = lax.all_gather(rows, TP, axis=1, tiled=True)
-    product = jnp.dot(rows, out_rows, preferred_element_type=jnp.float32)
+    rows = lax.all_gather(rows, TP)
+    out_rows = out_rows.reshape(rows.shape[0], width, block)
+    product = jnp.einsum("jtk,jkn->tn", rows, out_rows, preferred_element_type=jnp.float32)
     velocity = product[:token_count].reshape(z_size, slice_tokens, block)
     terms = product[token_count:].reshape(2, slice_tokens, block)
     start = sides[0, :, width:] + (terms[0] + terms[1])

time: 215 us -> 214 us (level)
  transfers between devices with their start and end apart: 4 -> 4, of which waited for: 1 -> 1; matrix products, arithmetic and copies ran while one was open for 4% -> 3% of each run, Pallas kernels for 0% -> 0%
where the time goes in v19:
time: 214 us; the launch traced here: 212 us
  blocking collectives  163 us (76%)
  between operations  16.1 us (8%)
  waiting for transfers between devices  9.37 us (4%)
  starting transfers between devices  7.27 us (3%)
  matrix products  6.7 us (3%)
  local copies, waits for them, and re-layouts  5.58 us (3%)
  other arithmetic  4.02 us (2%)
    psum x6, blocking collectives, tp_sum(): return lax.psum(lax.psum(value, 'core'), 'y')  50.2 us
    all_to_all x1, blocking collectives, on_device(): lax.all_to_all(latent.reshape(z_size, slice_tokens, block), 'z', 0, 0)  31 us
    all_to_all x1, blocking collectives, on_device(): got = lax.all_to_all(sent, 'z', 0, 0)  25.4 us
    all_gather x1, blocking collectives, on_device(): gathered = lax.all_gather(flipped, 'y')  22.3 us
    all_gather x1, blocking collectives, on_device(): rows = lax.all_gather(rows, TP)  16.7 us
    all_gather x1, blocking collectives, on_device(): lax.all_gather(jnp.concatenate([weighted, rows_here[0]], axis=1), 'x')  10.7 us
    all_to_all x1, waiting for transfers between devices, on_device(): query = jnp.sum(lax.all_to_all(partial, 'x', 0, 0), axis=0)  9.33 us
    all_to_all x1, starting transfers between devices, on_device(): query = jnp.sum(lax.all_to_all(partial, 'x', 0, 0), axis=0)  6.52 us
  transfers between devices with their start and end apart: 4, of which 1 were waited for; matrix products, arithmetic and copies ran while one was open for 3% of the time, Pallas kernels for 0%

profile of v19, /device:TPU:1, one launch (start us, length us, event | category | flops | bytes accessed | tf_op | source)
XLA Modules:
  0.0 212.3 jit_solution(16329659184088087671)
XLA Ops:
  7.2 0.0 all-gather.11.cloned.1.call-start
  7.2 1.5 fusion.10
  8.7 0.0 all-gather.11.cloned.1.call-update
  8.8 0.0 all-gather.9.cloned.1.call-start
  8.8 31.0 %all_to_all.15 = f32[16,8,640]{2,1,0:T(8,128)S(1)} all-to-all(f32[16,8,640]{2,1,0:T(8,128)} %bitcast.102), channel_id=1, replica_groups=mesh['x'=4,'z'=16,'y'=4,'core'=2] {'z'}, dimensions={0} | all-to-all | bytes 655360 | tf_op jit(solution)/shard_map/all_to_all | solution.py:45
  39.8 0.1 fusion.24
  39.9 0.1 stack.10
  40.0 0.1 stack.9
  40.1 11.3 %psum.42 = f32[2,128]{1,0:T(2,128)S(1)} all-reduce(f32[2,128]{1,0:T(2,128)S(1)} %pad_maximum_fusion.3), channel_id=1, replica_groups=mesh['x'=4,'z'=16,'y'=4,'core'=2] {'core'}, use_global_device_ids=true, to_apply=%region_2.3 | all-reduce | flops 256 | bytes 2048 | tf_op jit(solution)/shard_map/psum | solution.py:22
  51.5 9.9 %psum.43 = f32[2,128]{1,0:T(2,128)S(1)} all-reduce(f32[2,128]{1,0:T(2,128)S(1)} %psum.42), channel_id=1, replica_groups=mesh['x'=4,'z'=16,'y'=4,'core'=2] {'y'}, use_global_device_ids=true, to_apply=%region_3.4 | all-reduce | flops 256 | bytes 2048 | tf_op jit(solution)/shard_map/psum | solution.py:22
  61.3 0.8 fusion.7
  62.1 0.7 collective-permute-start
  62.8 22.3 %all-gather.1 = bf16[512,640]{1,0:T(8,128)(2,1)S(1)} all-gather(bf16[128,640]{1,0:T(8,128)(2,1)S(1)} %collective-permute-done), channel_id=3, replica_groups=mesh['x'=4,'z'=16,'y'=4,'core'=2] {'y'}, dimensions={0}, use_global_device_ids=true | all-gather | bytes 819200 | tf_op jit(solution)/shard_map/all_gather | solution.py:55
  85.2 4.4 %all-gather.3 = bf16[8,128,256]{2,1,0:T(8,128)(2,1)S(1)} all-gather(bf16[4,128,256]{2,1,0:T(8,128)(2,1)S(1)} %slice.102), channel_id=5, replica_groups=mesh['x'=4,'z'=16,'y'=4,'core'=2] {'core'}, dimensions={0}, use_global_device_ids=true | all-gather | bytes 786432 | tf_op jit(solution)/shard_map/all_gather | solution.py:56
  89.6 2.4 %all-gather.2 = bf16[8,128,384]{2,1,0:T(8,128)(2,1)S(1)} all-gather(bf16[4,128,384]{2,1,0:T(8,128)(2,1)S(1)} %slice.101), channel_id=4, replica_groups=mesh['x'=4,'z'=16,'y'=4,'core'=2] {'core'}, dimensions={0}, use_global_device_ids=true | all-gather | bytes 1179648 | tf_op jit(solution)/shard_map/all_gather | solution.py:56
  92.0 2.3 %slice.90 = bf16[16,48,640]{2,1,0:T(8,128)(2,1)} slice(bf16[16,128,640]{2,1,0:T(8,128)(2,1)} %bitcast.97), slice={[0:16], [80:128], [0:640]} | slice | bytes 1966080 | tf_op jit(solution)/shard_map/slice | solution.py:59
  94.3 0.0 all-gather.9.cloned.1.call-update
  94.3 1.4 slice.82
  95.7 0.4 convolution_bitcast_fusion
  96.2 1.5 fusion.3
  97.6 6.5 %all-to-all-start.1 = ((f32[4,128,384]{2,1,0:T(8,128)}), f32[4,128,384]{2,1,0:T(8,128)S(1)}, u32[]{:S(2)}, u32[]{:S(2)}) async-start(f32[4,128,384]{2,1,0:T(8,128)} %fusion.3), calls=%async_computation.1 | async-start | bytes 1572864 | tf_op jit(solution)/shard_map/all_to_all | solution.py:64
  104.1 0.2 copy.26
  104.3 0.2 copy.29
  104.6 0.1 slice.77
  104.6 0.1 divide_subtract_fusion
  104.7 0.1 dynamic_slice.3
  104.8 9.3 %all-to-all-done.1 = f32[4,128,384]{2,1,0:T(8,128)S(1)} async-done(((f32[4,128,384]{2,1,0:T(8,128)}), f32[4,128,384]{2,1,0:T(8,128)S(1)}, u32[]{:S(2)}, u32[]{:S(2)}) %all-to-all-start.1) | async-done | bytes 786464 | tf_op jit(solution)/shard_map/all_to_all | solution.py:64
  114.2 0.1 copy.25
  114.3 0.1 multiply_reduce_fusion.2
  114.4 6.3 %psum.44 = f32[128]{0:T(128)S(1)} all-reduce(f32[128]{0:T(128)S(1)} %multiply_reduce_fusion.2), channel_id=1, replica_groups=mesh['x'=4,'z'=16,'y'=4,'core'=2] {'core'}, use_global_device_ids=true, to_apply=%region_6.7 | all-reduce | flops 128 | bytes 1024 | tf_op jit(solution)/shard_map/psum | solution.py:22
  120.7 7.0 %psum.45 = f32[128]{0:T(128)S(1)} all-reduce(f32[128]{0:T(128)S(1)} %psum.44), channel_id=1, replica_groups=mesh['x'=4,'z'=16,'y'=4,'core'=2] {'y'}, use_global_device_ids=true, to_apply=%region_7.8 | all-reduce | flops 128 | bytes 1024 | tf_op jit(solution)/shard_map/psum | solution.py:22
  127.7 0.6 fusion.26
  128.2 0.4 convolution_multiply_fusion
  128.6 0.9 convolution_convert_fusion
  129.5 0.1 copy.30
  129.6 0.1 fusion.9
  129.7 10.7 %all-gather.4 = f32[32,1024]{1,0:T(8,128)S(1)} all-gather(f32[8,1024]{1,0:T(8,128)S(1)} %pad_maximum_fusion.2), channel_id=6, replica_groups=mesh['x'=4,'z'=16,'y'=4,'core'=2] {'x'}, dimensions={0}, use_global_device_ids=true | all-gather | bytes 163840 | tf_op jit(solution)/shard_map/all_gather | solution.py:89
  140.5 16.7 %all-gather.5 = bf16[1152,384]{1,0:T(8,128)(2,1)S(1)} all-gather(bf16[144,384]{1,0:T(8,128)(2,1)S(1)} %pad_maximum_fusion.1), channel_id=7, replica_groups=mesh['x'=4,'z'=16,'y'=4,'core'=2] {'y','core'}, dimensions={0}, use_global_device_ids=true | all-gather | bytes 995328 | tf_op jit(solution)/shard_map/all_gather | solution.py:97
  157.3 3.0 %convolution_bitcast_fusion.2 = f32[144,640]{1,0:T(8,128)S(1)} fusion(bf16[8,144,384]{2,1,0:T(8,128)(2,1)S(1)} %bitcast.90, bf16[8,384,640]{2,1,0:T(8,128)(2,1)} %bitcast.86), kind=kOutput, calls=%fused_computation.7 | convolution fusion | flops 566231040 | bytes 5185536 | tf_op jit(solution)/shard_map/jtk,jkn->tn/dot_general | solution.py:99
  160.3 0.1 fusion.4
  160.4 0.1 pad_add_fusion.3
  160.7 0.2 multiply_reduce_fusion
  161.0 0.1 broadcast_in_dim.9
  161.1 25.4 %all_to_all.16 = f32[16,8,768]{2,1,0:T(8,128)S(1)} all-to-all(f32[16,8,768]{2,1,0:T(8,128)S(1)} %pad_maximum_fusion), channel_id=1, replica_groups=mesh['x'=4,'z'=16,'y'=4,'core'=2] {'z'}, dimensions={0} | all-to-all | bytes 786432 | tf_op jit(solution)/shard_map/all_to_all | solution.py:114
  186.5 0.6 slice_reduce_fusion
  187.1 8.8 %psum.46 = f32[]{:T(128)} all-reduce(f32[]{:T(128)} %slice_reduce_fusion), channel_id=1, replica_groups=mesh['x'=4,'z'=16,'y'=4,'core'=2] {'core'}, use_global_device_ids=true, to_apply=%region_13.14 | all-reduce | flops 1 | bytes 8 | tf_op jit(solution)/shard_map/psum | solution.py:22
  195.9 7.0 %psum.47 = f32[]{:T(128)} all-reduce(f32[]{:T(128)} %psum.46), channel_id=1, replica_groups=mesh['x'=4,'z'=16,'y'=4,'core'=2] {'y'}, use_global_device_ids=true, to_apply=%region_14.15 | all-reduce | flops 1 | bytes 8 | tf_op jit(solution)/shard_map/psum | solution.py:22
  203.5 0.7 slice_bitcast_fusion.4
  (34 shorter events, 0.5 us)
Async XLA Ops:
  7.2 84.8 %all-gather.11.cloned.1.call-start = ((), (), s32[]{:S(2)}) async-start(), calls=%async_computation.4 | async-start | bytes 2785280 | tf_op jit(solution)/shard_map/all_gather | solution.py:43
  8.8 148.5 %all-gather.9.cloned.1.call-start = ((), (), s32[]{:S(2)}) async-start(), calls=%async_computation.3 | async-start | bytes 4915200 | tf_op jit(solution)/shard_map/all_gather | solution.py:60
  62.1 0.7 collective-permute-start
  94.3 9.9 %copy-start = (bf16[512,384]{1,0:T(8,128)(2,1)S(1)}, bf16[512,384]{1,0:T(8,128)(2,1)}, u32[]{:S(2)}) copy-start(bf16[512,384]{1,0:T(8,128)(2,1)} %param.10) | copy-start | bytes 1179652
  95.7 8.7 %copy-start.1 = (bf16[512,384]{1,0:T(8,128)(2,1)S(1)}, bf16[512,384]{1,0:T(8,128)(2,1)}, u32[]{:S(2)}) copy-start(bf16[512,384]{1,0:T(8,128)(2,1)} %param.11) | copy-start | bytes 1179652
  95.7 8.9 %copy-start.3 = (s32[64]{0:T(128)S(1)}, s32[64]{0:T(128)}, u32[]{:S(2)}) copy-start(s32[64]{0:T(128)} %param.9) | copy-start | bytes 772
  96.1 31.5 %copy-start.2 = (f32[384]{0:T(512)S(1)}, f32[384]{0:T(512)}, u32[]{:S(2)}) copy-start(f32[384]{0:T(512)} %param.13) | copy-start | bytes 4612
  97.6 16.5 %all-to-all-start.1 = ((f32[4,128,384]{2,1,0:T(8,128)}), f32[4,128,384]{2,1,0:T(8,128)S(1)}, u32[]{:S(2)}, u32[]{:S(2)}) async-start(f32[4,128,384]{2,1,0:T(8,128)} %fusion.3), calls=%async_computation.1 | async-start | bytes 1572864 | tf_op jit(solution)/shard_map/all_to_all | solution.py:64
Sparse Core Ops, SparseCore 0:
  10.7 77.4 all-gather.10
  94.4 55.5 all-gather.8

commit v20 on v19

--- a/solution.py
+++ b/solution.py
@@ -19,7 +19,7 @@
 
 
 def tp_sum(value):
-    return lax.psum(lax.psum(value, "core"), "y")
+    return lax.psum(lax.psum(value, "y"), "core")
 
 
 def transpose_plane(value):

time: 214 us -> 215 us (level)
    psum x6, blocking collectives: 50.2 us -> 55.2 us  [tp_sum(): return lax.psum(lax.psum(value, 'y'), 'core')]
    all_to_all x1, blocking collectives: 25.4 us -> 22.5 us  [on_device(): got = lax.all_to_all(sent, 'z', 0, 0)]
where the time goes in v20:
time: 215 us; the launch traced here: 214 us
  blocking collectives  165 us (77%)
  between operations  16.1 us (7%)
  waiting for transfers between devices  10.8 us (5%)
  matrix products  6.69 us (3%)
  starting transfers between devices  6.61 us (3%)
  local copies, waits for them, and re-layouts  5.58 us (3%)
  other arithmetic  4.02 us (2%)
    psum x6, blocking collectives, tp_sum(): return lax.psum(lax.psum(value, 'y'), 'core')  55.2 us
    all_to_all x1, blocking collectives, on_device(): lax.all_to_all(latent.reshape(z_size, slice_tokens, block), 'z', 0, 0)  31 us
    all_gather x1, blocking collectives, on_device(): gathered = lax.all_gather(flipped, 'y')  23.6 us
    all_to_all x1, blocking collectives, on_device(): got = lax.all_to_all(sent, 'z', 0, 0)  22.5 us
    all_gather x1, blocking collectives, on_device(): rows = lax.all_gather(rows, TP)  15.5 us
    all_to_all x1, waiting for transfers between devices, on_device(): query = jnp.sum(lax.all_to_all(partial, 'x', 0, 0), axis=0)  10.8 us
    all_gather x1, blocking collectives, on_device(): lax.all_gather(jnp.concatenate([weighted, rows_here[0]], axis=1), 'x')  10.7 us
    all_to_all x1, starting transfers between devices, on_device(): query = jnp.sum(lax.all_to_all(partial, 'x', 0, 0), axis=0)  5.85 us
  transfers between devices with their start and end apart: 4, of which 1 were waited for; matrix products, arithmetic and copies ran while one was open for 3% of the time, Pallas kernels for 0%

profile of v20, /device:TPU:1, one launch (start us, length us, event | category | flops | bytes accessed | tf_op | source)
XLA Modules:
  0.0 214.4 jit_solution(15526113394610271220)
XLA Ops:
  7.2 0.0 all-gather.11.cloned.1.call-start
  7.2 1.5 fusion.10
  8.7 0.0 all-gather.11.cloned.1.call-update
  8.8 0.0 all-gather.9.cloned.1.call-start
  8.8 31.0 %all_to_all.15 = f32[16,8,640]{2,1,0:T(8,128)S(1)} all-to-all(f32[16,8,640]{2,1,0:T(8,128)} %bitcast.102), channel_id=1, replica_groups=mesh['x'=4,'z'=16,'y'=4,'core'=2] {'z'}, dimensions={0} | all-to-all | bytes 655360 | tf_op jit(solution)/shard_map/all_to_all | solution.py:45
  39.8 0.1 fusion.24
  39.9 0.1 stack.10
  40.0 0.1 stack.9
  40.1 9.0 %psum.42 = f32[2,128]{1,0:T(2,128)S(1)} all-reduce(f32[2,128]{1,0:T(2,128)S(1)} %pad_maximum_fusion.3), channel_id=1, replica_groups=mesh['x'=4,'z'=16,'y'=4,'core'=2] {'y'}, use_global_device_ids=true, to_apply=%region_2.3 | all-reduce | flops 256 | bytes 2048 | tf_op jit(solution)/shard_map/psum | solution.py:22
  49.1 13.5 %psum.43 = f32[2,128]{1,0:T(2,128)S(1)} all-reduce(f32[2,128]{1,0:T(2,128)S(1)} %psum.42), channel_id=1, replica_groups=mesh['x'=4,'z'=16,'y'=4,'core'=2] {'core'}, use_global_device_ids=true, to_apply=%region_3.4 | all-reduce | flops 256 | bytes 2048 | tf_op jit(solution)/shard_map/psum | solution.py:22
  62.6 0.8 fusion.7
  63.4 0.7 collective-permute-start
  64.1 23.6 %all-gather.1 = bf16[512,640]{1,0:T(8,128)(2,1)S(1)} all-gather(bf16[128,640]{1,0:T(8,128)(2,1)S(1)} %collective-permute-done), channel_id=3, replica_groups=mesh['x'=4,'z'=16,'y'=4,'core'=2] {'y'}, dimensions={0}, use_global_device_ids=true | all-gather | bytes 819200 | tf_op jit(solution)/shard_map/all_gather | solution.py:55
  87.8 3.6 %all-gather.3 = bf16[8,128,256]{2,1,0:T(8,128)(2,1)S(1)} all-gather(bf16[4,128,256]{2,1,0:T(8,128)(2,1)S(1)} %slice.102), channel_id=5, replica_groups=mesh['x'=4,'z'=16,'y'=4,'core'=2] {'core'}, dimensions={0}, use_global_device_ids=true | all-gather | bytes 786432 | tf_op jit(solution)/shard_map/all_gather | solution.py:56
  91.4 2.4 %all-gather.2 = bf16[8,128,384]{2,1,0:T(8,128)(2,1)S(1)} all-gather(bf16[4,128,384]{2,1,0:T(8,128)(2,1)S(1)} %slice.101), channel_id=4, replica_groups=mesh['x'=4,'z'=16,'y'=4,'core'=2] {'core'}, dimensions={0}, use_global_device_ids=true | all-gather | bytes 1179648 | tf_op jit(solution)/shard_map/all_gather | solution.py:56
  93.8 2.3 %slice.90 = bf16[16,48,640]{2,1,0:T(8,128)(2,1)} slice(bf16[16,128,640]{2,1,0:T(8,128)(2,1)} %bitcast.97), slice={[0:16], [80:128], [0:640]} | slice | bytes 1966080 | tf_op jit(solution)/shard_map/slice | solution.py:59
  96.1 0.0 all-gather.9.cloned.1.call-update
  96.1 1.4 slice.82
  97.5 0.4 convolution_bitcast_fusion
  97.9 1.5 fusion.3
  99.4 5.9 %all-to-all-start.1 = ((f32[4,128,384]{2,1,0:T(8,128)}), f32[4,128,384]{2,1,0:T(8,128)S(1)}, u32[]{:S(2)}, u32[]{:S(2)}) async-start(f32[4,128,384]{2,1,0:T(8,128)} %fusion.3), calls=%async_computation.1 | async-start | bytes 1572864 | tf_op jit(solution)/shard_map/all_to_all | solution.py:64
  105.3 0.2 copy.26
  105.5 0.2 copy.29
  105.7 0.1 slice.77
  105.8 0.1 divide_subtract_fusion
  105.8 0.1 dynamic_slice.3
  105.9 10.8 %all-to-all-done.1 = f32[4,128,384]{2,1,0:T(8,128)S(1)} async-done(((f32[4,128,384]{2,1,0:T(8,128)}), f32[4,128,384]{2,1,0:T(8,128)S(1)}, u32[]{:S(2)}, u32[]{:S(2)}) %all-to-all-start.1) | async-done | bytes 786464 | tf_op jit(solution)/shard_map/all_to_all | solution.py:64
  116.7 0.1 copy.25
  116.9 0.1 multiply_reduce_fusion.2
  117.0 6.8 %psum.44 = f32[128]{0:T(128)S(1)} all-reduce(f32[128]{0:T(128)S(1)} %multiply_reduce_fusion.2), channel_id=1, replica_groups=mesh['x'=4,'z'=16,'y'=4,'core'=2] {'y'}, use_global_device_ids=true, to_apply=%region_6.7 | all-reduce | flops 128 | bytes 1024 | tf_op jit(solution)/shard_map/psum | solution.py:22
  123.8 7.8 %psum.45 = f32[128]{0:T(128)S(1)} all-reduce(f32[128]{0:T(128)S(1)} %psum.44), channel_id=1, replica_groups=mesh['x'=4,'z'=16,'y'=4,'core'=2] {'core'}, use_global_device_ids=true, to_apply=%region_7.8 | all-reduce | flops 128 | bytes 1024 | tf_op jit(solution)/shard_map/psum | solution.py:22
  131.6 0.6 fusion.26
  132.2 0.4 convolution_multiply_fusion
  132.6 0.9 convolution_convert_fusion
  133.5 0.1 copy.30
  133.6 0.1 fusion.9
  133.7 10.7 %all-gather.4 = f32[32,1024]{1,0:T(8,128)S(1)} all-gather(f32[8,1024]{1,0:T(8,128)S(1)} %pad_maximum_fusion.2), channel_id=6, replica_groups=mesh['x'=4,'z'=16,'y'=4,'core'=2] {'x'}, dimensions={0}, use_global_device_ids=true | all-gather | bytes 163840 | tf_op jit(solution)/shard_map/all_gather | solution.py:89
  144.5 15.5 %all-gather.5 = bf16[1152,384]{1,0:T(8,128)(2,1)S(1)} all-gather(bf16[144,384]{1,0:T(8,128)(2,1)S(1)} %pad_maximum_fusion.1), channel_id=7, replica_groups=mesh['x'=4,'z'=16,'y'=4,'core'=2] {'y','core'}, dimensions={0}, use_global_device_ids=true | all-gather | bytes 995328 | tf_op jit(solution)/shard_map/all_gather | solution.py:97
  160.0 3.0 %convolution_bitcast_fusion.2 = f32[144,640]{1,0:T(8,128)S(1)} fusion(bf16[8,144,384]{2,1,0:T(8,128)(2,1)S(1)} %bitcast.90, bf16[8,384,640]{2,1,0:T(8,128)(2,1)} %bitcast.86), kind=kOutput, calls=%fused_computation.7 | convolution fusion | flops 566231040 | bytes 5185536 | tf_op jit(solution)/shard_map/jtk,jkn->tn/dot_general | solution.py:99
  163.0 0.1 fusion.4
  163.1 0.1 pad_add_fusion.3
  163.5 0.2 multiply_reduce_fusion
  163.7 0.1 broadcast_in_dim.9
  163.8 22.5 %all_to_all.16 = f32[16,8,768]{2,1,0:T(8,128)S(1)} all-to-all(f32[16,8,768]{2,1,0:T(8,128)S(1)} %pad_maximum_fusion), channel_id=1, replica_groups=mesh['x'=4,'z'=16,'y'=4,'core'=2] {'z'}, dimensions={0} | all-to-all | bytes 786432 | tf_op jit(solution)/shard_map/all_to_all | solution.py:114
  186.3 0.6 slice_reduce_fusion
  187.0 8.1 %psum.46 = f32[]{:T(128)} all-reduce(f32[]{:T(128)} %slice_reduce_fusion), channel_id=1, replica_groups=mesh['x'=4,'z'=16,'y'=4,'core'=2] {'y'}, use_global_device_ids=true, to_apply=%region_13.14 | all-reduce | flops 1 | bytes 8 | tf_op jit(solution)/shard_map/psum | solution.py:22
  195.1 10.0 %psum.47 = f32[]{:T(128)} all-reduce(f32[]{:T(128)} %psum.46), channel_id=1, replica_groups=mesh['x'=4,'z'=16,'y'=4,'core'=2] {'core'}, use_global_device_ids=true, to_apply=%region_14.15 | all-reduce | flops 1 | bytes 8 | tf_op jit(solution)/shard_map/psum | solution.py:22
  205.7 0.7 slice_bitcast_fusion.4
  (34 shorter events, 0.5 us)
Async XLA Ops:
  7.2 86.6 %all-gather.11.cloned.1.call-start = ((), (), s32[]{:S(2)}) async-start(), calls=%async_computation.4 | async-start | bytes 2785280 | tf_op jit(solution)/shard_map/all_gather | solution.py:43
  8.8 151.2 %all-gather.9.cloned.1.call-start = ((), (), s32[]{:S(2)}) async-start(), calls=%async_computation.3 | async-start | bytes 4915200 | tf_op jit(solution)/shard_map/all_gather | solution.py:60
  63.4 0.7 collective-permute-start
  96.1 9.2 %copy-start = (bf16[512,384]{1,0:T(8,128)(2,1)S(1)}, bf16[512,384]{1,0:T(8,128)(2,1)}, u32[]{:S(2)}) copy-start(bf16[512,384]{1,0:T(8,128)(2,1)} %param.10) | copy-start | bytes 1179652
  97.5 8.0 %copy-start.1 = (bf16[512,384]{1,0:T(8,128)(2,1)S(1)}, bf16[512,384]{1,0:T(8,128)(2,1)}, u32[]{:S(2)}) copy-start(bf16[512,384]{1,0:T(8,128)(2,1)} %param.11) | copy-start | bytes 1179652
  97.5 8.2 %copy-start.3 = (s32[64]{0:T(128)S(1)}, s32[64]{0:T(128)}, u32[]{:S(2)}) copy-start(s32[64]{0:T(128)} %param.9) | copy-start | bytes 772
  97.9 33.7 %copy-start.2 = (f32[384]{0:T(512)S(1)}, f32[384]{0:T(512)}, u32[]{:S(2)}) copy-start(f32[384]{0:T(512)} %param.13) | copy-start | bytes 4612
  99.4 17.3 %all-to-all-start.1 = ((f32[4,128,384]{2,1,0:T(8,128)}), f32[4,128,384]{2,1,0:T(8,128)S(1)}, u32[]{:S(2)}, u32[]{:S(2)}) async-start(f32[4,128,384]{2,1,0:T(8,128)} %fusion.3), calls=%async_computation.1 | async-start | bytes 1572864 | tf_op jit(solution)/shard_map/all_to_all | solution.py:64
Sparse Core Ops, SparseCore 0:
  10.7 77.4 all-gather.10
  96.2 54.8 all-gather.8
